TPU v7x, 32 devices: a whole 2x2x4 slice. The times are simulated.
32 devices in a mesh: seq: 8 (over y, x, core), head: 4 (over z).
Axes of the slice: x: 2, y: 2, z: 4, core: 2. Of those that a mesh axis runs over, the one named last changes fastest.
Arguments:
- tokens: bfloat16 [4, 4096, 1536], P(None, 'seq'), may hold values from -6 to 6
- norm_gain: float32 [1536], replicated, may hold values from 0.25 to 1.75
- gate_weight: bfloat16 [1536, 3072], P(None, 'head'), may hold values from -0.15625 to 0.15625
- value_weight: bfloat16 [1536, 3072], P(None, 'head'), may hold values from -0.15625 to 0.15625
- state_weight: bfloat16 [1536, 256], replicated, may hold values from -0.15625 to 0.15625
- step_weight: bfloat16 [1536, 48], P(None, 'head'), may hold values from -0.15625 to 0.15625
- value_kernel: float32 [4, 3072], P(None, 'head'), may hold values from -3 to 3
- value_offset: float32 [3072], P('head'), may hold values from -3 to 3
- state_kernel: float32 [4, 256], replicated, may hold values from -3 to 3
- state_offset: float32 [256], replicated, may hold values from -3 to 3
- step_bias: float32 [48], P('head'), may hold values from -3.5 to -2
- log_rate: float32 [48], P('head'), may hold values from -16 to 0, as said below
- skip_gain: float32 [48], P('head'), may hold values from 0.5 to 2
- mixer_gain: float32 [3072], P('head'), may hold values from 0.25 to 1.75
- out_weight: bfloat16 [3072, 1536], P('head'), may hold values from -0.109375 to 0.109375
- cotangent: bfloat16 [4, 4096, 1536], P(None, 'seq'), may hold values from -6 to 6
Outputs:
- result: bfloat16 [4, 4096, 1536], P(None, 'seq')
- tokens_grad: float32 [4, 4096, 1536], P(None, 'seq')
- norm_gain_grad: float32 [1536], replicated
- gate_weight_grad: float32 [1536, 3072], P(None, 'head')
- value_weight_grad: float32 [1536, 3072], P(None, 'head')
- state_weight_grad: float32 [1536, 256], replicated
- step_weight_grad: float32 [1536, 48], P(None, 'head')
- value_filter_gradient: float32 [4, 3072], P(None, 'head')
- value_offset_grad: float32 [3072], P('head')
- state_kernel_grad: float32 [4, 256], replicated
- state_offset_grad: float32 [256], replicated
- step_bias_grad: float32 [48], P('head')
- log_rate_grad: float32 [48], P('head')
- skip_gain_grad: float32 [48], P('head')
- mixer_gain_grad: float32 [3072], P('head')
- out_weight_grad: float32 [3072, 1536], P('head')
Inputs may be any that keep to these rules, and one draw needn't show every extreme that they name: `log_rate`: one value a head.
All inputs are finite; a program needn't handle non-finite values.
Results may differ from a plain program's by a relative error of at most 0.025.
The roundings to bfloat16 on the way count: a program that leaves them out, or rounds other values in their place, can miss the bound.
Values may be sent and summed in bfloat16 or wider, within the bound.
A program may use at most 320 MiB of HBM per device.

v0:
```python
import jax
import jax.numpy as jnp
from jax import lax
from jax.sharding import PartitionSpec as P

INNER = 3072
GROUP = 256


epsilon = 1e-05


def from_behind(block, axis, distance):
    devices = range(lax.axis_size(axis))
    route = [(i - distance, i) for i in devices if i - distance in devices]
    return lax.ppermute(block, axis, route)


def entering(value, axis, join, neutral, backward):
    count, mine = (lax.axis_size(axis), lax.axis_index(axis))
    pieces = jax.tree.map(lambda part: lax.all_gather(part, axis), value)
    if backward:
        pieces = jax.tree.map(lambda part: part[::-1], pieces)
        mine = count - 1 - mine
    subtotal = jax.tree.map(
        lambda part, zero: jnp.full_like(part, 0) + jnp.asarray(zero, part.dtype), value, neutral
    )

    def hop(position, subtotal):
        longer = join(subtotal, jax.tree.map(lambda part: part[position], pieces))
        return jax.tree.map(lambda new, old: jnp.where(position < mine, new, old), longer, subtotal)

    return lax.fori_loop(0, count - 1, hop, subtotal)


def inner_product_fn(left, right):
    return lax.dot_general(
        left, right, (((0,), (0,)), ((), ())), preferred_element_type=jnp.float32
    )


def outer_dot(left, right):
    return lax.dot_general(
        left, right, (((1,), (1,)), ((), ())), preferred_element_type=jnp.float32
    )


def swish_slope(value):
    sigma = jax.nn.sigmoid(value)
    return sigma * (1.0 + value * (1.0 - sigma))


def chain_link(earlier, later):
    return (earlier[0] * later[0], later[0][..., None, None] * earlier[1] + later[1])


def causal_conv(extended, kernel, offset, length):
    total = offset + kernel[0] * extended[:, 0:length]
    for tap in range(1, kernel.shape[0]):
        total = total + kernel[tap] * extended[:, tap : tap + length]
    return total


def conv_back(extended, grad_out, kernel):
    taps = kernel.shape[0]
    length = grad_out.shape[1]
    padded = jnp.pad(grad_out, ((0, 0), (taps - 1, taps - 1), (0, 0)))
    span = length + taps - 1
    grad_ext = kernel[0] * padded[:, taps - 1 : taps - 1 + span]
    for tap in range(1, taps):
        grad_ext = grad_ext + kernel[tap] * padded[:, taps - 1 - tap : taps - 1 - tap + span]
    kernel_grad = jnp.stack(
        [jnp.sum(grad_out * extended[:, tap : tap + length], axis=(0, 1)) for tap in range(taps)]
    )
    return (grad_ext, kernel_grad, jnp.sum(grad_out, axis=(0, 1)))


def shards(
    tokens,
    norm_gain,
    gate_weight,
    value_weight,
    state_weight,
    step_weight,
    value_kernel,
    value_offset,
    state_kernel,
    state_offset,
    step_bias,
    log_rate,
    skip_gain,
    mixer_gain,
    out_weight,
    cotangent,
):
    seqs, length, width = tokens.shape
    flat = seqs * length
    inner_loc = gate_weight.shape[1]
    heads_loc = step_weight.shape[1]
    head_size = inner_loc // heads_loc
    state_dimension = state_weight.shape[1] // 2
    taps = value_kernel.shape[0]
    block = GROUP
    blocks = length // block
    resid = tokens.astype(jnp.float32)
    inv_rms = lax.rsqrt(jnp.mean(resid * resid, axis=-1, keepdims=True) + epsilon)
    normed = (resid * inv_rms * norm_gain).astype(jnp.bfloat16).reshape(flat, width)
    gate = jnp.dot(normed, gate_weight, preferred_element_type=jnp.float32).reshape(
        seqs, length, inner_loc
    )
    x_part = jnp.dot(normed, value_weight, preferred_element_type=jnp.float32).astype(jnp.bfloat16)
    x_part = x_part.reshape(seqs, length, inner_loc)
    bc_part = jnp.dot(normed, state_weight, preferred_element_type=jnp.float32).astype(jnp.bfloat16)
    bc_part = bc_part.reshape(seqs, length, 2 * state_dimension)
    step_raw = jnp.dot(normed, step_weight, preferred_element_type=jnp.float32).reshape(
        seqs, length, heads_loc
    )
    edge_x, edge_bc = from_behind(
        (x_part[:, length - taps + 1 :], bc_part[:, length - taps + 1 :]), "seq", 1
    )
    ext_x = jnp.concatenate([edge_x, x_part], axis=1)
    ext_bc = jnp.concatenate([edge_bc, bc_part], axis=1)
    x_conv = causal_conv(ext_x, value_kernel, value_offset, length)
    bc_conv = causal_conv(ext_bc, state_kernel, state_offset, length)
    x_act = jax.nn.silu(x_conv).astype(jnp.bfloat16)
    bc_act = jax.nn.silu(bc_conv).astype(jnp.bfloat16)
    step = jax.nn.softplus(step_raw + step_bias)
    rate = -jnp.exp(log_rate)
    x_heads = x_act.reshape(seqs, blocks, block, heads_loc, head_size)
    b_mat = bc_act[..., :state_dimension].reshape(seqs, blocks, block, state_dimension)
    c_mat = bc_act[..., state_dimension:].reshape(seqs, blocks, block, state_dimension)
    step_heads = jnp.transpose(step.reshape(seqs, blocks, block, heads_loc), (0, 1, 3, 2))
    cum = jnp.cumsum(step_heads * rate[:, None], axis=-1)
    lower = jnp.arange(block)[:, None] >= jnp.arange(block)[None, :]
    decay = jnp.exp(jnp.where(lower, cum[..., :, None] - cum[..., None, :], -jnp.inf))
    cross = jnp.einsum("sbtn,sbun->sbtu", c_mat, b_mat, preferred_element_type=jnp.float32)
    cross_decay = cross[:, :, None] * decay
    mix = (cross_decay * step_heads[..., None, :]).astype(jnp.bfloat16)
    within = jnp.einsum("sbhtu,sbuhp->sbthp", mix, x_heads, preferred_element_type=jnp.float32)
    growth = jnp.exp(cum)
    c_scaled = (c_mat[:, :, None] * growth[..., None]).astype(jnp.bfloat16)
    last = cum[..., -1]
    weight_u = jnp.exp(last[..., None] - cum) * step_heads
    weight_t = jnp.transpose(weight_u, (0, 1, 3, 2))[..., None]
    weighted = (x_heads * weight_t).astype(jnp.bfloat16)
    contrib = jnp.einsum("sbuhp,sbun->sbhpn", weighted, b_mat, preferred_element_type=jnp.float32)
    fade = jnp.exp(last)
    local_state = jnp.zeros_like(contrib[:, 0])
    total_fade = jnp.ones_like(fade[:, 0])
    for number in range(blocks):
        local_state = fade[:, number, :, None, None] * local_state + contrib[:, number]
        total_fade = total_fade * fade[:, number]
    state_ones = jnp.ones_like(total_fade)
    state_zeros = jnp.zeros_like(local_state)
    entry_fade, entry = entering(
        (total_fade, local_state), "seq", chain_link, (state_ones, state_zeros), False
    )
    starts = []
    current = entry
    for number in range(blocks):
        starts.append(current)
        current = fade[:, number, :, None, None] * current + contrib[:, number]
    start_state = jnp.stack(starts, axis=1)
    start_low = start_state.astype(jnp.bfloat16)
    across = jnp.einsum(
        "sbhtn,sbhpn->sbthp", c_scaled, start_low, preferred_element_type=jnp.float32
    )
    ssd = (within + across).reshape(seqs, length, inner_loc)
    skip_wide = jnp.repeat(skip_gain, head_size)
    mixed = ssd + skip_wide * x_act
    gated = mixed * jax.nn.silu(gate)
    square_sum = lax.psum(jnp.sum(gated * gated, axis=-1), "head")
    mixer_rms = lax.rsqrt(square_sum / INNER + epsilon)[..., None]
    gnormed = (gated * mixer_rms * mixer_gain).astype(jnp.bfloat16).reshape(flat, inner_loc)
    branch_out = jnp.dot(gnormed, out_weight, preferred_element_type=jnp.float32).reshape(
        seqs, length, width
    )
    summed = lax.psum(branch_out, "head")
    result = (resid + summed).astype(jnp.bfloat16)
    cot_flat = cotangent.reshape(flat, width)
    out_weight_grad = inner_product_fn(gnormed, cot_flat)
    grad_norm = outer_dot(cot_flat, out_weight).reshape(seqs, length, inner_loc)
    mixer_gain_grad = jnp.sum(grad_norm * gated * mixer_rms, axis=(0, 1))
    scaled_grad = grad_norm * mixer_gain
    row_dot = lax.psum(jnp.sum(scaled_grad * gated, axis=-1), "head")
    grad_gated = mixer_rms * scaled_grad - gated * mixer_rms**3 * (row_dot[..., None] / INNER)
    gate_grad = (
        (grad_gated * mixed * swish_slope(gate)).astype(jnp.bfloat16).reshape(flat, inner_loc)
    )
    grad_mixed = grad_gated * jax.nn.silu(gate)
    skip_gain_grad = jnp.sum(
        (grad_mixed * x_act).reshape(seqs, length, heads_loc, head_size), axis=(0, 1, 3)
    )
    ssd_grad = grad_mixed.astype(jnp.bfloat16).reshape(seqs, blocks, block, heads_loc, head_size)
    mix_grad = jnp.einsum(
        "sbthp,sbuhp->sbhtu", ssd_grad, x_heads, preferred_element_type=jnp.float32
    )
    x_grad_within = jnp.einsum(
        "sbhtu,sbthp->sbuhp", mix, ssd_grad, preferred_element_type=jnp.float32
    )
    cross_part = jnp.sum(mix_grad * decay * step_heads[..., None, :], axis=2)
    pair = mix_grad * cross_decay
    step_grad = jnp.sum(pair, axis=-2)
    pair_step = pair * step_heads[..., None, :]
    cum_grad = jnp.sum(pair_step, axis=-1) - jnp.sum(pair_step, axis=-2)
    start_grad = jnp.einsum(
        "sbthp,sbhtn->sbhpn", ssd_grad, c_scaled, preferred_element_type=jnp.float32
    )
    scaled_c_grad = jnp.einsum(
        "sbthp,sbhpn->sbhtn", ssd_grad, start_low, preferred_element_type=jnp.float32
    )
    c_grad = jnp.einsum("sbhtn,sbht->sbtn", scaled_c_grad, growth)
    cum_grad = cum_grad + growth * jnp.einsum("sbhtn,sbtn->sbht", scaled_c_grad, c_mat)
    local_grad = jnp.zeros_like(start_grad[:, 0])
    for number in reversed(range(blocks)):
        local_grad = fade[:, number, :, None, None] * local_grad + start_grad[:, number]
    after_fade, after_grad = entering(
        (total_fade, local_grad), "seq", chain_link, (state_ones, state_zeros), True
    )
    ends = []
    current = after_grad
    for number in reversed(range(blocks)):
        ends.append(current)
        current = fade[:, number, :, None, None] * current + start_grad[:, number]
    end_grad = jnp.stack(ends[::-1], axis=1)
    contrib_grad = end_grad.astype(jnp.bfloat16)
    fade_grad = fade * jnp.sum(end_grad * start_state, axis=(-2, -1))
    weighted_grad = jnp.einsum(
        "sbun,sbhpn->sbuhp", b_mat, contrib_grad, preferred_element_type=jnp.float32
    )
    b_grad = jnp.einsum(
        "sbuhp,sbhpn->sbun", weighted, contrib_grad, preferred_element_type=jnp.float32
    )
    x_grad = x_grad_within + weighted_grad * weight_t
    weight_grad = jnp.transpose(jnp.sum(weighted_grad * x_heads, axis=-1), (0, 1, 3, 2))
    weight_part = weight_grad * weight_u
    step_grad = step_grad + weight_grad * jnp.exp(last[..., None] - cum)
    cum_grad = cum_grad - weight_part
    cum_grad = cum_grad.at[..., -1].add(fade_grad + jnp.sum(weight_part, axis=-1))
    rise_grad = lax.cumsum(cum_grad, axis=3, reverse=True)
    step_grad = step_grad + rise_grad * rate[:, None]
    log_rate_grad = jnp.sum(rise_grad * step_heads, axis=(0, 1, 3)) * rate
    cross_all, b_total, c_total = lax.psum((cross_part, b_grad, c_grad), "head")
    cross_low = cross_all.astype(jnp.bfloat16)
    c_total = c_total + jnp.einsum(
        "sbtu,sbun->sbtn", cross_low, b_mat, preferred_element_type=jnp.float32
    )
    b_total = b_total + jnp.einsum(
        "sbtu,sbtn->sbun", cross_low, c_mat, preferred_element_type=jnp.float32
    )
    x_act_grad = x_grad.reshape(seqs, length, inner_loc) + skip_wide * grad_mixed
    x_conv_grad = x_act_grad * swish_slope(x_conv)
    bc_act_grad = jnp.concatenate(
        [
            b_total.reshape(seqs, length, state_dimension),
            c_total.reshape(seqs, length, state_dimension),
        ],
        axis=-1,
    )
    bc_conv_grad = bc_act_grad * swish_slope(bc_conv)
    x_ext_grad, value_filter_gradient, value_offset_grad = conv_back(
        ext_x, x_conv_grad, value_kernel
    )
    bc_ext_grad, state_kernel_grad, state_offset_grad = conv_back(
        ext_bc, bc_conv_grad, state_kernel
    )
    tail_x, tail_bc = (
        from_behind(x_ext_grad[:, : taps - 1].astype(jnp.bfloat16), "seq", -1).astype(jnp.float32),
        from_behind(bc_ext_grad[:, : taps - 1].astype(jnp.bfloat16), "seq", -1).astype(jnp.float32),
    )
    x_part_grad = x_ext_grad[:, taps - 1 :].at[:, length - taps + 1 :].add(tail_x)
    x_part_grad = x_part_grad.astype(jnp.bfloat16).reshape(flat, inner_loc)
    bc_part_grad = bc_ext_grad[:, taps - 1 :].at[:, length - taps + 1 :].add(tail_bc)
    bc_part_grad = bc_part_grad.astype(jnp.bfloat16).reshape(flat, 2 * state_dimension)
    step_rows = jnp.transpose(step_grad, (0, 1, 3, 2)).reshape(seqs, length, heads_loc)
    raw_grad = step_rows * jax.nn.sigmoid(step_raw + step_bias)
    step_bias_grad = jnp.sum(raw_grad, axis=(0, 1))
    raw_low = raw_grad.astype(jnp.bfloat16).reshape(flat, heads_loc)
    gate_weight_grad = inner_product_fn(normed, gate_grad)
    value_weight_grad = inner_product_fn(normed, x_part_grad)
    state_weight_grad = inner_product_fn(normed, bc_part_grad)
    step_weight_grad = inner_product_fn(normed, raw_low)
    head_terms = (
        outer_dot(gate_grad, gate_weight)
        + outer_dot(x_part_grad, value_weight)
        + outer_dot(raw_low, step_weight)
    )
    normed_grad = lax.psum(head_terms.reshape(seqs, length, width), "head")
    normed_grad = normed_grad + outer_dot(bc_part_grad, state_weight).reshape(seqs, length, width)
    norm_gain_grad = jnp.sum(normed_grad * resid * inv_rms, axis=(0, 1))
    scaled_in = normed_grad * norm_gain
    tokens_grad = (
        cotangent.astype(jnp.float32)
        + inv_rms * scaled_in
        - resid * inv_rms**3 * (jnp.sum(scaled_in * resid, axis=-1, keepdims=True) / width)
    )
    summed_grads = lax.psum(
        (
            norm_gain_grad,
            gate_weight_grad,
            value_weight_grad,
            state_weight_grad,
            step_weight_grad,
            value_filter_gradient,
            value_offset_grad,
            state_kernel_grad,
            state_offset_grad,
            step_bias_grad,
            log_rate_grad,
            skip_gain_grad,
            mixer_gain_grad,
            out_weight_grad,
        ),
        "seq",
    )
    return (result, tokens_grad) + tuple(summed_grads)


def solution(mesh):
    in_specs = (
        P(None, "seq", None),
        P(),
        P(None, "head"),
        P(None, "head"),
        P(),
        P(None, "head"),
        P(None, "head"),
        P("head"),
        P(),
        P(),
        P("head"),
        P("head"),
        P("head"),
        P("head"),
        P("head", None),
        P(None, "seq", None),
    )
    out_specs = (
        P(None, "seq", None),
        P(None, "seq", None),
        P(),
        P(None, "head"),
        P(None, "head"),
        P(),
        P(None, "head"),
        P(None, "head"),
        P("head"),
        P(),
        P(),
        P("head"),
        P("head"),
        P("head"),
        P("head"),
        P("head", None),
    )
    return jax.shard_map(shards, mesh=mesh, in_specs=in_specs, out_specs=out_specs, check_vma=False)
```

profile of v0, /device:TPU:0, one launch (start us, length us, event | category | flops | bytes accessed | tf_op | source)
XLA Modules:
  0.0 1767.1 jit_solution(13856319611288210647)
XLA Ops:
  91.5 10.3 all-gather
  115.5 45.1 %all-gather.4.cloned.1.call-done = f32[8,4,12,64,128]{4,3,2,1,0:T(8,128)} async-done(((f32[1,4,12,64,128]{4,3,2,1,0:T(8,128)}), f32[8,4,12,64,128]{4,3,2,1,0:T(8,128)}) %all-gather.4.cloned.1.call-update) | async-done | bytes 12582928 | tf_op jit(solution)/shard_map/all_gather | solution.py:21
  160.6 27.2 %while.31 = (s32[]{:T(128)}, f32[4,12,64,128]{3,2,1,0:T(8,128)}, s32[]{:T(128)}, f32[8,4,12]{2,1,0:T(4,128)}, f32[8,4,12,64,128]{4,3,2,1,0:T(8,128)}, /*index=5*/s32[]{:T(128)}, s32[]{:T(128)}) while((s32[]{:T(128)}, f32[4,12,64,128]{3,2,1,0:T(8,128)}, s32[]{:T(128)}, f32[8,4,12]{2,1,0:T(4,128)}, f32[8,4,12,64,128]{4,3,2,1,0:T(8,128)}, ...), condition=%wide.region_4.5_spmd.clone, body=%wide.region_3.4_spmd.clone.sunk | while | flops 1572868 | bytes 4719273 | solution.py:33
  201.0 11.1 copy.290
  227.6 14.6 multiply_reduce_fusion.5
  242.3 12.4 psum.147
  255.3 11.6 multiply_reduce_fusion.3
  275.6 12.9 fusion.31
  316.2 18.8 %multiply_reduce_fusion.1 = (f32[4,2,12,256]{3,2,1,0:T(8,128)}, f32[4,2,12,256]{3,2,1,0:T(8,128)}, f32[4,2,12,256]{3,2,1,0:T(8,128)}, f32[4,2,256,256]{3,2,1,0:T(8,128)}) fusion(f32[4,2,12,256]{3,2,1,0:T(8,128)S(1)} %copy-done.45, f32[4,2,12,256]{3,2,1,0:T(8,128)} %copy.276, pred[256,256]{1,0:T(8,128)(4,1)} %copy-done.50, ...), kind=kOutput, calls=%fused_computation.17 | convolution fusion | flops 873914368 | bytes 11042816 | tf_op jit(solution)/shard_map/sbthp,sbuhp->sbhtu/dot_general | solution.py:195
  361.7 10.2 fusion.119
  385.4 11.9 rev.7
  397.3 17.4 while.32
  434.9 19.8 %reduce-window.16 = f32[4,2,12,2,128]{4,2,3,1,0:T(8,128)S(1)} reduce-window(f32[4,2,12,2,128]{4,2,3,1,0:T(8,128)S(1)} %copy.314, f32[]{:T(128)} %constant.153.clone.1), window={size=1x1x1x1x128 pad=0_0x0_0x0_0x0_0x0_127}, to_apply=%region_18.19 | reduce-window | flops 3121152 | bytes 196612 | tf_op jit(solution)/shard_map/reduce-window.2
  457.7 11.7 bitcast_add_fusion.2
  469.4 11.0 copy.298
  496.1 17.9 %fusion.110 = (f32[768]{0:T(1024)S(1)}, f32[768]{0:T(1024)S(1)}, f32[768]{0:T(1024)S(1)}, f32[768]{0:T(1024)S(1)}, f32[768]{0:T(1024)S(1)}, /*index=5*/f32[4,512,768]{2,1,0:T(8,128)S(1)}) fusion(bf16[2048,768]{1,0:T(8,128)(2,1)} %copy-done.10, bf16[4,512,768]{2,1,0:T(8,128)(2,1)} %bitcast.241, bf16[4,3,768]{2,1,0:T(4,128)(2,1)} %collective-permute-done, ...), kind=kLoop, calls=%fused_computation.222 | loop fusion | flops 77066496 | bytes 25218048 | tf_op jit(solution)/shard_map/reduce_sum | solution.py:75
  530.7 11.2 add_add_fusion
  554.9 10.8 convolution_bitcast_fusion
  565.7 145.9 %all-reduce.12 = bf16[4,2,256,256]{2,3,1,0:T(8,128)(2,1)S(1)} all-reduce(f32[4,2,256,256]{2,3,1,0:T(8,128)} %copy.324), channel_id=1, replica_groups=mesh['seq'=8,'head'=4] {'head'}, use_global_device_ids=true, to_apply=%region_23.24 | all-reduce | flops 524288 | bytes 3145728 | tf_op jit(solution)/shard_map/psum | solution.py:243
  716.5 799.0 %all-reduce.11.cloned.1.call-done = (f32[4,512,1536]{2,1,0:T(8,128)}, f32[4,512,1536]{2,1,0:T(8,128)}, f32[4,2,256,128]{3,2,1,0:T(8,128)}, f32[4,2,256,128]{3,2,1,0:T(8,128)}) async-done(((f32[4,512,1536]{2,1,0:T(8,128)}, f32[4,512,1536]{2,1,0:T(8,128)}, f32[4,2,256,128]{3,2,1,0:T(8,128)}, f32[4,2,256,128]{3,2,1,0:T(8,128)}), (f32[4,512,1536]{2,1,0:T(8,128)}, f32[4,512,1536]{2,1,0:T(8,128)}, ...) | async-done | bytes 27262992 | tf_op jit(solution)/shard_map/psum | solution.py:178
  1538.4 13.7 fusion.16
  1552.1 27.9 %all-reduce.2 = (f32[1536]{0:T(1024)}, f32[4,768]{1,0:T(4,128)}, f32[768]{0:T(1024)}, f32[4,256]{1,0:T(4,128)}, f32[256]{0:T(256)}, /*index=5*/f32[12]{0:T(128)}, f32[12]{0:T(128)}, f32[12]{0:T(128)}, f32[768]{0:T(1024)}) all-reduce(f32[1536]{0:T(1024)S(1)} %get-tuple-element.282, ...), channel_id=1, replica_groups=mesh['seq'=8,'head'=4] {'seq'}, use_global_device_ids=true, to_apply=%region_27.28 | all-reduce | flops 7460 | bytes 59680 | tf_op jit(solution)/shard_map/psum | solution.py:297
  1580.0 21.1 %fusion.13 = (f32[4,512,1536]{2,1,0:T(8,128)}, bf16[4,512,1536]{2,1,0:T(8,128)(2,1)}) fusion(bf16[4,512,1536]{2,1,0:T(8,128)(2,1)} %param.26, bf16[4,512,1536]{2,1,0:T(8,128)(2,1)} %param.41, f32[4,512,1536]{2,1,0:T(8,128)} %get-tuple-element.381, f32[4,512]{1,0:T(4,128)S(1)} %broadcast_multiply_fusion.2, f32[4,512]{1,0:T(4,128)S(1)} %copy-done.65, ...), kind=kLoop, calls=%fused_computation.28 | loop fusion | flops 31457280 | bytes 56653824 | tf_op jit(solution)/shard_map/sub | solution.py:293
  1601.1 146.5 %all-reduce.9.cloned.1.call-done = (f32[1536,768]{1,0:T(8,128)}, f32[1536,768]{1,0:T(8,128)}, f32[1536,256]{1,0:T(8,128)}, f32[1536,12]{0,1:T(8,128)}, f32[768,1536]{1,0:T(8,128)}) async-done(((f32[1536,768]{1,0:T(8,128)}, f32[1536,768]{1,0:T(8,128)}, f32[1536,256]{1,0:T(8,128)}, f32[1536,12]{0,1:T(8,128)}, f32[768,1536]{1,0:T(8,128)}), (f32[1536,768]{1,0:T(8,128)}, f32[1536,768]{1,0:T(8,128)}, ...) | async-done | bytes 15802384 | tf_op jit(solution)/shard_map/psum | solution.py:297
  (384 shorter events, 355.9 us)
Async XLA Ops:
  7.2 220.5 %copy-start = (bf16[1536,768]{1,0:T(8,128)(2,1)S(1)}, bf16[1536,768]{1,0:T(8,128)(2,1)}, u32[]{:S(2)}) copy-start(bf16[1536,768]{1,0:T(8,128)(2,1)} %param.28) | copy-start | bytes 7077892
  7.2 153.4 %all-gather.4.cloned.1.call-start = ((), (), s32[]{:S(2)}) async-start(), calls=%async_computation | async-start | bytes 14155776 | tf_op jit(solution)/shard_map/all_gather | solution.py:21
  23.1 42.2 %collective-permute-start = (bf16[4,3,768]{2,1,0:T(4,128)(2,1)}, bf16[4,3,768]{2,1,0:T(4,128)(2,1)}, u32[]{:S(2)}, u32[]{:S(2)}) collective-permute-start(bf16[4,3,768]{2,1,0:T(4,128)(2,1)} %slice.268), channel_id=1, source_target_pairs={{0,4},{4,8},{8,12},{12,16},{16,20},{20,24},{24,28},{1,5},{5,9},{9,... | collective-permute-start | bytes 55304 | tf_op jit(solution)/shard_map/ppermute | solution.py:16
  28.8 31.8 %collective-permute-start.1 = (bf16[4,3,256]{2,1,0:T(4,128)(2,1)}, bf16[4,3,256]{2,1,0:T(4,128)(2,1)S(1)}, u32[]{:S(2)}, u32[]{:S(2)}) collective-permute-start(bf16[4,3,256]{2,1,0:T(4,128)(2,1)} %slice.273), channel_id=1, source_target_pairs={{0,4},{4,8},{8,12},{12,16},{16,20},{20,24},{24,28},{1,5},{5,9},{9,... | collective-permute-start | bytes 18440 | tf_op jit(solution)/shard_map/ppermute | solution.py:16
  35.7 53.0 %copy-start.12 = (f32[4,512,12]{2,0,1:T(4,128)}, f32[4,512,12]{2,0,1:T(4,128)S(1)}, u32[]{:S(2)}) copy-start(f32[4,512,12]{2,0,1:T(4,128)S(1)} %copy.350) | copy-start | bytes 294916
  56.8 45.0 %copy-start.66 = (f32[4,1,12]{2,1,0:T(1,128)}, f32[4,1,12]{2,1,0:T(1,128)S(1)}, u32[]{:S(2)}) copy-start(f32[4,1,12]{2,1,0:T(1,128)S(1)} %get-tuple-element.368) | copy-start | bytes 580
  56.8 131.1 %copy-start.68 = (f32[4,1,12]{2,1,0:T(1,128)}, f32[4,1,12]{2,1,0:T(1,128)S(1)}, u32[]{:S(2)}) copy-start(f32[4,1,12]{2,1,0:T(1,128)S(1)} %get-tuple-element.370) | copy-start | bytes 580
  88.0 297.4 %all-gather.6.cloned.1.call-start = ((), (), s32[]{:S(2)}) async-start(), calls=%async_computation.1 | async-start | bytes 14155776 | tf_op jit(solution)/shard_map/all_gather | solution.py:21
  91.4 184.1 %copy-start.61 = (f32[768]{0:T(1024)}, f32[768]{0:T(1024)S(1)}, u32[]{:S(2)}) copy-start(f32[768]{0:T(1024)S(1)} %mul.641) | copy-start | bytes 9220
  227.6 27.7 %copy-start.85 = (f32[768]{0:T(1024)S(1)}, f32[768]{0:T(1024)}, u32[]{:S(2)}) copy-start(f32[768]{0:T(1024)} %param.39) | copy-start | bytes 9220
  314.4 1201.1 %all-reduce.11.cloned.1.call-start = ((), (), s32[]{:S(2)}) async-start(), calls=%async_computation.3 | async-start | bytes 54525952 | tf_op jit(solution)/shard_map/psum | solution.py:178
  516.9 4.0 collective-permute-start.2
  541.9 1205.6 %all-reduce.9.cloned.1.call-start = ((), (), s32[]{:S(2)}) async-start(), calls=%async_computation.2 | async-start | bytes 31653888 | tf_op jit(solution)/shard_map/psum | solution.py:297
  711.6 803.9 %copy-start.25 = (bf16[4,512,128]{2,1,0:T(8,128)(2,1)S(1)}, bf16[4,512,128]{2,1,0:T(8,128)(2,1)}, u32[]{:S(2)}) copy-start(bf16[4,512,128]{2,1,0:T(8,128)(2,1)} %get-tuple-element.361) | copy-start | bytes 1572868
  711.7 805.7 %copy-start.23 = (bf16[4,512,128]{2,1,0:T(8,128)(2,1)S(1)}, bf16[4,512,128]{2,1,0:T(8,128)(2,1)}, u32[]{:S(2)}) copy-start(bf16[4,512,128]{2,1,0:T(8,128)(2,1)} %get-tuple-element.360) | copy-start | bytes 1572868
  716.5 802.6 %copy-start.21 = (bf16[2048,256]{1,0:T(8,128)(2,1)S(1)}, bf16[2048,256]{1,0:T(8,128)(2,1)}, u32[]{:S(2)}) copy-start(bf16[2048,256]{1,0:T(8,128)(2,1)} %copy-done.20) | copy-start | bytes 3145732
  716.5 802.6 %copy-start.64 = (bf16[4,3,256]{2,1,0:T(4,128)(2,1)S(1)}, bf16[4,3,256]{2,1,0:T(4,128)(2,1)}, u32[]{:S(2)}) copy-start(bf16[4,3,256]{2,1,0:T(4,128)(2,1)} %copy-done.63) | copy-start | bytes 18436
  716.5 802.6 %copy-start.73 = (f32[1,256]{1,0:T(1,128)S(1)}, f32[1,256]{1,0:T(1,128)}, u32[]{:S(2)}) copy-start(f32[1,256]{1,0:T(1,128)} %copy-done.72) | copy-start | bytes 3076
  716.5 802.6 %copy-start.75 = (f32[1,256]{1,0:T(1,128)S(1)}, f32[1,256]{1,0:T(1,128)}, u32[]{:S(2)}) copy-start(f32[1,256]{1,0:T(1,128)} %copy-done.74) | copy-start | bytes 3076
  716.5 802.7 %copy-start.77 = (f32[1,256]{1,0:T(1,128)S(1)}, f32[1,256]{1,0:T(1,128)}, u32[]{:S(2)}) copy-start(f32[1,256]{1,0:T(1,128)} %copy-done.76) | copy-start | bytes 3076
  716.5 802.7 %copy-start.79 = (f32[1,256]{1,0:T(1,128)S(1)}, f32[1,256]{1,0:T(1,128)}, u32[]{:S(2)}) copy-start(f32[1,256]{1,0:T(1,128)} %copy-done.78) | copy-start | bytes 3076
  716.5 802.7 %copy-start.88 = (f32[256]{0:T(256)S(1)}, f32[256]{0:T(256)}, u32[]{:S(2)}) copy-start(f32[256]{0:T(256)} %param.35) | copy-start | bytes 3076
  1522.8 8.4 collective-permute-start.3
  1538.4 41.7 %copy-start.65 = (f32[4,512]{1,0:T(4,128)S(1)}, f32[4,512]{1,0:T(4,128)}, u32[]{:S(2)}) copy-start(f32[4,512]{1,0:T(4,128)} %get-tuple-element.364) | copy-start | bytes 24580
  (87 other events, 661.0 us)
Sparse Core Ops, SparseCore 0:
  88.1 72.4 all-gather.3
  314.5 70.7 all-gather.5
  542.1 973.4 all-reduce.10
  1537.3 210.1 all-reduce.8
where the time goes:
time: 1780 us; the launch traced here: 1770 us
  waiting for transfers between devices  996 us (56%)
  matrix products  221 us (12%)
  blocking collectives  205 us (12%)
  other arithmetic  164 us (9%)
  local copies, waits for them, and re-layouts  156 us (9%)
    psum x1, waiting for transfers between devices, shards(): summed = lax.psum(branch_out, 'head')  799 us
    psum x1, waiting for transfers between devices, shards(): lax.psum((norm_gain_grad, gate_weight_grad, value_weight_grad, state_weig...  146 us
    psum x1, blocking collectives, shards(): cross_all, b_total, c_total = lax.psum((cross_part, b_grad, c_grad), 'head')  146 us
    dot_general x5, matrix products, outer_dot(): lax.dot_general(left, right, (((1,), (1,)), ((), ())), preferred_element_...  54.8 us
    all_gather x2, waiting for transfers between devices, entering(): pieces = jax.tree.map(lambda part: lax.all_gather(part, axis), value)  50.5 us
    dot_general x5, matrix products, inner_product_fn(): lax.dot_general(left, right, (((0,), (0,)), ((), ())), preferred_element_...  37.8 us
  transfers between devices with their start and end apart: 8, of which 4 were waited for; matrix products, arithmetic and copies ran while one was open for 10% of the time, Pallas kernels for 0%

commit v1 on v0

v1 whole, which is shorter than its diff:
```python
import functools

import jax
import jax.numpy as jnp
from jax import lax
from jax.experimental import pallas as pl
from jax.experimental.pallas import tpu as pltpu
from jax.sharding import PartitionSpec as P

EPS = 1e-05
T = 128
HALO = 16
LANES = 128
F32 = jnp.float32
BF16 = jnp.bfloat16


def mm(a, b):
    return lax.dot_general(a, b, (((1,), (0,)), ((), ())), preferred_element_type=F32)


def mm_t(a, b):
    return lax.dot_general(a, b, (((1,), (1,)), ((), ())), preferred_element_type=F32)


def t_mm(a, b):
    return lax.dot_general(a, b, (((0,), (0,)), ((), ())), preferred_element_type=F32)


def split(v, parts):
    pieces = []
    for _ in range(parts):
        piece = v.astype(BF16)
        pieces.append(piece)
        v = v - piece.astype(F32)
    return pieces


def expand(v, wide):
    return mm(jnp.concatenate(split(v, 2), axis=1), wide)


def expand_row(v, wide):
    return expand(jnp.broadcast_to(v, (16, LANES)), wide)[0:1]


def head_sum(v, wide):
    hi, lo = split(v, 2)
    return mm_t(hi, wide[:LANES]) + mm_t(lo, wide[:LANES])


def exact_tri(tri, v):
    a, b, c = split(v, 3)
    return mm(tri, a) + (mm(tri, b) + mm(tri, c))


def sigmoid(v):
    return 0.5 * jnp.tanh(0.5 * v) + 0.5


def softplus(v):
    return jnp.maximum(v, 0.0) + jnp.log(1.0 + jnp.exp(-jnp.abs(v)))


def lower():
    row = lax.broadcasted_iota(jnp.int32, (T, T), 0)
    col = lax.broadcasted_iota(jnp.int32, (T, T), 1)
    return row >= col


def half_mask(rows):
    return lax.broadcasted_iota(jnp.int32, (rows, LANES), 1) < LANES // 2


def pair_rows(v):
    left = half_mask(v.shape[0])
    zero = jnp.zeros_like(v)
    return jnp.concatenate([jnp.where(left, v, zero), jnp.where(left, zero, v)], axis=0)


def rows_of(b):
    return pl.ds(pl.multiple_of(b * T, T), T)


def front(
    tok, halo, ngain, gate_w, value_w, state_w, step_w, vk, vo, sk, so, sbias, rate, wide, tri,
    normed_o, gate_o, xext_o, bcext_o, sraw_o, xact_o, bcact_o, step_o, cum_o, lstart_o, lstate_o, pre_o,
    nx, xe, be, st, run,
):
    length = tok.shape[1]
    blocks = length // T
    n = bcact_o.shape[2] // 2

    def norm(v):
        v = v.astype(F32)
        inv = lax.rsqrt(jnp.mean(v * v, axis=1, keepdims=True) + EPS)
        return (v * inv * ngain[...]).astype(BF16)

    nx[0:HALO] = norm(halo[0])

    def norm_rows(b, _):
        r = rows_of(b)
        v = norm(tok[0, r, :])
        nx[pl.ds(pl.multiple_of(HALO + b * T, HALO), T), :] = v
        normed_o[0, r, :] = v
        return 0

    lax.fori_loop(0, blocks, norm_rows, 0)
    x = mm(nx[...], value_w[...]).astype(BF16)
    xext_o[0] = x
    xe[...] = x.astype(F32)
    bc = mm(nx[...], state_w[...]).astype(BF16)
    bcext_o[0] = bc
    be[...] = bc.astype(F32)
    gate_o[0] = mm(nx[HALO:], gate_w[...])
    sraw_o[0] = mm(nx[HALO:], step_w[...])
    st[...] = jnp.zeros_like(st)
    run[...] = jnp.zeros_like(run)
    pre_o[0] = jnp.zeros_like(pre_o[0])
    for b in range(blocks):
        r0 = b * T
        r = slice(r0, r0 + T)
        taps = vk.shape[0]
        base = HALO - taps + 1
        xc = vo[...] + vk[0:1] * xe[r0 + base : r0 + base + T]
        bcc = so[...] + sk[0:1] * be[r0 + base : r0 + base + T]
        for k in range(1, taps):
            xc = xc + vk[k : k + 1] * xe[r0 + base + k : r0 + base + k + T]
            bcc = bcc + sk[k : k + 1] * be[r0 + base + k : r0 + base + k + T]
        xa = (xc * sigmoid(xc)).astype(BF16)
        bca = (bcc * sigmoid(bcc)).astype(BF16)
        xact_o[0, r, :] = xa
        bcact_o[0, r, :] = bca
        step = softplus(sraw_o[0, r, :] + sbias[...])
        cum = exact_tri(tri[...], step * rate[...])
        step_o[0, r, :] = step
        cum_o[0, r, :] = cum
        last = cum[T - 1 : T]
        weight = jnp.exp(last - cum) * step
        weighted = (xa.astype(F32) * expand(weight, wide[...])).astype(BF16)
        contrib = t_mm(bca[:, :n], weighted)
        lstart_o[0, b] = st[...].astype(BF16)
        st[...] = expand_row(jnp.exp(last), wide[...]) * st[...] + contrib
        run[0:1] = run[0:1] + last
        pre_o[0, b + 1 : b + 2] = run[0:1]
    lstate_o[0, 0:n] = st[...].astype(BF16)
    hi, mid, lo = split(expand_row(run[0:1], wide[...]), 3)
    at = lax.broadcasted_iota(jnp.int32, (HALO, hi.shape[1]), 0)
    hi, mid, lo = [jnp.broadcast_to(v.astype(F32), at.shape) for v in (hi, mid, lo)]
    tail = jnp.where(at == 0, hi, jnp.where(at == 1, mid, jnp.where(at == 2, lo, 0.0)))
    lstate_o[0, n : n + HALO] = tail.astype(BF16)


def scan_out(
    xact, bcact, step_i, cum_i, gate, lstart, entry, pre, cot, out_w, mgain, skip, wide,
    ssd_o, gn_o, y_o, sums_o,
    gm,
):
    length = xact.shape[1]
    blocks = length // T
    n = bcact.shape[2] // 2
    inner = xact.shape[2]
    gn_o[0] = mm_t(cot[0], out_w[...])

    def block(b, _):
        r = rows_of(b)
        xa = xact[0, r, :]
        bca = bcact[0, r, :]
        bm, cm = bca[:, :n], bca[:, n:]
        cum = cum_i[0, r, :]
        cum_t = cum.T
        cross = jnp.where(lower(), mm_t(cm, bm), 0.0)
        start = expand_row(jnp.exp(pre[0, pl.ds(b, 1), :]), wide[...]) * entry[0] + lstart[0, b].astype(F32)
        across = expand(jnp.exp(cum), wide[...]) * mm(cm, start.astype(BF16))
        xs = (xa.astype(F32) * expand(step_i[0, r, :], wide[...])).astype(BF16)
        for p in range(inner // LANES):
            mix = []
            for h in (2 * p, 2 * p + 1):
                decay = jnp.exp(jnp.minimum(cum[:, h : h + 1] - cum_t[h : h + 1, :], 0.0))
                mix.append((cross * decay).astype(BF16))
            lanes = slice(p * LANES, (p + 1) * LANES)
            within = mm(jnp.concatenate(mix, axis=1), pair_rows(xs[:, lanes]))
            ssd_o[0, r, lanes] = within + across[:, lanes]
        mixed = ssd_o[0, r, :] + skip[...] * xa.astype(F32)
        g = gate[0, r, :]
        gated = mixed * (g * sigmoid(g))
        gg = gated * mgain[...]
        gm[r, :] = gg.astype(BF16)
        squares = jnp.sum(gated * gated, axis=1, keepdims=True)
        dots = jnp.sum(gg * gn_o[0, r, :], axis=1, keepdims=True)
        lane = lax.broadcasted_iota(jnp.int32, (T, LANES), 1)
        both = jnp.where(lane == 0, squares, jnp.where(lane == 1, dots, 0.0))
        sums_o[0, :, r] = both.T[0:8]
        return 0

    lax.fori_loop(0, blocks, block, 0)
    y_o[0] = mm(gm[...], out_w[...]).astype(BF16)


def back_one(
    xact, bcact, step_i, cum_i, gate, ssd, gn, sums, lstart, entry, pre, mgain, skip, wide,
    gnormed_o, gate_grad_o, xg_o, cumg_o, stepg_o, bcg_o, lend_o, lgrad_o, mgg_o, skg_o,
    z, acc,
    *, inner_all,
):
    length = xact.shape[1]
    blocks = length // T
    n = bcact.shape[2] // 2
    inner = xact.shape[2]

    @pl.when(pl.program_id(0) == 0)
    def _():
        mgg_o[...] = jnp.zeros_like(mgg_o)
        skg_o[...] = jnp.zeros_like(skg_o)

    acc[...] = jnp.zeros_like(acc)

    def block(i, _):
        b = blocks - 1 - i
        r = rows_of(b)
        low_x = xact[0, r, :]
        xa = low_x.astype(F32)
        bca = bcact[0, r, :]
        bm, cm = bca[:, :n], bca[:, n:]
        cum = cum_i[0, r, :]
        cum_t = cum.T
        sums_b = sums[0, :, r]
        columns = jnp.concatenate([sums_b, jnp.zeros((LANES - 8, T), F32)], axis=0).T
        rms = lax.rsqrt(columns[:, 0:1] / inner_all + EPS)
        coef = rms * rms * rms * (columns[:, 1:2] / inner_all)
        ssd_b = ssd[0, r, :]
        mixed = ssd_b + skip[...] * xa
        g = gate[0, r, :]
        sg = sigmoid(g)
        gated = mixed * (g * sg)
        grad_norm = gn[0, r, :]
        normalised = gated * rms
        gnormed_o[0, r, :] = (normalised * mgain[...]).astype(BF16)
        mgg_o[0:1] += jnp.sum(grad_norm * normalised, axis=0, keepdims=True)
        grad_gated = rms * (grad_norm * mgain[...]) - gated * coef
        gate_grad_o[0, r, :] = (grad_gated * mixed * (sg * (1.0 + g * (1.0 - sg)))).astype(BF16)
        grad_mixed = grad_gated * (g * sg)
        skg_o[0:1] += jnp.sum(grad_mixed * xa, axis=0, keepdims=True)
        dy = grad_mixed.astype(BF16)
        start = expand_row(jnp.exp(pre[0, pl.ds(b, 1), :]), wide[...]) * entry[0] + lstart[0, b].astype(F32)
        gdy = (expand(jnp.exp(cum), wide[...]) * dy.astype(F32)).astype(BF16)
        c_grad = mm_t(gdy, start.astype(BF16))
        lend_o[0, b] = acc[...].astype(BF16)
        acc[...] = expand_row(jnp.exp(cum[T - 1 : T]), wide[...]) * acc[...] + t_mm(cm, gdy)
        step_wide = expand(step_i[0, r, :], wide[...])
        xs = (xa * step_wide).astype(BF16)
        cross = jnp.where(lower(), mm_t(cm, bm), 0.0)
        cross_part = jnp.zeros((T, T), F32)
        for p in range(inner // LANES):
            lanes = slice(p * LANES, (p + 1) * LANES)
            dy_two = pair_rows(dy[:, lanes])
            mix_grad = mm_t(dy_two, xs[:, lanes])
            mix = []
            for j in (0, 1):
                h = 2 * p + j
                decay = jnp.exp(jnp.minimum(cum[:, h : h + 1] - cum_t[h : h + 1, :], 0.0))
                mix.append((cross * decay).astype(BF16))
                cross_part = cross_part + mix_grad[j * T : (j + 1) * T] * decay
            z[:, lanes] = t_mm(jnp.concatenate(mix, axis=0), dy_two)
        cross_low = jnp.where(lower(), cross_part, 0.0).astype(BF16)
        bcg_o[0, r, 0:n] = t_mm(cross_low, cm)
        bcg_o[0, r, n : 2 * n] = c_grad + mm(cross_low, bm)
        zz = z[...]
        xg_o[0, r, :] = step_wide * zz + skip[...] * grad_mixed
        cumg_o[0, r, :] = head_sum(dy.astype(F32) * ssd_b - xs.astype(F32) * zz, wide[...])
        stepg_o[0, r, :] = head_sum(xa * zz, wide[...])
        return 0

    lax.fori_loop(0, blocks, block, 0)
    lgrad_o[0] = acc[...].astype(BF16)


def back_two(
    xact, bcact, xext, bcext, step_i, cum_i, sraw, xg, cumg, stepg, bcg, lstart, entry, lend, after, pre,
    vk, vo, sk, so, sbias, rate, wide, tri,
    xpg_o, xhalo_o, bpg_o, bhalo_o, raw_o, vkg_o, skg_o, heads_o,
    xe, be, xcg, bcg_s,
):
    length = xact.shape[1]
    blocks = length // T
    n = bcact.shape[2] // 2
    taps = vk.shape[0]
    base = HALO - taps + 1

    @pl.when(pl.program_id(0) == 0)
    def _():
        vkg_o[...] = jnp.zeros_like(vkg_o)
        skg_o[...] = jnp.zeros_like(skg_o)
        heads_o[...] = jnp.zeros_like(heads_o)

    xe[...] = xext[0].astype(F32)
    be[...] = bcext[0].astype(F32)
    for ref in (xcg, bcg_s):
        ref[0:HALO] = jnp.zeros((HALO, ref.shape[1]), F32)
        ref[HALO + length :] = jnp.zeros((HALO, ref.shape[1]), F32)

    def conv_rows(ext, kernel, offset, r0):
        total = offset[...] + kernel[0:1] * ext[r0 + base : r0 + base + T]
        for k in range(1, taps):
            total = total + kernel[k : k + 1] * ext[r0 + base + k : r0 + base + k + T]
        sg = sigmoid(total)
        return sg * (1.0 + total * (1.0 - sg))

    def filter_grad(grad, ext, out, r0):
        for k in range(taps):
            out[k : k + 1] += jnp.sum(grad * ext[r0 + base + k : r0 + base + k + T], axis=0, keepdims=True)
        out[taps : taps + 1] += jnp.sum(grad, axis=0, keepdims=True)

    for b in range(blocks):
        r0 = b * T
        r = slice(r0, r0 + T)
        xa = xact[0, r, :].astype(F32)
        bm = bcact[0, r, 0:n]
        cum = cum_i[0, r, :]
        step = step_i[0, r, :]
        last = cum[T - 1 : T]
        start = expand_row(jnp.exp(pre[0, b : b + 1]), wide[...]) * entry[0] + lstart[0, b].astype(F32)
        suffix = jnp.exp(pre[0, blocks : blocks + 1] - pre[0, b + 1 : b + 2])
        end = expand_row(suffix, wide[...]) * after[0] + lend[0, b].astype(F32)
        end_low = end.astype(BF16)
        weighted_grad = mm(bm, end_low)
        reach = jnp.exp(last - cum)
        weight = reach * step
        weight_wide = expand(weight, wide[...])
        weighted = (xa * weight_wide).astype(BF16)
        bcg_b = bcg[0, r, :]
        b_total = bcg_b[:, 0:n] + mm_t(weighted, end_low)
        bc_total = jnp.concatenate([b_total, bcg_b[:, n:]], axis=1)
        w_grad = head_sum(weighted_grad * xa, wide[...])
        part = w_grad * weight
        product = jnp.broadcast_to(jnp.sum(end * start, axis=0, keepdims=True), (16, end.shape[1]))
        fade_grad = jnp.exp(last) * head_sum(product, wide[...])[0:1]
        at_last = lax.broadcasted_iota(jnp.int32, (T, LANES), 0) == T - 1
        extra = fade_grad + jnp.sum(part, axis=0, keepdims=True)
        cum_grad = cumg[0, r, :] - part + jnp.where(at_last, extra, 0.0)
        a, bb, c = split(cum_grad, 3)
        rise = t_mm(tri[...], a) + (t_mm(tri[...], bb) + t_mm(tri[...], c))
        step_grad = stepg[0, r, :] + w_grad * reach + rise * rate[...]
        raw = step_grad * sigmoid(sraw[0, r, :] + sbias[...])
        raw_o[0, r, :] = raw.astype(BF16)
        heads_o[0:1] += jnp.sum(raw, axis=0, keepdims=True)
        heads_o[1:2] += jnp.sum(rise * step, axis=0, keepdims=True)
        grad = (xg[0, r, :] + weighted_grad * weight_wide) * conv_rows(xe, vk, vo, r0)
        filter_grad(grad, xe, vkg_o, r0)
        xcg[HALO + r0 : HALO + r0 + T] = grad
        grad = bc_total * conv_rows(be, sk, so, r0)
        filter_grad(grad, be, skg_o, r0)
        bcg_s[HALO + r0 : HALO + r0 + T] = grad

    def conv_back(ref, kernel, r0, rows):
        total = kernel[0:1] * ref[r0 + taps - 1 : r0 + taps - 1 + rows]
        for k in range(1, taps):
            total = total + kernel[k : k + 1] * ref[r0 + taps - 1 - k : r0 + taps - 1 - k + rows]
        return total.astype(BF16)

    xhalo_o[0] = conv_back(xcg, vk, 0, HALO)
    bhalo_o[0] = conv_back(bcg_s, sk, 0, HALO)
    for b in range(blocks):
        r0 = b * T
        xpg_o[0, r0 : r0 + T] = conv_back(xcg, vk, HALO + r0, T)
        bpg_o[0, r0 : r0 + T] = conv_back(bcg_s, sk, HALO + r0, T)


def per_seq(shape):
    rest = shape[1:]
    return pl.BlockSpec((1,) + tuple(rest), lambda s: (s,) + (0,) * len(rest))


def whole(shape):
    return pl.BlockSpec(tuple(shape), lambda s: (0,) * len(shape))


def call(body, seqs, ins, outs, scratch, flops):
    in_specs = [per_seq(a.shape) if a.ndim >= 3 else whole(a.shape) for a in ins]
    out_specs = [per_seq(s) if cut else whole(s) for s, _, cut in outs]
    moved = sum(a.size * a.dtype.itemsize for a in ins)
    for s, d, _ in outs:
        size = jnp.dtype(d).itemsize
        for k in s:
            size *= k
        moved += size
    return pl.pallas_call(
        body,
        grid=(seqs,),
        in_specs=in_specs,
        out_specs=out_specs,
        out_shape=[jax.ShapeDtypeStruct(s, d) for s, d, _ in outs],
        scratch_shapes=scratch,
        compiler_params=pltpu.CompilerParams(
            dimension_semantics=("arbitrary",), vmem_limit_bytes=56 * 1024 * 1024
        ),
        cost_estimate=pl.CostEstimate(flops=flops, bytes_accessed=moved, transcendentals=0),
    )(*ins)


def shards(
    tokens, norm_gain, gate_weight, value_weight, state_weight, step_weight, value_kernel, value_offset,
    state_kernel, state_offset, step_bias, log_rate, skip_gain, mixer_gain, out_weight, cotangent,
):
    seqs, length, width = tokens.shape
    flat = seqs * length
    inner = gate_weight.shape[1]
    heads = step_weight.shape[1]
    head_size = inner // heads
    n2 = state_weight.shape[1]
    n = n2 // 2
    taps = value_kernel.shape[0]
    blocks = length // T
    devices, me = lax.axis_size("seq"), lax.axis_index("seq")
    inner_all = inner * lax.axis_size("head")

    halo = lax.ppermute(tokens[:, length - HALO :], "seq", [(i, i + 1) for i in range(devices - 1)])
    pad = LANES - heads
    rate_row = -jnp.exp(log_rate)
    rate = jnp.pad(rate_row, (0, pad))[None]
    bias = jnp.pad(step_bias, (0, pad))[None]
    step_w = jnp.pad(step_weight, ((0, 0), (0, pad)))
    skip = jnp.repeat(skip_gain, head_size)[None]
    gain = mixer_gain[None]
    one = (jnp.arange(inner)[None, :] // head_size == jnp.arange(LANES)[:, None]).astype(BF16)
    wide = jnp.concatenate([one, one], axis=0)
    tri = (jnp.arange(T)[:, None] >= jnp.arange(T)[None, :]).astype(BF16)
    vo, so = value_offset[None], state_offset[None]

    def big(cols, dtype, rows=length):
        return ((seqs, rows, cols), dtype, True)

    vmem = pltpu.VMEM
    ext = length + HALO
    (normed, gate, xext, bcext, sraw, xact, bcact, step, cum, lstart, lstate, pre) = call(
        front, seqs,
        [tokens, halo, norm_gain[None], gate_weight, value_weight, state_weight, step_w,
         value_kernel, vo, state_kernel, so, bias, rate, wide, tri],
        [big(width, BF16), big(inner, F32), big(inner, BF16, ext), big(n2, BF16, ext), big(LANES, F32),
         big(inner, BF16), big(n2, BF16), big(LANES, F32), big(LANES, F32),
         ((seqs, blocks, n, inner), BF16, True), big(inner, BF16, n + HALO), big(LANES, F32, 8)],
        [vmem((ext, width), BF16), vmem((ext, inner), F32), vmem((ext, n2), F32), vmem((n, inner), F32),
         vmem((8, LANES), F32)],
        2 * flat * width * (2 * inner + n2 + LANES),
    )
    states = lax.all_gather(lstate, "seq")
    log_fade = jnp.sum(states[:, :, n : n + 3].astype(F32), axis=2)
    index = jnp.arange(devices)
    prefix = jnp.cumsum(log_fade, axis=0)
    zero = jnp.zeros_like(prefix[:1])
    before = jnp.concatenate([zero, prefix[:-1]], axis=0)
    my_before = lax.dynamic_index_in_dim(before, me, 0)
    my_prefix = lax.dynamic_index_in_dim(prefix, me, 0)
    earlier = (index < me)[:, None, None]
    later = (index > me)[:, None, None]
    from_left = jnp.where(earlier, jnp.exp(jnp.where(earlier, my_before - prefix, 0.0)), 0.0)
    from_right = jnp.where(later, jnp.exp(jnp.where(later, before - my_prefix, 0.0)), 0.0)
    entry = jnp.sum(from_left[:, :, None] * states[:, :, :n].astype(F32), axis=0)

    ssd, gn, y, sums = call(
        scan_out, seqs,
        [xact, bcact, step, cum, gate, lstart, entry, pre, cotangent, out_weight, gain, skip, wide],
        [big(inner, F32), big(inner, F32), big(width, BF16), ((seqs, 8, length), F32, True)],
        [vmem((length, inner), BF16)],
        4 * flat * width * inner,
    )
    y = lax.psum(y, "head")
    sums = lax.psum(sums, "head")
    gnormed, gate_grad, xg, cumg, stepg, bcg, lend, lgrad, mgg, skg = call(
        functools.partial(back_one, inner_all=inner_all), seqs,
        [xact, bcact, step, cum, gate, ssd, gn, sums, lstart, entry, pre, gain, skip, wide],
        [big(inner, BF16), big(inner, BF16), big(inner, F32), big(LANES, F32), big(LANES, F32), big(n2, F32),
         ((seqs, blocks, n, inner), BF16, True), big(inner, BF16, n),
         ((8, inner), F32, False), ((8, inner), F32, False)],
        [vmem((T, inner), F32), vmem((n, inner), F32)],
        2 * flat * T * inner * 8,
    )
    grads = lax.all_gather(lgrad, "seq")
    after = jnp.sum(from_right[:, :, None] * grads.astype(F32), axis=0)
    xpg, xhalo, bpg, bhalo, raw, vkg, skgr, head_rows = call(
        back_two, seqs,
        [xact, bcact, xext, bcext, step, cum, sraw, xg, cumg, stepg, bcg, lstart, entry, lend, after, pre,
         value_kernel, vo, state_kernel, so, bias, rate, wide, tri],
        [big(inner, BF16), big(inner, BF16, HALO), big(n2, BF16), big(n2, BF16, HALO), big(LANES, BF16),
         ((8, inner), F32, False), ((8, n2), F32, False), ((8, LANES), F32, False)],
        [vmem((ext, inner), F32), vmem((ext, n2), F32), vmem((ext + HALO, inner), F32),
         vmem((ext + HALO, n2), F32)],
        2 * flat * T * inner * 4,
    )
    back = [(i + 1, i) for i in range(devices - 1)]
    xhalo, bhalo = lax.ppermute((xhalo, bhalo), "seq", back)
    xpg = xpg.at[:, length - HALO :].add(xhalo)
    bpg = bpg.at[:, length - HALO :].add(bhalo)

    def flatten(v):
        return v.reshape(flat, v.shape[-1])

    normed_f, xpg_f, bpg_f, raw_f, gg_f = [flatten(v) for v in (normed, xpg, bpg, raw, gate_grad)]
    out_weight_grad = t_mm(flatten(gnormed), flatten(cotangent)).astype(BF16)
    gate_weight_grad = t_mm(normed_f, gg_f).astype(BF16)
    value_weight_grad = t_mm(normed_f, xpg_f).astype(BF16)
    state_weight_grad = t_mm(normed_f, bpg_f).astype(BF16)
    step_weight_grad = t_mm(normed_f, raw_f)[:, :heads].astype(BF16)
    normed_grad = (
        mm_t(gg_f, gate_weight) + mm_t(xpg_f, value_weight) + mm_t(bpg_f, state_weight) + mm_t(raw_f, step_w)
    ).astype(BF16)
    normed_grad = lax.psum(normed_grad, "head").astype(F32).reshape(seqs, length, width)

    resid = tokens.astype(F32)
    inv_rms = lax.rsqrt(jnp.mean(resid * resid, axis=-1, keepdims=True) + EPS)
    mixer_rms = lax.rsqrt(sums[:, 0] / inner_all + EPS)[..., None]
    result = (resid + y.astype(F32) * mixer_rms).astype(BF16)
    norm_gain_grad = jnp.sum(normed_grad * resid * inv_rms, axis=(0, 1))
    scaled_in = normed_grad * norm_gain
    tokens_grad = (
        cotangent.astype(F32)
        + inv_rms * scaled_in
        - resid * inv_rms**3 * (jnp.sum(scaled_in * resid, axis=-1, keepdims=True) / width)
    )
    skip_gain_grad = jnp.sum(skg[0].reshape(heads, head_size), axis=1)
    step_bias_grad = head_rows[0, :heads]
    log_rate_grad = head_rows[1, :heads] * rate_row
    own = lax.psum(
        (norm_gain_grad, vkg[: taps + 1], step_bias_grad, log_rate_grad, skip_gain_grad, mgg[0]), "seq"
    )
    norm_gain_grad, vkg, step_bias_grad, log_rate_grad, skip_gain_grad, mixer_gain_grad = own
    skgr = lax.psum(skgr[: taps + 1], ("seq", "head"))
    weights = lax.psum((gate_weight_grad, value_weight_grad, step_weight_grad, out_weight_grad), "seq")
    gate_weight_grad, value_weight_grad, step_weight_grad, out_weight_grad = [v.astype(F32) for v in weights]
    state_weight_grad = lax.psum(state_weight_grad, ("seq", "head")).astype(F32)
    return (
        result, tokens_grad, norm_gain_grad, gate_weight_grad, value_weight_grad, state_weight_grad,
        step_weight_grad, vkg[:taps], vkg[taps], skgr[:taps], skgr[taps], step_bias_grad, log_rate_grad,
        skip_gain_grad, mixer_gain_grad, out_weight_grad,
    )


def solution(mesh):
    rows, cols, vec = P(None, "seq", None), P(None, "head"), P("head")
    in_specs = (rows, P(), cols, cols, P(), cols, cols, vec, P(), P(), vec, vec, vec, vec, P("head", None), rows)
    out_specs = (rows, rows, P(), cols, cols, P(), cols, cols, vec, P(), P(), vec, vec, vec, vec, P("head", None))
    return jax.shard_map(shards, mesh=mesh, in_specs=in_specs, out_specs=out_specs, check_vma=False)
```

time: 1780 us -> 1060 us (0.60)
  waiting for transfers between devices: 996 us -> 654 us
  matrix products: 221 us -> 78.1 us
  local copies, waits for them, and re-layouts: 156 us -> 13.3 us
  Pallas kernels: 0 us -> 131 us
  blocking collectives: 205 us -> 91.1 us
  other arithmetic: 164 us -> 58.4 us
    psum x2 -> x4, waiting for transfers between devices: 946 us -> 568 us  [the longest x1 419 us: shards(): y = lax.psum(y, 'head')]
    dot_general x29 -> x9, matrix products: 221 us -> 78.1 us  [the longest x4 40.9 us: mm_t(): lax.dot_general(a, b, (((1,), (1,)), ((), ())), preferred_element_type=F32)]
    pallas_call x0 -> x4, Pallas kernels: none -> 131 us  [call(): pl.pallas_call(body, grid=(seqs,), in_specs=in_specs, out_specs=out_specs...]
    psum x4 -> x3, blocking collectives: 195 us -> 91.1 us  [the longest x1 42 us: shards(): skgr = lax.psum(skgr[:taps + 1], ('seq', 'head'))]
    reshape x8 -> x0, local copies, waits for them, and re-layouts: 42.9 us -> none  [the longest x2 15.6 us: shards(): x_grad.reshape(seqs, length, inner_loc) + skip_wide * grad_mixed]
    all_gather x2, waiting for transfers between devices: 50.5 us -> 85.9 us  [the longest x1 50.2 us: shards(): states = lax.all_gather(lstate, 'seq')]
    select_n x14 -> x3, other arithmetic: 34.9 us -> 0.21 us  [the longest x1 0.1 us: shards(): jnp.where(earlier, jnp.exp(jnp.where(earlier, my_before - prefix, 0.0)),...]
    another operation x10 -> x1, other arithmetic: 32.6 us -> 0.02 us  [shards(): prefix = jnp.cumsum(log_fade, axis=0)]
  transfers between devices with their start and end apart: 8 -> 9, of which waited for: 4 -> 6; matrix products, arithmetic and copies ran while one was open for 10% -> 11% of each run, Pallas kernels for 0% -> 0%
where the time goes in v1:
time: 1060 us; the launch traced here: 1050 us
  waiting for transfers between devices  654 us (62%)
  Pallas kernels  131 us (12%)
  blocking collectives  91.1 us (9%)
  matrix products  78.1 us (7%)
  other arithmetic  58.4 us (6%)
  between operations  14.6 us (1%)
  local copies, waits for them, and re-layouts  13.3 us (1%)
    psum x1, waiting for transfers between devices, shards(): y = lax.psum(y, 'head')  419 us
    pallas_call x4, Pallas kernels, call(): pl.pallas_call(body, grid=(seqs,), in_specs=in_specs, out_specs=out_specs...  131 us
    psum x1, waiting for transfers between devices, shards(): lax.psum((gate_weight_grad, value_weight_grad, step_weight_grad, out_weig...  114 us
    all_gather x1, waiting for transfers between devices, shards(): states = lax.all_gather(lstate, 'seq')  50.2 us
    psum x1, blocking collectives, shards(): skgr = lax.psum(skgr[:taps + 1], ('seq', 'head'))  42 us
    dot_general x4, matrix products, mm_t(): lax.dot_general(a, b, (((1,), (1,)), ((), ())), preferred_element_type=F32)  40.9 us
    dot_general x5, matrix products, t_mm(): lax.dot_general(a, b, (((0,), (0,)), ((), ())), preferred_element_type=F32)  37.2 us
    all_gather x1, waiting for transfers between devices, shards(): grads = lax.all_gather(lgrad, 'seq')  35.7 us
  transfers between devices with their start and end apart: 9, of which 6 were waited for; matrix products, arithmetic and copies ran while one was open for 11% of the time, Pallas kernels for 0%

profile of v1, /device:TPU:0, one launch (start us, length us, event | category | flops | bytes accessed | tf_op | source)
XLA Modules:
  0.0 1046.8 jit_solution(542084202357104950)
XLA Ops:
  19.0 32.4 %shard_map.279 = (bf16[4,512,1536]{2,1,0:T(8,128)(2,1)}, f32[4,512,768]{2,1,0:T(8,128)}, bf16[4,528,768]{2,1,0:T(8,128)(2,1)}, bf16[4,528,256]{2,1,0:T(8,128)(2,...) custom-call(bf16[4,512,1536]{2,1,0:T(8,128)(2,1)} %tok.1, ...), custom_call_target="tpu_custom_call" | custom-call | flops 12079595520 | bytes 41135104 | tf_op jit(solution)/shard_map/pallas_call | solution.py:387
  52.8 50.2 %all-gather.5.cloned.1.call-done = bf16[32,144,768]{2,1,0:T(8,128)(2,1)} async-done(((bf16[4,144,768]{2,1,0:T(8,128)(2,1)}), bf16[32,144,768]{2,1,0:T(8,128)(2,1)}) %all-gather.5.cloned.1.call-update) | async-done | bytes 7077904 | tf_op jit(solution)/shard_map/all_gather | solution.py:446
  104.4 5.4 multiply_reduce_fusion.entry
  109.8 30.7 %shard_map.280 = (f32[4,512,768]{2,1,0:T(8,128)}, f32[4,512,768]{2,1,0:T(8,128)}, bf16[4,512,1536]{2,1,0:T(8,128)(2,1)}, f32[4,8,512]{2,1,0:T(8,128)}) custom-call(bf16[4,512,768]{2,1,0:T(8,128)(2,1)} %get-tuple-element.74.xact, bf16[4,512,256]{2,1,0:T(8,128)(2,1)} %get-tuple-element.75.bcact, f32[4,512,128]{2,1,0:T(8,128)} %get-tuple-element.76.step_i, ...), custom_call_target="tpu_custom_call" | custom-call | flops 9663676416 | bytes 45307904 | tf_op jit(solution)/shard_map/pallas_call | solution.py:387
  140.6 34.1 %all-reduce.12.cloned.1.call-done.sums = f32[4,8,512]{2,1,0:T(8,128)} async-done(((f32[4,8,512]{2,1,0:T(8,128)}), f32[4,8,512]{2,1,0:T(8,128)}) %all-reduce.12.cloned.1.call-update) | async-done | bytes 65552 | tf_op jit(solution)/shard_map/psum | solution.py:468
  174.7 34.7 %shard_map.281 = (bf16[4,512,768]{2,1,0:T(8,128)(2,1)}, bf16[4,512,768]{2,1,0:T(8,128)(2,1)}, f32[4,512,768]{2,1,0:T(8,128)}, f32[4,512,128]{2,1,0:T(8,128)}, f3...) custom-call(bf16[4,512,768]{2,1,0:T(8,128)(2,1)} %get-tuple-element., ...), custom_call_target="tpu_custom_call" | custom-call | flops 3221225472 | bytes 51124224 | tf_op jit(solution)/shard_map/pallas_call | solution.py:387
  209.8 9.3 bitcast_convert_fusion
  219.1 35.7 %all-gather.7.cloned.1.call-done = bf16[32,128,768]{2,1,0:T(8,128)(2,1)} async-done(((bf16[4,128,768]{2,1,0:T(8,128)(2,1)}), bf16[32,128,768]{2,1,0:T(8,128)(2,1)}) %all-gather.7.cloned.1.call-update) | async-done | bytes 6291472 | tf_op jit(solution)/shard_map/all_gather | solution.py:478
  254.8 5.4 fusion.9.after
  260.2 33.3 %shard_map.282 = (bf16[4,512,768]{2,1,0:T(8,128)(2,1)}, bf16[4,16,768]{2,1,0:T(8,128)(2,1)}, bf16[4,512,256]{2,1,0:T(8,128)(2,1)}, bf16[4,16,256]{2,1,0:T(8,128)...) custom-call(bf16[4,512,768]{2,1,0:T(8,128)(2,1)} %get-tuple-element.74.xact, ...), custom_call_target="tpu_custom_call" | custom-call | flops 1610612736 | bytes 36938752 | tf_op jit(solution)/shard_map/pallas_call | solution.py:387
  295.3 9.3 bitcast_convert_fusion.2
  305.9 5.5 fusion.10
  313.1 9.2 bitcast_convert_fusion.1
  322.6 10.2 fusion.22
  332.7 6.6 fusion.18
  339.3 8.3 fusion.23
  347.6 15.8 %add_convert_fusion = bf16[2048,1536]{1,0:T(8,128)(2,1)} fusion(f32[2048,1536]{1,0:T(8,128)} %fusion.18, f32[2048,1536]{1,0:T(8,128)} %fusion.22, f32[2048,1536]{1,0:T(8,128)} %fusion.23, bf16[2048,256]{1,0:T(8,128)(2,1)S(1)} %bitcast.61, bf16[1536,256]{1,0:T(8,128)(2,1)S(1)} %copy-done.4), kind=kOutput, calls=%fused_computation.17 | convolution fusion | flops 1623195648 | bytes 45875200 | tf_op jit(solution)/shard_map/dot_general | solution.py:23
  370.3 42.0 %psum.114 = f32[5,256]{1,0:T(8,128)S(1)} all-reduce(f32[5,256]{1,0:T(8,128)S(1)} %bitcast.65), channel_id=1, replica_groups=mesh['seq'=8,'head'=4] {'seq','head'}, use_global_device_ids=true, to_apply=%region_16.17 | all-reduce | flops 1280 | bytes 10240 | tf_op jit(solution)/shard_map/psum | solution.py:527
  417.2 24.1 %psum.112 = bf16[1536,12]{0,1:T(8,128)(2,1)S(1)} all-reduce(bf16[1536,12]{0,1:T(8,128)(2,1)S(1)} %slice.139), channel_id=1, replica_groups=mesh['seq'=8,'head'=4] {'seq'}, use_global_device_ids=true, to_apply=%region_14.15 | all-reduce | flops 18432 | bytes 73728 | tf_op jit(solution)/shard_map/psum | solution.py:528
  445.9 114.5 %all-reduce.16.cloned.1.call-done = (bf16[1536,768]{1,0:T(8,128)(2,1)}, bf16[1536,768]{1,0:T(8,128)(2,1)}, bf16[768,1536]{1,0:T(8,128)(2,1)}) async-done(((bf16[1536,768]{1,0:T(8,128)(2,1)}, bf16[1536,768]{1,0:T(8,128)(2,1)}, bf16[768,1536]{1,0:T(8,128)(2,1)}), (bf16[1536,768]{1,0:T(8,128)(2,1)}, bf16[1536,768]{1,0:T(8,128)(2,1)}, bf16[768,1536]{1,0:T(8,128)(2,1)})) %all-reduce.16.cloned.1.call-update) | async-done | bytes 7077904 | tf_op jit(solution)/shard_map/psum | solution.py:528
  570.4 419.5 %all-reduce.18.cloned.1.call-done = (bf16[4,512,1536]{2,1,0:T(8,128)(2,1)}, bf16[4,512,1536]{2,1,0:T(8,128)(2,1)}) async-done(((bf16[4,512,1536]{2,1,0:T(8,128)(2,1)}, bf16[4,512,1536]{2,1,0:T(8,128)(2,1)}), (bf16[4,512,1536]{2,1,0:T(8,128)(2,1)}, bf16[4,512,1536]{2,1,0:T(8,128)(2,1)})) %all-reduce.18.cloned.1.call-update) | async-done | bytes 12582928 | tf_op jit(solution)/shard_map/psum | solution.py:467
  989.8 7.9 fusion.8
  997.7 25.0 %all-reduce.4 = (f32[1536]{0:T(1024)}, f32[5,768]{1,0:T(8,128)S(1)}, f32[12]{0:T(128)}, f32[12]{0:T(128)}, f32[12]{0:T(128)}, /*index=5*/f32[768]{0:T(1024)}) all-reduce(f32[1536]{0:T(1024)S(1)} %get-tuple-element.108, f32[5,768]{1,0:T(8,128)S(1)} %bitcast.64, ...), channel_id=1, replica_groups=mesh['seq'=8,'head'=4] {'seq'}, use_global_device_ids=true, to_apply=%region_10.11 | all-reduce | flops 6180 | bytes 49440 | tf_op jit(solution)/shard_map/psum | solution.py:523
  1024.0 15.8 %fusion.2 = (f32[4,512,1536]{2,1,0:T(8,128)}, bf16[4,512,1536]{2,1,0:T(8,128)(2,1)}) fusion(bf16[4,512,1536]{2,1,0:T(8,128)(2,1)} %get-tuple-element.120, bf16[4,512,1536]{2,1,0:T(8,128)(2,1)} %tok.1, bf16[4,512,1536]{2,1,0:T(8,128)(2,1)} %cot.1, f32[4,512]{1,0:T(4,128)S(1)} %broadcast_multiply_fusion, f32[4,512]{1,0:T(4,128)S(1)} %get-tuple-element.123, ...), kind=kLoop, calls=%fused_computation.8 | loop fusion | flops 40894464 | bytes 44079104 | tf_op jit(solution)/shard_map/sub | solution.py:516
  (98 shorter events, 47.4 us)
Async XLA Ops:
  7.2 95.8 %all-gather.5.cloned.1.call-start = ((), (), s32[]{:S(2)}) async-start(), calls=%async_computation.2 | async-start | bytes 7962624 | tf_op jit(solution)/shard_map/all_gather | solution.py:446
  8.2 10.1 collective-permute-start
  19.0 32.5 %copy-start.8 = (f32[768]{0:T(1024)S(1)}, f32[768]{0:T(1024)}, u32[]{:S(2)}) copy-start(f32[768]{0:T(1024)} %param.33) | copy-start | bytes 9220
  19.0 33.1 %copy-start.10 = (f32[12]{0:T(128)S(1)}, f32[12]{0:T(128)}, u32[]{:S(2)}) copy-start(f32[12]{0:T(128)} %param.32) | copy-start | bytes 148
  51.4 123.3 %all-reduce.12.cloned.1.call-start = ((), (), s32[]{:S(2)}) async-start(), calls=%async_computation | async-start | bytes 131072 | tf_op jit(solution)/shard_map/psum | solution.py:468
  140.5 114.3 %all-gather.7.cloned.1.call-start = ((), (), s32[]{:S(2)}) async-start(), calls=%async_computation.3 | async-start | bytes 7077888 | tf_op jit(solution)/shard_map/all_gather | solution.py:478
  209.4 234.1 %all-reduce.14.cloned.1.call-start = ((), (), s32[]{:S(2)}) async-start(), calls=%async_computation.1 | async-start | bytes 1572864 | tf_op jit(solution)/shard_map/psum | solution.py:530
  260.2 35.1 %copy-start.11 = (bf16[4,512,768]{2,1,0:T(8,128)(2,1)S(1)}, bf16[4,512,768]{2,1,0:T(8,128)(2,1)}, u32[]{:S(2)}) copy-start(bf16[4,512,768]{2,1,0:T(8,128)(2,1)} %get-tuple-element.86) | copy-start | bytes 9437188
  293.5 12.3 %collective-permute-start.2 = (bf16[4,16,256]{2,1,0:T(8,128)(2,1)}, bf16[4,16,256]{2,1,0:T(8,128)(2,1)S(1)}, u32[]{:S(2)}, u32[]{:S(2)}) collective-permute-start(bf16[4,16,256]{2,1,0:T(8,128)(2,1)} %get-tuple-element.99), channel_id=1, source_target_pairs={{4,0},{8,4},{12,8},{16,12},{20,16},{24,20},{28,24},{5,1},{9,5},{13... | collective-permute-start | bytes 98312 | tf_op jit(solution)/shard_map/ppermute | solution.py:491
  295.3 9.3 copy-start.14
  295.3 10.6 %copy-start.2 = (bf16[4,512,256]{2,1,0:T(8,128)(2,1)S(1)}, bf16[4,512,256]{2,1,0:T(8,128)(2,1)}, u32[]{:S(2)}) copy-start(bf16[4,512,256]{2,1,0:T(8,128)(2,1)} %get-tuple-element.98) | copy-start | bytes 3145732
  304.6 6.9 collective-permute-start.1
  311.5 249.0 %all-reduce.16.cloned.1.call-start = ((), (), s32[]{:S(2)}) async-start(), calls=%async_computation.4 | async-start | bytes 14155776 | tf_op jit(solution)/shard_map/psum | solution.py:528
  322.3 667.5 %all-reduce.18.cloned.1.call-start = ((), (), s32[]{:S(2)}) async-start(), calls=%async_computation.5 | async-start | bytes 25165824 | tf_op jit(solution)/shard_map/psum | solution.py:467
  322.6 10.2 copy-start.3
  332.7 6.6 copy-start.9
  332.7 6.6 copy-start.12
  339.3 8.3 copy-start.4
  363.5 6.7 copy-start.7
  363.5 79.1 %copy-start.15 = (f32[12]{0:T(128)S(1)}, f32[12]{0:T(128)}, u32[]{:S(2)}) copy-start(f32[12]{0:T(128)} %param.31) | copy-start | bytes 148
  560.4 4.4 copy-start.1
  560.4 6.9 copy-start
  564.8 425.0 %copy-start.5 = (f32[1536]{0:T(1024)S(1)}, f32[1536]{0:T(1024)}, u32[]{:S(2)}) copy-start(f32[1536]{0:T(1024)} %param.21) | copy-start | bytes 18436
  989.8 7.9 copy-start.6
  (1 other events, 0.7 us)
Sparse Core Ops, SparseCore 0:
  51.5 51.3 all-gather.4
  140.7 33.9 all-reduce.11
  209.5 45.2 all-gather.6
  311.6 131.9 all-reduce.13
  448.2 112.1 all-reduce.15
  562.9 426.9 all-reduce.17

commit v2 on v1

--- a/solution.py
+++ b/solution.py
@@ -8,7 +8,8 @@
 from jax.sharding import PartitionSpec as P
 
 EPS = 1e-05
-T = 128
+T = 256
+SUB = 128
 HALO = 16
 LANES = 128
 F32 = jnp.float32
@@ -59,13 +60,34 @@
 
 
 def softplus(v):
-    return jnp.maximum(v, 0.0) + jnp.log(1.0 + jnp.exp(-jnp.abs(v)))
+    return jnp.maximum(v, 0.0) + jnp.log1p(jnp.exp(-jnp.abs(v)))
 
 
 def lower():
-    row = lax.broadcasted_iota(jnp.int32, (T, T), 0)
-    col = lax.broadcasted_iota(jnp.int32, (T, T), 1)
+    row = lax.broadcasted_iota(jnp.int32, (SUB, SUB), 0)
+    col = lax.broadcasted_iota(jnp.int32, (SUB, SUB), 1)
     return row >= col
+
+
+def tile(i):
+    return slice(i * SUB, (i + 1) * SUB)
+
+
+def tiles():
+    return [(i, j) for i in range(T // SUB) for j in range(i + 1)]
+
+
+def cross_tiles(cm, bm):
+    found = {}
+    for i, j in tiles():
+        value = mm_t(cm[tile(i)], bm[tile(j)])
+        found[i, j] = jnp.where(lower(), value, 0.0) if i == j else value
+    return found
+
+
+def decay_tile(cum, cum_t, h, i, j):
+    gap = cum[tile(i), h : h + 1] - cum_t[h : h + 1, tile(j)]
+    return jnp.exp(jnp.minimum(gap, 0.0) if i == j else gap)
 
 
 def half_mask(rows):
@@ -82,9 +104,121 @@
     return pl.ds(pl.multiple_of(b * T, T), T)
 
 
+MESH = pl.DeviceIdType.MESH
+
+
+class Exchange:
+    def __init__(self, rounds, backward, total, before, logs, out, back, send, recv):
+        self.rounds, self.backward = rounds, backward
+        self.total, self.before, self.logs = total, before, logs
+        self.out, self.back, self.send, self.recv = out, back, send, recv
+        self.me = lax.axis_index("seq")
+
+    def partner(self, r):
+        bit = 1 << r
+        return self.me + bit - 2 * bit * (lax.div(self.me, bit) % 2)
+
+    def greet(self):
+        barrier = pltpu.get_barrier_semaphore()
+        for r in range(self.rounds):
+            pl.semaphore_signal(barrier, inc=1, device_id={"seq": self.partner(r)}, device_id_type=MESH)
+        pl.semaphore_wait(barrier, self.rounds)
+
+    def copy(self, r, s):
+        return pltpu.make_async_remote_copy(
+            src_ref=self.out.at[r, s], dst_ref=self.back.at[r, s],
+            send_sem=self.send.at[r, s], recv_sem=self.recv.at[r, s],
+            device_id={"seq": self.partner(r)}, device_id_type=MESH,
+        )
+
+    def begin(self, s, state, log):
+        self.total[s] = state
+        self.before[s] = jnp.zeros_like(state)
+        self.logs[s] = jnp.zeros(self.logs.shape[1:], F32)
+        self.logs[s, 0:1] = log
+
+    def push(self, r, s):
+        n = self.total.shape[1]
+        self.out[r, s, 0:n] = self.total[s].astype(BF16)
+        hi, mid, lo = [v.astype(F32) for v in split(self.logs[s, 0:1], 3)]
+        at = lax.broadcasted_iota(jnp.int32, (HALO, hi.shape[1]), 0)
+        tail = jnp.where(at == 0, hi, jnp.where(at == 1, mid, jnp.where(at == 2, lo, 0.0)))
+        self.out[r, s, n : n + HALO] = tail.astype(BF16)
+        self.copy(r, s).start()
+
+    def take(self, r, s):
+        n = self.total.shape[1]
+        copy = self.copy(r, s)
+        copy.wait_recv()
+        copy.wait_send()
+        state = self.back[r, s, 0:n].astype(F32)
+        tail = self.back[r, s, n : n + HALO].astype(F32)
+        log = tail[0:1] + tail[1:2] + tail[2:3]
+        upper = lax.div(self.me, 1 << r) % 2 == 1
+        near = jnp.logical_not(upper) if self.backward else upper
+        mine, theirs = self.logs[s, 0:1], self.logs[s, 1:2]
+        self.before[s] = self.before[s] + jnp.where(near, jnp.exp(theirs), 0.0) * state
+        self.logs[s, 1:2] = theirs + jnp.where(near, log, 0.0)
+        own = jnp.where(near, 1.0, jnp.exp(log))
+        other = jnp.where(near, jnp.exp(mine), 1.0)
+        self.total[s] = own * self.total[s] + other * state
+        self.logs[s, 0:1] = mine + log
+
+    def advance(self, i, seqs):
+        @pl.when(i < seqs)
+        def _():
+            self.push(0, i)
+
+        for r in range(self.rounds):
+            s = i - 1 - r
+
+            @pl.when((s >= 0) & (s < seqs))
+            def _():
+                self.take(r, s)
+                if r + 1 < self.rounds:
+                    self.push(r + 1, s)
+
+    @staticmethod
+    def scratch(rounds, seqs, n, inner):
+        return [
+            pltpu.VMEM((seqs, n, inner), F32), pltpu.VMEM((seqs, n, inner), F32), pltpu.VMEM((seqs, 8, inner), F32),
+            pltpu.VMEM((rounds, seqs, n + HALO, inner), BF16), pltpu.VMEM((rounds, seqs, n + HALO, inner), BF16),
+            pltpu.SemaphoreType.DMA((rounds, seqs)), pltpu.SemaphoreType.DMA((rounds, seqs)),
+        ]
+
+
 def front(
     tok, halo, ngain, gate_w, value_w, state_w, step_w, vk, vo, sk, so, sbias, rate, wide, tri,
-    normed_o, gate_o, xext_o, bcext_o, sraw_o, xact_o, bcact_o, step_o, cum_o, lstart_o, lstate_o, pre_o,
+    normed_o, gate_o, xext_o, bcext_o, sraw_o, xact_o, bcact_o, step_o, cum_o, lstart_o, pre_o, entry_o,
+    nx, xe, be, st, run, total, before, logs, out, back, send, recv,
+    *, seqs, rounds,
+):
+    i = pl.program_id(0)
+    scan = Exchange(rounds, False, total, before, logs, out, back, send, recv)
+
+    @pl.when(i == 0)
+    def _():
+        scan.greet()
+
+    @pl.when(i < seqs)
+    def _():
+        front_rows(
+            tok, halo, ngain, gate_w, value_w, state_w, step_w, vk, vo, sk, so, sbias, rate, wide, tri,
+            normed_o, gate_o, xext_o, bcext_o, sraw_o, xact_o, bcact_o, step_o, cum_o, lstart_o, pre_o,
+            nx, xe, be, st, run,
+        )
+        scan.begin(i, st[...], expand_row(run[0:1], wide[...]))
+
+    scan.advance(i, seqs)
+
+    @pl.when(i == seqs + rounds - 1)
+    def _():
+        entry_o[...] = before[...]
+
+
+def front_rows(
+    tok, halo, ngain, gate_w, value_w, state_w, step_w, vk, vo, sk, so, sbias, rate, wide, tri,
+    normed_o, gate_o, xext_o, bcext_o, sraw_o, xact_o, bcact_o, step_o, cum_o, lstart_o, pre_o,
     nx, xe, be, st, run,
 ):
     length = tok.shape[1]
@@ -139,16 +273,10 @@
         weight = jnp.exp(last - cum) * step
         weighted = (xa.astype(F32) * expand(weight, wide[...])).astype(BF16)
         contrib = t_mm(bca[:, :n], weighted)
-        lstart_o[0, b] = st[...].astype(BF16)
+        lstart_o[0, b] = st[...]
         st[...] = expand_row(jnp.exp(last), wide[...]) * st[...] + contrib
         run[0:1] = run[0:1] + last
         pre_o[0, b + 1 : b + 2] = run[0:1]
-    lstate_o[0, 0:n] = st[...].astype(BF16)
-    hi, mid, lo = split(expand_row(run[0:1], wide[...]), 3)
-    at = lax.broadcasted_iota(jnp.int32, (HALO, hi.shape[1]), 0)
-    hi, mid, lo = [jnp.broadcast_to(v.astype(F32), at.shape) for v in (hi, mid, lo)]
-    tail = jnp.where(at == 0, hi, jnp.where(at == 1, mid, jnp.where(at == 2, lo, 0.0)))
-    lstate_o[0, n : n + HALO] = tail.astype(BF16)
 
 
 def scan_out(
@@ -169,18 +297,25 @@
         bm, cm = bca[:, :n], bca[:, n:]
         cum = cum_i[0, r, :]
         cum_t = cum.T
-        cross = jnp.where(lower(), mm_t(cm, bm), 0.0)
-        start = expand_row(jnp.exp(pre[0, pl.ds(b, 1), :]), wide[...]) * entry[0] + lstart[0, b].astype(F32)
-        across = expand(jnp.exp(cum), wide[...]) * mm(cm, start.astype(BF16))
+        cross = cross_tiles(cm, bm)
+        start = expand_row(jnp.exp(pre[0, pl.ds(b, 1), :]), wide[...]) * entry[0] + lstart[0, b]
+        start = start.astype(BF16)
+        grown = jnp.exp(cum)
+        cm = cm.astype(F32)
         xs = (xa.astype(F32) * expand(step_i[0, r, :], wide[...])).astype(BF16)
         for p in range(inner // LANES):
-            mix = []
-            for h in (2 * p, 2 * p + 1):
-                decay = jnp.exp(jnp.minimum(cum[:, h : h + 1] - cum_t[h : h + 1, :], 0.0))
-                mix.append((cross * decay).astype(BF16))
             lanes = slice(p * LANES, (p + 1) * LANES)
-            within = mm(jnp.concatenate(mix, axis=1), pair_rows(xs[:, lanes]))
-            ssd_o[0, r, lanes] = within + across[:, lanes]
+            two = (2 * p, 2 * p + 1)
+            start_two = pair_rows(start[:, lanes])
+            xs_two = [pair_rows(xs[tile(j), lanes]) for j in range(T // SUB)]
+            for i in range(T // SUB):
+                left = [(cm[tile(i)] * grown[tile(i), h : h + 1]).astype(BF16) for h in two]
+                right = [start_two]
+                for j in range(i + 1):
+                    left += [(cross[i, j] * decay_tile(cum, cum_t, h, i, j)).astype(BF16) for h in two]
+                    right.append(xs_two[j])
+                rows = pl.ds(pl.multiple_of(b * T + i * SUB, SUB), SUB)
+                ssd_o[0, rows, lanes] = mm(jnp.concatenate(left, axis=1), jnp.concatenate(right, axis=0))
         mixed = ssd_o[0, r, :] + skip[...] * xa.astype(F32)
         g = gate[0, r, :]
         gated = mixed * (g * sigmoid(g))
@@ -199,80 +334,127 @@
 
 def back_one(
     xact, bcact, step_i, cum_i, gate, ssd, gn, sums, lstart, entry, pre, mgain, skip, wide,
-    gnormed_o, gate_grad_o, xg_o, cumg_o, stepg_o, bcg_o, lend_o, lgrad_o, mgg_o, skg_o,
-    z, acc,
-    *, inner_all,
+    gnormed_o, gate_grad_o, xg_o, cumg_o, stepg_o, bcg_o, lend_o, rms_o, mgg_o, skg_o, after_o,
+    z, acc, dys, use, total, before, logs, out, back, send, recv,
+    *, inner_all, seqs, rounds,
+):
+    i = pl.program_id(0)
+    scan = Exchange(rounds, True, total, before, logs, out, back, send, recv)
+
+    @pl.when(i == 0)
+    def _():
+        scan.greet()
+        mgg_o[...] = jnp.zeros_like(mgg_o)
+        skg_o[...] = jnp.zeros_like(skg_o)
+
+    @pl.when(i < seqs)
+    def _():
+        back_one_rows(
+            xact, bcact, step_i, cum_i, gate, ssd, gn, sums, lstart, entry, pre, mgain, skip, wide,
+            gnormed_o, gate_grad_o, xg_o, cumg_o, stepg_o, bcg_o, lend_o, rms_o, mgg_o, skg_o,
+            z, acc, dys, use, inner_all,
+        )
+        blocks = xact.shape[1] // T
+        scan.begin(i, acc[...], expand_row(pre[0, blocks : blocks + 1], wide[...]))
+
+    scan.advance(i, seqs)
+
+    @pl.when(i == seqs + rounds - 1)
+    def _():
+        after_o[...] = before[...]
+
+
+def back_one_rows(
+    xact, bcact, step_i, cum_i, gate, ssd, gn, sums, lstart, entry, pre, mgain, skip, wide,
+    gnormed_o, gate_grad_o, xg_o, cumg_o, stepg_o, bcg_o, lend_o, rms_o, mgg_o, skg_o,
+    z, acc, dys, use, inner_all,
 ):
     length = xact.shape[1]
     blocks = length // T
     n = bcact.shape[2] // 2
     inner = xact.shape[2]
-
-    @pl.when(pl.program_id(0) == 0)
-    def _():
-        mgg_o[...] = jnp.zeros_like(mgg_o)
-        skg_o[...] = jnp.zeros_like(skg_o)
-
     acc[...] = jnp.zeros_like(acc)
 
     def block(i, _):
         b = blocks - 1 - i
         r = rows_of(b)
-        low_x = xact[0, r, :]
-        xa = low_x.astype(F32)
+        sums_b = sums[0, :, r]
+        columns = jnp.concatenate([sums_b, jnp.zeros((LANES - 8, T), F32)], axis=0).T
+        for i in range(T // SUB):
+            ri = pl.ds(pl.multiple_of(b * T + i * SUB, SUB), SUB)
+            xa = xact[0, ri, :].astype(F32)
+            rms = lax.rsqrt(columns[tile(i), 0:1] / inner_all + EPS)
+            rms_o[0, ri, :] = jnp.broadcast_to(rms, (SUB, LANES))
+            coef = rms * rms * rms * (columns[tile(i), 1:2] / inner_all)
+            mixed = ssd[0, ri, :] + skip[...] * xa
+            g = gate[0, ri, :]
+            sg = sigmoid(g)
+            gated = mixed * (g * sg)
+            grad_norm = gn[0, ri, :]
+            normalised = gated * rms
+            gnormed_o[0, ri, :] = (normalised * mgain[...]).astype(BF16)
+            mgg_o[0:1] += jnp.sum(grad_norm * normalised, axis=0, keepdims=True)
+            grad_gated = rms * (grad_norm * mgain[...]) - gated * coef
+            gate_grad_o[0, ri, :] = (grad_gated * mixed * (sg * (1.0 + g * (1.0 - sg)))).astype(BF16)
+            grad_mixed = grad_gated * (g * sg)
+            skg_o[0:1] += jnp.sum(grad_mixed * xa, axis=0, keepdims=True)
+            xg_o[0, ri, :] = skip[...] * grad_mixed
+            dys[tile(i)] = grad_mixed.astype(BF16)
+        dy = dys[...]
+        xa = xact[0, r, :].astype(F32)
         bca = bcact[0, r, :]
         bm, cm = bca[:, :n], bca[:, n:]
+        cm32 = cm.astype(F32)
         cum = cum_i[0, r, :]
         cum_t = cum.T
-        sums_b = sums[0, :, r]
-        columns = jnp.concatenate([sums_b, jnp.zeros((LANES - 8, T), F32)], axis=0).T
-        rms = lax.rsqrt(columns[:, 0:1] / inner_all + EPS)
-        coef = rms * rms * rms * (columns[:, 1:2] / inner_all)
-        ssd_b = ssd[0, r, :]
-        mixed = ssd_b + skip[...] * xa
-        g = gate[0, r, :]
-        sg = sigmoid(g)
-        gated = mixed * (g * sg)
-        grad_norm = gn[0, r, :]
-        normalised = gated * rms
-        gnormed_o[0, r, :] = (normalised * mgain[...]).astype(BF16)
-        mgg_o[0:1] += jnp.sum(grad_norm * normalised, axis=0, keepdims=True)
-        grad_gated = rms * (grad_norm * mgain[...]) - gated * coef
-        gate_grad_o[0, r, :] = (grad_gated * mixed * (sg * (1.0 + g * (1.0 - sg)))).astype(BF16)
-        grad_mixed = grad_gated * (g * sg)
-        skg_o[0:1] += jnp.sum(grad_mixed * xa, axis=0, keepdims=True)
-        dy = grad_mixed.astype(BF16)
-        start = expand_row(jnp.exp(pre[0, pl.ds(b, 1), :]), wide[...]) * entry[0] + lstart[0, b].astype(F32)
-        gdy = (expand(jnp.exp(cum), wide[...]) * dy.astype(F32)).astype(BF16)
-        c_grad = mm_t(gdy, start.astype(BF16))
-        lend_o[0, b] = acc[...].astype(BF16)
-        acc[...] = expand_row(jnp.exp(cum[T - 1 : T]), wide[...]) * acc[...] + t_mm(cm, gdy)
+        grown = jnp.exp(cum)
+        start = expand_row(jnp.exp(pre[0, pl.ds(b, 1), :]), wide[...]) * entry[0] + lstart[0, b]
+        start = start.astype(BF16)
+        gdy_hi, gdy_lo = split(expand(grown, wide[...]) * dy.astype(F32), 2)
+        c_grad = mm_t(gdy_hi, start) + mm_t(gdy_lo, start)
         step_wide = expand(step_i[0, r, :], wide[...])
         xs = (xa * step_wide).astype(BF16)
-        cross = jnp.where(lower(), mm_t(cm, bm), 0.0)
-        cross_part = jnp.zeros((T, T), F32)
+        cross = cross_tiles(cm, bm)
+        cross_part = {ij: jnp.zeros((SUB, SUB), F32) for ij in tiles()}
         for p in range(inner // LANES):
             lanes = slice(p * LANES, (p + 1) * LANES)
-            dy_two = pair_rows(dy[:, lanes])
-            mix_grad = mm_t(dy_two, xs[:, lanes])
-            mix = []
-            for j in (0, 1):
-                h = 2 * p + j
-                decay = jnp.exp(jnp.minimum(cum[:, h : h + 1] - cum_t[h : h + 1, :], 0.0))
-                mix.append((cross * decay).astype(BF16))
-                cross_part = cross_part + mix_grad[j * T : (j + 1) * T] * decay
-            z[:, lanes] = t_mm(jnp.concatenate(mix, axis=0), dy_two)
-        cross_low = jnp.where(lower(), cross_part, 0.0).astype(BF16)
+            two = (2 * p, 2 * p + 1)
+            scaled = [(cm32 * grown[:, h : h + 1]).astype(BF16) for h in two]
+            used = None
+            zs = [None] * (T // SUB)
+            for i in range(T // SUB):
+                dy_two = pair_rows(dy[tile(i), lanes])
+                term = t_mm(jnp.concatenate([v[tile(i)] for v in scaled], axis=0), dy_two)
+                used = term if used is None else used + term
+                for j in range(i + 1):
+                    mix_grad = mm_t(dy_two, xs[tile(j), lanes])
+                    mix = []
+                    for k, h in enumerate(two):
+                        decay = decay_tile(cum, cum_t, h, i, j)
+                        mix.append((cross[i, j] * decay).astype(BF16))
+                        cross_part[i, j] = cross_part[i, j] + mix_grad[tile(k)] * decay
+                    term = t_mm(jnp.concatenate(mix, axis=0), dy_two)
+                    zs[j] = term if zs[j] is None else zs[j] + term
+            use[:, lanes] = used
+            for j in range(T // SUB):
+                z[tile(j), lanes] = zs[j]
+        lend_o[0, b] = acc[...]
+        acc[...] = expand_row(grown[T - 1 : T], wide[...]) * acc[...] + use[...]
+        rows = []
+        for i in range(T // SUB):
+            row = [jnp.where(lower(), cross_part[i, j], 0.0) if i == j else cross_part[i, j] for j in range(i + 1)]
+            row += [jnp.zeros((SUB, SUB), F32)] * (T // SUB - 1 - i)
+            rows.append(jnp.concatenate(row, axis=1))
+        cross_low = jnp.concatenate(rows, axis=0).astype(BF16)
         bcg_o[0, r, 0:n] = t_mm(cross_low, cm)
         bcg_o[0, r, n : 2 * n] = c_grad + mm(cross_low, bm)
         zz = z[...]
-        xg_o[0, r, :] = step_wide * zz + skip[...] * grad_mixed
-        cumg_o[0, r, :] = head_sum(dy.astype(F32) * ssd_b - xs.astype(F32) * zz, wide[...])
+        xg_o[0, r, :] = xg_o[0, r, :] + step_wide * zz
+        cumg_o[0, r, :] = head_sum(dy.astype(F32) * ssd[0, r, :] - xs.astype(F32) * zz, wide[...])
         stepg_o[0, r, :] = head_sum(xa * zz, wide[...])
         return 0
 
     lax.fori_loop(0, blocks, block, 0)
-    lgrad_o[0] = acc[...].astype(BF16)
 
 
 def back_two(
@@ -319,9 +501,9 @@
         cum = cum_i[0, r, :]
         step = step_i[0, r, :]
         last = cum[T - 1 : T]
-        start = expand_row(jnp.exp(pre[0, b : b + 1]), wide[...]) * entry[0] + lstart[0, b].astype(F32)
+        start = expand_row(jnp.exp(pre[0, b : b + 1]), wide[...]) * entry[0] + lstart[0, b]
         suffix = jnp.exp(pre[0, blocks : blocks + 1] - pre[0, b + 1 : b + 2])
-        end = expand_row(suffix, wide[...]) * after[0] + lend[0, b].astype(F32)
+        end = expand_row(suffix, wide[...]) * after[0] + lend[0, b]
         end_low = end.astype(BF16)
         weighted_grad = mm(bm, end_low)
         reach = jnp.exp(last - cum)
@@ -366,18 +548,312 @@
         bpg_o[0, r0 : r0 + T] = conv_back(bcg_s, sk, HALO + r0, T)
 
 
-def per_seq(shape):
-    rest = shape[1:]
-    return pl.BlockSpec((1,) + tuple(rest), lambda s: (s,) + (0,) * len(rest))
-
-
-def whole(shape):
-    return pl.BlockSpec(tuple(shape), lambda s: (0,) * len(shape))
-
-
-def call(body, seqs, ins, outs, scratch, flops):
-    in_specs = [per_seq(a.shape) if a.ndim >= 3 else whole(a.shape) for a in ins]
-    out_specs = [per_seq(s) if cut else whole(s) for s, _, cut in outs]
+def head_sums(mine, out, slots, send, recv):
+    z = lax.axis_index("head")
+    count = slots.shape[0]
+    barrier = pltpu.get_barrier_semaphore()
+    for d in range(1, count):
+        pl.semaphore_signal(barrier, inc=1, device_id={"head": lax.rem(z + d, count)}, device_id_type=MESH)
+    pl.semaphore_wait(barrier, count - 1)
+    copies = []
+    for d in range(1, count):
+        copies.append(pltpu.make_async_remote_copy(
+            src_ref=mine, dst_ref=slots.at[z], send_sem=send.at[d], recv_sem=recv.at[d],
+            device_id={"head": lax.rem(z + d, count)}, device_id_type=MESH,
+        ))
+        copies[-1].start()
+    slots[z] = mine[...]
+    for copy in copies:
+        copy.wait_recv()
+    total = slots[0]
+    for d in range(1, count):
+        total = total + slots[d]
+    out[...] = total
+    for copy in copies:
+        copy.wait_send()
+
+
+class Chain:
+    def __init__(self, own, got, far, sems):
+        z = lax.axis_index("head")
+        self.end = (z == 0) | (z == 3)
+        self.side = z + 1 - 2 * (z % 2)
+        self.other = 3 - z
+        self.own, self.got, self.far = own, got, far
+        self.sems = sems
+
+    @staticmethod
+    def scratch(n, chunk, width):
+        buffer = pltpu.VMEM((n, chunk, width), BF16)
+        return [buffer, buffer, buffer] + [pltpu.SemaphoreType.DMA((n,))] * 6
+
+    def copy(self, kind, k, source=None):
+        src, dst, to = [(self.own, self.got, self.side), (self.own, self.far, self.other), (self.got, self.got, self.side)][kind]
+        return pltpu.make_async_remote_copy(
+            src_ref=src.at[k] if source is None else source, dst_ref=dst.at[k],
+            send_sem=self.sems[2 * kind].at[k], recv_sem=self.sems[2 * kind + 1].at[k],
+            device_id={"head": to}, device_id_type=MESH,
+        )
+
+    def inward(self, k, source=None):
+        @pl.when(self.end)
+        def _():
+            self.copy(0, k, source).start()
+
+    def across(self, k, mine=None):
+        @pl.when(jnp.logical_not(self.end))
+        def _():
+            self.copy(0, k).wait_recv()
+            value = (self.own[k] if mine is None else mine[...]).astype(F32)
+            self.own[k] = (value + self.got[k].astype(F32)).astype(BF16)
+            self.copy(1, k).start()
+
+    def outward(self, k):
+        @pl.when(jnp.logical_not(self.end))
+        def _():
+            self.copy(1, k).wait_recv()
+            self.got[k] = (self.own[k].astype(F32) + self.far[k].astype(F32)).astype(BF16)
+            self.copy(2, k).start()
+
+    def total(self, k):
+        @pl.when(self.end)
+        def _():
+            self.copy(2, k).wait_recv()
+
+        return self.got[k].astype(F32)
+
+    def drain(self, n):
+        def one(k, _):
+            @pl.when(self.end)
+            def _():
+                self.copy(0, k).wait_send()
+
+            @pl.when(jnp.logical_not(self.end))
+            def _():
+                self.copy(1, k).wait_send()
+                self.copy(2, k).wait_send()
+
+            return 0
+
+        lax.fori_loop(0, n, one, 0)
+
+
+class SmallSums:
+    def __init__(self, rounds, acc, out, back, zback, done, sems, vec, vback, vsems):
+        self.rounds = rounds
+        self.acc, self.out, self.back, self.zback, self.done, self.sems = acc, out, back, zback, done, sems
+        self.vec, self.vback, self.vsems = vec, vback, vsems
+        self.me, self.z = lax.axis_index("seq"), lax.axis_index("head")
+        self.stages = 2 * rounds + 2
+
+    @staticmethod
+    def scratch(rounds, rows, cols, vec_shape):
+        half = pltpu.VMEM((rounds, rows // 2, cols), BF16)
+        return [
+            pltpu.VMEM((rows, cols), F32), half, half, pltpu.VMEM((4, rows >> rounds, cols), BF16), pltpu.VMEM((rows, cols), BF16),
+            pltpu.SemaphoreType.DMA((4 * rounds + 8,)), pltpu.VMEM(vec_shape, F32), pltpu.VMEM((4,) + vec_shape, F32), pltpu.SemaphoreType.DMA((8,)),
+        ]
+
+    def partner(self, r):
+        bit = 1 << r
+        return self.me + bit - 2 * bit * (lax.div(self.me, bit) % 2)
+
+    def start_of(self, r):
+        rows = self.acc.shape[0]
+        first = 0
+        for k in range(r):
+            first = first + (lax.div(self.me, 1 << k) % 2) * (rows >> (k + 1))
+        return first, rows >> r
+
+    def halving(self, r):
+        size = self.acc.shape[0] >> (r + 1)
+        return pltpu.make_async_remote_copy(
+            src_ref=self.out.at[r, pl.ds(0, size)], dst_ref=self.back.at[r, pl.ds(0, size)],
+            send_sem=self.sems.at[r], recv_sem=self.sems.at[self.rounds + r],
+            device_id={"seq": self.partner(r)}, device_id_type=MESH,
+        )
+
+    def gathering(self, r, mine):
+        first, size = self.start_of(r + 1)
+        if not mine:
+            first = first + size - 2 * size * (lax.div(self.me, 1 << r) % 2)
+        at = pl.ds(pl.multiple_of(first, 16), size)
+        return pltpu.make_async_remote_copy(
+            src_ref=self.done.at[at], dst_ref=self.done.at[at],
+            send_sem=self.sems.at[2 * self.rounds + r], recv_sem=self.sems.at[3 * self.rounds + r],
+            device_id={"seq": self.partner(r)}, device_id_type=MESH,
+        )
+
+    def to_head(self, d, vec):
+        src, dst, sems, base = (self.vec, self.vback, self.vsems, 0) if vec else (self.share(), self.zback, self.sems, 4 * self.rounds)
+        return pltpu.make_async_remote_copy(
+            src_ref=src, dst_ref=dst.at[self.z], send_sem=sems.at[base + d], recv_sem=sems.at[base + 4 + d],
+            device_id={"head": lax.rem(self.z + d, 4)}, device_id_type=MESH,
+        )
+
+    def share(self):
+        first, size = self.start_of(self.rounds)
+        return self.done.at[pl.ds(pl.multiple_of(first, 16), size)]
+
+    def push_half(self, r):
+        first, size = self.start_of(r)
+        half = size // 2
+        theirs = first + half - half * (lax.div(self.me, 1 << r) % 2)
+        self.out[r, pl.ds(0, half), :] = self.acc[pl.ds(pl.multiple_of(theirs, 16), half), :].astype(BF16)
+        self.halving(r).start()
+
+    def stage(self, k):
+        rounds = self.rounds
+        if k == 0:
+            for d in range(1, 4):
+                self.to_head(d, True).start()
+            self.vback[self.z] = self.vec[...]
+        if 0 < k <= rounds:
+            r = k - 1
+            copy = self.halving(r)
+            copy.wait()
+            first, size = self.start_of(r + 1)
+            at = pl.ds(pl.multiple_of(first, 16), size)
+            self.acc[at, :] = self.acc[at, :] + self.back[r, pl.ds(0, size), :].astype(F32)
+        if k < rounds:
+            self.push_half(k)
+        if k == rounds:
+            first, size = self.start_of(rounds)
+            at = pl.ds(pl.multiple_of(first, 16), size)
+            self.done[at, :] = self.acc[at, :].astype(BF16)
+            for d in range(1, 4):
+                self.to_head(d, False).start()
+            self.zback[self.z] = self.done[at, :]
+        if k == rounds + 1:
+            for d in range(1, 4):
+                self.to_head(d, False).wait()
+                self.to_head(d, True).wait()
+            first, size = self.start_of(rounds)
+            at = pl.ds(pl.multiple_of(first, 16), size)
+            total = self.zback[0].astype(F32)
+            vec = self.vback[0]
+            for d in range(1, 4):
+                total = total + self.zback[d].astype(F32)
+                vec = vec + self.vback[d]
+            self.done[at, :] = total.astype(BF16)
+            self.vec[...] = vec
+            self.gathering(rounds - 1, True).start()
+        if k > rounds + 1:
+            r = rounds - 1 - (k - rounds - 2)
+            self.gathering(r, True).wait_send()
+            self.gathering(r, False).wait_recv()
+            if r > 0:
+                self.gathering(r - 1, True).start()
+
+
+CHUNK = 64
+LAG = 2
+
+
+def finish(
+    y_all, y, gate_grad, xpg, bpg, raw, tok, cot, rms, gate_w, value_w, state_w, step_w, ngain, small, state_grad, state_rows,
+    result_o, tokens_grad_o, small_o, state_o,
+    own, got, far, sa, sb, sc, sd, se, sf, yown, ygot, yfar, ta, tb, tc, td, te, tf, rows, out, back, send, recv,
+    s_acc, s_out, s_back, s_zback, s_done, s_sems, s_vec, s_vback, s_vsems,
+    *, n, rounds,
+):
+    i = pl.program_id(0)
+    sums = SmallSums(rounds, s_acc, s_out, s_back, s_zback, s_done, s_sems, s_vec, s_vback, s_vsems)
+    chain = Chain(own, got, far, (sa, sb, sc, sd, se, sf))
+    ychain = Chain(yown, ygot, yfar, (ta, tb, tc, td, te, tf))
+    me = lax.axis_index("seq")
+
+    def partner(r):
+        bit = 1 << r
+        return me + bit - 2 * bit * (lax.div(me, bit) % 2)
+
+    @pl.when(i == 0)
+    def _():
+        barrier = pltpu.get_barrier_semaphore()
+        for r in range(rounds):
+            pl.semaphore_signal(barrier, inc=1, device_id={"seq": partner(r)}, device_id_type=MESH)
+        z = lax.axis_index("head")
+        for d in range(1, 4):
+            pl.semaphore_signal(barrier, inc=1, device_id={"head": lax.rem(z + d, 4)}, device_id_type=MESH)
+        pl.semaphore_wait(barrier, rounds + 3)
+        s_acc[...] = state_grad[...].astype(F32)
+        s_vec[...] = state_rows[...]
+        rows[0:8] = small[...]
+        rows[8:] = jnp.zeros_like(rows[8:])
+
+    k = i - 2 * LAG
+
+    @pl.when((k >= 0) & (k < n))
+    def _():
+        chain.outward(k)
+        ychain.outward(k)
+
+    k = i - LAG
+
+    @pl.when((k >= 0) & (k < n))
+    def _():
+        chain.across(k)
+        ychain.across(k, y)
+
+    @pl.when(i < n)
+    def _():
+        ychain.inward(i, y_all.at[pl.ds(pl.multiple_of(i * CHUNK, CHUNK), CHUNK)])
+        value = mm_t(gate_grad[...], gate_w[...]) + mm_t(xpg[...], value_w[...])
+        own[i] = (value + (mm_t(bpg[...], state_w[...]) + mm_t(raw[...], step_w[...]))).astype(BF16)
+        chain.inward(i)
+
+    for stage in range(sums.stages):
+
+        @pl.when(i == 1 + 2 * stage)
+        def _():
+            sums.stage(stage)
+
+    k = i - 3 * LAG
+
+    @pl.when(k >= 0)
+    def _():
+        grad = chain.total(k)
+        branch = ychain.total(k)
+        t = tok[...].astype(F32)
+        width = t.shape[1]
+        inv = lax.rsqrt(jnp.mean(t * t, axis=1, keepdims=True) + EPS)
+        result_o[...] = (t + branch * rms[:, 0:1]).astype(BF16)
+        scaled = grad * ngain[...]
+        dot = jnp.sum(scaled * t, axis=1, keepdims=True) / width
+        tokens_grad_o[...] = cot[...].astype(F32) + inv * scaled - t * (inv * inv * inv * dot)
+        gain = jnp.sum(grad * t * inv, axis=0, keepdims=True)
+        half = width // 2
+        rows[8:9] += gain[:, :half]
+        rows[9:10] += gain[:, half:]
+
+    @pl.when(i == n + 3 * LAG - 1)
+    def _():
+        chain.drain(n)
+        ychain.drain(n)
+        rows[16:24, 0 : s_vec.shape[1]] = s_vec[...]
+        for r in range(rounds):
+            copy = pltpu.make_async_remote_copy(
+                src_ref=out.at[r], dst_ref=back.at[r], send_sem=send.at[r], recv_sem=recv.at[r],
+                device_id={"seq": partner(r)}, device_id_type=MESH,
+            )
+            out[r] = rows[...]
+            copy.start()
+            copy.wait()
+            rows[...] = rows[...] + back[r]
+        state_o[...] = s_done[...]
+        small_o[...] = rows[...]
+
+
+def call(body, steps, seqs, ins, outs, scratch, flops, collective_id=None):
+    def cut(shape):
+        rest = tuple(shape[1:])
+        return pl.BlockSpec((1,) + rest, lambda s: (jnp.minimum(s, seqs - 1),) + (0,) * len(rest))
+
+    def whole(shape):
+        return pl.BlockSpec(tuple(shape), lambda s: (0,) * len(shape))
+
+    in_specs = [cut(a.shape) if a.ndim >= 3 else whole(a.shape) for a in ins]
+    out_specs = [cut(s) if c else whole(s) for s, _, c in outs]
     moved = sum(a.size * a.dtype.itemsize for a in ins)
     for s, d, _ in outs:
         size = jnp.dtype(d).itemsize
@@ -386,13 +862,14 @@
         moved += size
     return pl.pallas_call(
         body,
-        grid=(seqs,),
+        grid=(steps,),
         in_specs=in_specs,
         out_specs=out_specs,
         out_shape=[jax.ShapeDtypeStruct(s, d) for s, d, _ in outs],
         scratch_shapes=scratch,
         compiler_params=pltpu.CompilerParams(
-            dimension_semantics=("arbitrary",), vmem_limit_bytes=56 * 1024 * 1024
+            dimension_semantics=("arbitrary",), vmem_limit_bytes=60 * 1024 * 1024,
+            collective_id=collective_id, has_side_effects=collective_id is not None,
         ),
         cost_estimate=pl.CostEstimate(flops=flops, bytes_accessed=moved, transcendentals=0),
     )(*ins)
@@ -411,7 +888,9 @@
     n = n2 // 2
     taps = value_kernel.shape[0]
     blocks = length // T
-    devices, me = lax.axis_size("seq"), lax.axis_index("seq")
+    devices = lax.axis_size("seq")
+    rounds = devices.bit_length() - 1
+    assert devices == 1 << rounds
     inner_all = inner * lax.axis_size("head")
 
     halo = lax.ppermute(tokens[:, length - HALO :], "seq", [(i, i + 1) for i in range(devices - 1)])
@@ -432,53 +911,46 @@
 
     vmem = pltpu.VMEM
     ext = length + HALO
-    (normed, gate, xext, bcext, sraw, xact, bcact, step, cum, lstart, lstate, pre) = call(
-        front, seqs,
+    (normed, gate, xext, bcext, sraw, xact, bcact, step, cum, lstart, pre, entry) = call(
+        functools.partial(front, seqs=seqs, rounds=rounds), seqs + rounds, seqs,
         [tokens, halo, norm_gain[None], gate_weight, value_weight, state_weight, step_w,
          value_kernel, vo, state_kernel, so, bias, rate, wide, tri],
         [big(width, BF16), big(inner, F32), big(inner, BF16, ext), big(n2, BF16, ext), big(LANES, F32),
          big(inner, BF16), big(n2, BF16), big(LANES, F32), big(LANES, F32),
-         ((seqs, blocks, n, inner), BF16, True), big(inner, BF16, n + HALO), big(LANES, F32, 8)],
+         ((seqs, blocks, n, inner), F32, True), big(LANES, F32, 8),
+         ((seqs, n, inner), F32, False)],
         [vmem((ext, width), BF16), vmem((ext, inner), F32), vmem((ext, n2), F32), vmem((n, inner), F32),
-         vmem((8, LANES), F32)],
-        2 * flat * width * (2 * inner + n2 + LANES),
+         vmem((8, LANES), F32)] + Exchange.scratch(rounds, seqs, n, inner),
+        2 * flat * width * (2 * inner + n2 + LANES), 1,
     )
-    states = lax.all_gather(lstate, "seq")
-    log_fade = jnp.sum(states[:, :, n : n + 3].astype(F32), axis=2)
-    index = jnp.arange(devices)
-    prefix = jnp.cumsum(log_fade, axis=0)
-    zero = jnp.zeros_like(prefix[:1])
-    before = jnp.concatenate([zero, prefix[:-1]], axis=0)
-    my_before = lax.dynamic_index_in_dim(before, me, 0)
-    my_prefix = lax.dynamic_index_in_dim(prefix, me, 0)
-    earlier = (index < me)[:, None, None]
-    later = (index > me)[:, None, None]
-    from_left = jnp.where(earlier, jnp.exp(jnp.where(earlier, my_before - prefix, 0.0)), 0.0)
-    from_right = jnp.where(later, jnp.exp(jnp.where(later, before - my_prefix, 0.0)), 0.0)
-    entry = jnp.sum(from_left[:, :, None] * states[:, :, :n].astype(F32), axis=0)
-
     ssd, gn, y, sums = call(
-        scan_out, seqs,
+        scan_out, seqs, seqs,
         [xact, bcact, step, cum, gate, lstart, entry, pre, cotangent, out_weight, gain, skip, wide],
         [big(inner, F32), big(inner, F32), big(width, BF16), ((seqs, 8, length), F32, True)],
         [vmem((length, inner), BF16)],
         4 * flat * width * inner,
     )
-    y = lax.psum(y, "head")
-    sums = lax.psum(sums, "head")
-    gnormed, gate_grad, xg, cumg, stepg, bcg, lend, lgrad, mgg, skg = call(
-        functools.partial(back_one, inner_all=inner_all), seqs,
+    group = lax.axis_size("head")
+    sums = pl.pallas_call(
+        head_sums,
+        out_shape=jax.ShapeDtypeStruct(sums.shape, F32),
+        in_specs=[pl.BlockSpec(memory_space=pltpu.VMEM)],
+        out_specs=pl.BlockSpec(memory_space=pltpu.VMEM),
+        scratch_shapes=[vmem((group,) + sums.shape, F32), pltpu.SemaphoreType.DMA((group,)), pltpu.SemaphoreType.DMA((group,))],
+        compiler_params=pltpu.CompilerParams(collective_id=2, has_side_effects=True),
+    )(sums)
+    gnormed, gate_grad, xg, cumg, stepg, bcg, lend, rms, mgg, skg, after = call(
+        functools.partial(back_one, inner_all=inner_all, seqs=seqs, rounds=rounds), seqs + rounds, seqs,
         [xact, bcact, step, cum, gate, ssd, gn, sums, lstart, entry, pre, gain, skip, wide],
         [big(inner, BF16), big(inner, BF16), big(inner, F32), big(LANES, F32), big(LANES, F32), big(n2, F32),
-         ((seqs, blocks, n, inner), BF16, True), big(inner, BF16, n),
-         ((8, inner), F32, False), ((8, inner), F32, False)],
-        [vmem((T, inner), F32), vmem((n, inner), F32)],
-        2 * flat * T * inner * 8,
+         ((seqs, blocks, n, inner), F32, True), big(LANES, F32),
+         ((8, inner), F32, False), ((8, inner), F32, False), ((seqs, n, inner), F32, False)],
+        [vmem((T, inner), F32), vmem((n, inner), F32), vmem((T, inner), BF16), vmem((n, inner), F32)]
+        + Exchange.scratch(rounds, seqs, n, inner),
+        2 * flat * T * inner * 8, 3,
     )
-    grads = lax.all_gather(lgrad, "seq")
-    after = jnp.sum(from_right[:, :, None] * grads.astype(F32), axis=0)
     xpg, xhalo, bpg, bhalo, raw, vkg, skgr, head_rows = call(
-        back_two, seqs,
+        back_two, seqs, seqs,
         [xact, bcact, xext, bcext, step, cum, sraw, xg, cumg, stepg, bcg, lstart, entry, lend, after, pre,
          value_kernel, vo, state_kernel, so, bias, rate, wide, tri],
         [big(inner, BF16), big(inner, BF16, HALO), big(n2, BF16), big(n2, BF16, HALO), big(LANES, BF16),
@@ -500,34 +972,54 @@
     gate_weight_grad = t_mm(normed_f, gg_f).astype(BF16)
     value_weight_grad = t_mm(normed_f, xpg_f).astype(BF16)
     state_weight_grad = t_mm(normed_f, bpg_f).astype(BF16)
-    step_weight_grad = t_mm(normed_f, raw_f)[:, :heads].astype(BF16)
-    normed_grad = (
-        mm_t(gg_f, gate_weight) + mm_t(xpg_f, value_weight) + mm_t(bpg_f, state_weight) + mm_t(raw_f, step_w)
-    ).astype(BF16)
-    normed_grad = lax.psum(normed_grad, "head").astype(F32).reshape(seqs, length, width)
-
-    resid = tokens.astype(F32)
-    inv_rms = lax.rsqrt(jnp.mean(resid * resid, axis=-1, keepdims=True) + EPS)
-    mixer_rms = lax.rsqrt(sums[:, 0] / inner_all + EPS)[..., None]
-    result = (resid + y.astype(F32) * mixer_rms).astype(BF16)
-    norm_gain_grad = jnp.sum(normed_grad * resid * inv_rms, axis=(0, 1))
-    scaled_in = normed_grad * norm_gain
-    tokens_grad = (
-        cotangent.astype(F32)
-        + inv_rms * scaled_in
-        - resid * inv_rms**3 * (jnp.sum(scaled_in * resid, axis=-1, keepdims=True) / width)
-    )
-    skip_gain_grad = jnp.sum(skg[0].reshape(heads, head_size), axis=1)
-    step_bias_grad = head_rows[0, :heads]
-    log_rate_grad = head_rows[1, :heads] * rate_row
-    own = lax.psum(
-        (norm_gain_grad, vkg[: taps + 1], step_bias_grad, log_rate_grad, skip_gain_grad, mgg[0]), "seq"
-    )
-    norm_gain_grad, vkg, step_bias_grad, log_rate_grad, skip_gain_grad, mixer_gain_grad = own
-    skgr = lax.psum(skgr[: taps + 1], ("seq", "head"))
-    weights = lax.psum((gate_weight_grad, value_weight_grad, step_weight_grad, out_weight_grad), "seq")
-    gate_weight_grad, value_weight_grad, step_weight_grad, out_weight_grad = [v.astype(F32) for v in weights]
-    state_weight_grad = lax.psum(state_weight_grad, ("seq", "head")).astype(F32)
+    step_weight_grad = t_mm(normed_f, raw_f).astype(BF16)
+    head_row = jnp.pad(head_rows[:2].reshape(1, 2 * LANES), ((0, 0), (0, inner - 2 * LANES)))
+    small = jnp.concatenate([vkg[: taps + 1], mgg[:1], skg[:1], head_row], axis=0)
+    n_chunks = flat // CHUNK
+
+    def lagged(cols, lag):
+        return pl.BlockSpec((CHUNK, cols), lambda i: (jnp.clip(i - lag, 0, n_chunks - 1), 0))
+
+    def once(v):
+        return pl.BlockSpec(v.shape, lambda i: (0,) * v.ndim, pipeline_mode=pl.Buffered(1))
+
+    y_f = flatten(y)
+    late = (gate_weight, value_weight, state_weight, step_w, norm_gain[None], small, state_weight_grad, skgr)
+    result, tokens_grad, small, state_weight_grad = pl.pallas_call(
+        functools.partial(finish, n=n_chunks, rounds=rounds),
+        grid=(n_chunks + 3 * LAG,),
+        in_specs=[pl.BlockSpec(memory_space=pl.ANY), lagged(width, LAG)]
+        + [lagged(v.shape[1], 0) for v in (gg_f, xpg_f, bpg_f, raw_f)]
+        + [lagged(width, 3 * LAG), lagged(width, 3 * LAG), lagged(LANES, 3 * LAG)]
+        + [once(v) for v in late],
+        out_specs=[lagged(width, 3 * LAG), lagged(width, 3 * LAG), pl.BlockSpec((24, inner), lambda i: (0, 0)),
+                   once(state_weight_grad)],
+        out_shape=[
+            jax.ShapeDtypeStruct((flat, width), BF16), jax.ShapeDtypeStruct((flat, width), F32),
+            jax.ShapeDtypeStruct((24, inner), F32), jax.ShapeDtypeStruct(state_weight_grad.shape, BF16),
+        ],
+        scratch_shapes=Chain.scratch(n_chunks, CHUNK, width) + Chain.scratch(n_chunks, CHUNK, width) + [
+            vmem((24, inner), F32), vmem((rounds, 24, inner), F32), vmem((rounds, 24, inner), F32),
+            pltpu.SemaphoreType.DMA((rounds,)), pltpu.SemaphoreType.DMA((rounds,)),
+        ] + SmallSums.scratch(rounds, width, n2, skgr.shape),
+        compiler_params=pltpu.CompilerParams(
+            dimension_semantics=("arbitrary",), vmem_limit_bytes=62 * 1024 * 1024, collective_id=4, has_side_effects=True
+        ),
+        cost_estimate=pl.CostEstimate(flops=10**11, bytes_accessed=10**8, transcendentals=0),
+    )(y_f, y_f, gg_f, xpg_f, bpg_f, raw_f, flatten(tokens), flatten(cotangent), flatten(rms),
+      *late)
+    result, tokens_grad = result.reshape(tokens.shape), tokens_grad.reshape(tokens.shape)
+    vkg, mixer_gain_grad, skg, head_row = small[: taps + 1], small[taps + 1], small[taps + 2], small[taps + 3]
+    norm_gain_grad = small[8:10].reshape(width)
+    skgr = small[16:24, :n2]
+    skip_gain_grad = jnp.sum(skg.reshape(heads, head_size), axis=1)
+    step_bias_grad = head_row[:heads]
+    log_rate_grad = head_row[LANES : LANES + heads] * rate_row
+    out_weight_grad = lax.psum(out_weight_grad, "seq").astype(F32)
+    gate_weight_grad = lax.psum(gate_weight_grad, "seq").astype(F32)
+    value_weight_grad = lax.psum(value_weight_grad, "seq").astype(F32)
+    step_weight_grad = lax.psum(step_weight_grad, "seq")[:, :heads].astype(F32)
+    state_weight_grad = state_weight_grad.astype(F32)
     return (
         result, tokens_grad, norm_gain_grad, gate_weight_grad, value_weight_grad, state_weight_grad,
         step_weight_grad, vkg[:taps], vkg[taps], skgr[:taps], skgr[taps], step_bias_grad, log_rate_grad,

time: 1060 us -> 623 us (0.59)
  waiting for transfers between devices: 654 us -> 0.03 us
  Pallas kernels: 131 us -> 513 us
  blocking collectives: 91.1 us -> 0 us
  matrix products: 78.1 us -> 30 us
  other arithmetic: 58.4 us -> 18.4 us
  local copies, waits for them, and re-layouts: 13.3 us -> 33.4 us
    psum x4 -> x1, waiting for transfers between devices: 568 us -> 0.01 us  [shards(): gate_weight_grad = lax.psum(gate_weight_grad, 'seq').astype(F32)]
    pallas_call x4 -> x6, Pallas kernels: 131 us -> 513 us  [the longest x1 322 us: shards(): pl.pallas_call(functools.partial(finish, n=n_chunks, rounds=rounds), grid...]
    psum x3 -> x0, blocking collectives: 91.1 us -> none  [the longest x1 42 us: shards(): skgr = lax.psum(skgr[:taps + 1], ('seq', 'head'))]
    all_gather x2 -> x0, waiting for transfers between devices: 85.9 us -> none  [the longest x1 50.2 us: shards(): states = lax.all_gather(lstate, 'seq')]
    dot_general x4 -> x0, matrix products: 40.9 us -> none  [mm_t(): lax.dot_general(a, b, (((1,), (1,)), ((), ())), preferred_element_type=F32)]
    reduce_sum x6 -> x1, other arithmetic: 24.1 us -> 0.63 us  [shards(): skip_gain_grad = jnp.sum(skg.reshape(heads, head_size), axis=1)]
    sub x1 -> x0, other arithmetic: 15.8 us -> none  [shards(): cotangent.astype(F32) + inv_rms * scaled_in]
    unnamed x34 -> x37, local copies, waits for them, and re-layouts: 1.78 us -> 15.1 us
  transfers between devices with their start and end apart: 9 -> 4, of which waited for: 6 -> 0; matrix products, arithmetic and copies ran while one was open for 11% -> 8% of each run, Pallas kernels for 0% -> 52%
where the time goes in v2:
time: 623 us; the launch traced here: 615 us
  Pallas kernels  513 us (82%)
  local copies, waits for them, and re-layouts  33.4 us (5%)
  matrix products  30 us (5%)
  other arithmetic  18.4 us (3%)
  between operations  14.7 us (2%)
    pallas_call x1, Pallas kernels, shards(): pl.pallas_call(functools.partial(finish, n=n_chunks, rounds=rounds), grid...  322 us
    pallas_call x4, Pallas kernels, call(): pl.pallas_call(body, grid=(steps,), in_specs=in_specs, out_specs=out_spec...  181 us
    dot_general x5, matrix products, t_mm(): lax.dot_general(a, b, (((0,), (0,)), ((), ())), preferred_element_type=F32)  30 us
    unnamed x37, local copies, waits for them, and re-layouts  15.1 us
  transfers between devices with their start and end apart: 4, of which 0 were waited for; matrix products, arithmetic and copies ran while one was open for 8% of the time, Pallas kernels for 52%

profile of v2, /device:TPU:0, one launch (start us, length us, event | category | flops | bytes accessed | tf_op | source)
XLA Modules:
  0.0 614.7 jit_solution(12241211783571458865)
XLA Ops:
  8.2 2.4 collective-permute-start
  14.4 1.3 broadcast_in_dim.26.ngain
  21.7 55.1 %shard_map.279 = (bf16[4,512,1536]{2,1,0:T(8,128)(2,1)}, f32[4,512,768]{2,1,0:T(8,128)}, bf16[4,528,768]{2,1,0:T(8,128)(2,1)}, bf16[4,528,256]{2,1,0:T(8,128)(2,...) custom-call(bf16[4,512,1536]{2,1,0:T(8,128)(2,1)} %tok.1, ...), custom_call_target="tpu_custom_call" | custom-call | flops 12079595520 | bytes 41921536 | tf_op jit(solution)/shard_map/pallas_call | solution.py:863
  76.8 31.3 %shard_map.280 = (f32[4,512,768]{2,1,0:T(8,128)}, f32[4,512,768]{2,1,0:T(8,128)}, bf16[4,512,1536]{2,1,0:T(8,128)(2,1)}, f32[4,8,512]{2,1,0:T(8,128)}) custom-call(bf16[4,512,768]{2,1,0:T(8,128)(2,1)} %get-tuple-element.79.xact, bf16[4,512,256]{2,1,0:T(8,128)(2,1)} %get-tuple-element.80.bcact, f32[4,512,128]{2,1,0:T(8,128)} %get-tuple-element.81.step_i, ...), custom_call_target="tpu_custom_call" | custom-call | flops 9663676416 | bytes 45307904 | tf_op jit(solution)/shard_map/pallas_call | solution.py:863
  108.1 10.0 %shard_map.281.sums = f32[4,8,512]{2,1,0:T(8,128)} custom-call(f32[4,8,512]{2,1,0:T(8,128)} %get-tuple-element.90.mine), custom_call_target="tpu_custom_call" | custom-call | tf_op jit(solution)/shard_map/pallas_call | solution.py:934
  118.1 61.5 %shard_map.282 = (bf16[4,512,768]{2,1,0:T(8,128)(2,1)}, bf16[4,512,768]{2,1,0:T(8,128)(2,1)}, f32[4,512,768]{2,1,0:T(8,128)}, f32[4,512,128]{2,1,0:T(8,128)}, f3...) custom-call(bf16[4,512,768]{2,1,0:T(8,128)(2,1)} %get-tuple-element., ...), custom_call_target="tpu_custom_call" | custom-call | flops 6442450944 | bytes 52959232 | tf_op jit(solution)/shard_map/pallas_call | solution.py:863
  179.7 33.6 %shard_map.283 = (bf16[4,512,768]{2,1,0:T(8,128)(2,1)}, bf16[4,16,768]{2,1,0:T(8,128)(2,1)}, bf16[4,512,256]{2,1,0:T(8,128)(2,1)}, bf16[4,16,256]{2,1,0:T(8,128)...) custom-call(bf16[4,512,768]{2,1,0:T(8,128)(2,1)} %get-tuple-element.79.xact, ...), custom_call_target="tpu_custom_call" | custom-call | flops 3221225472 | bytes 37037056 | tf_op jit(solution)/shard_map/pallas_call | solution.py:863
  216.7 1.3 collective-permute-start.1
  218.0 4.8 fusion.1
  222.8 9.6 %bitcast_convert_fusion.2 = bf16[1536,768]{1,0:T(8,128)(2,1)} fusion(bf16[4,512,1536]{2,1,0:T(8,128)(2,1)} %get-tuple-element.111, bf16[4,512,768]{2,1,0:T(8,128)(2,1)S(1)} %copy-done.7), kind=kOutput, calls=%fused_computation.2 | convolution fusion | flops 4833017856 | bytes 11796480 | tf_op jit(solution)/shard_map/dot_general | solution.py:28
  232.5 6.4 %bitcast_convert_fusion = bf16[768,1536]{1,0:T(8,128)(2,1)} fusion(bf16[4,512,768]{2,1,0:T(8,128)(2,1)S(1)} %copy-done.8, bf16[4,512,1536]{2,1,0:T(8,128)(2,1)S(1)} %bitcast.60), kind=kOutput, calls=%fused_computation | convolution fusion | flops 4833017856 | bytes 11796480 | tf_op jit(solution)/shard_map/dot_general | solution.py:28
  239.6 2.7 fusion.state_grad
  242.4 6.4 %bitcast_convert_fusion.1 = bf16[1536,768]{1,0:T(8,128)(2,1)} fusion(bf16[4,512,1536]{2,1,0:T(8,128)(2,1)S(1)} %bitcast.67, bf16[4,512,768]{2,1,0:T(8,128)(2,1)S(1)} %add_dynamic-update-slice_fusion), kind=kOutput, calls=%fused_computation.1 | convolution fusion | flops 4833017856 | bytes 11796480 | tf_op jit(solution)/shard_map/dot_general | solution.py:28
  248.9 321.7 %shard_map.284 = (bf16[2048,1536]{1,0:T(8,128)(2,1)}, f32[2048,1536]{1,0:T(8,128)}, f32[24,768]{1,0:T(8,128)}, bf16[1536,256]{1,0:T(8,128)(2,1)}) custom-call(bf16[2048,1536]{1,0:T(8,128)(2,1)} %bitcast.64, bf16[2048,1536]{1,0:T(8,128)(2,1)} %bitcast.65, bf16[2048,768]{1,0:T(8,128)(2,1)} %bitcast.61, bf16[2048,768]{1,0:T(8,128)(2,1)} %bitcast.53, ...), custom_call_target="tpu_custom_call" | custom-call | flops 99999997952 | bytes 100000000 | tf_op jit(solution)/shard_map/pallas_call | solution.py:988
  571.8 1.3 slice.119
  573.8 1.3 slice.117
  575.8 1.5 slice_reduce_fusion
  577.3 2.4 convert_element_type.49
  582.7 1.4 slice_convert_fusion
  584.2 4.4 convert_element_type.46
  588.5 2.8 convert_element_type.48
  591.3 2.8 convert_element_type.53
  594.1 2.7 copy.51
  596.8 10.6 %copy.52 = f32[4,512,1536]{2,1,0:T(8,128)} copy(f32[4,512,1536]{2,1,0:T(8,128)} %bitcast.46) | data formatting | bytes 25165824
  (70 shorter events, 20.7 us)
Async XLA Ops:
  7.2 575.5 %all-reduce.7.cloned.1.call-start = ((), (), s32[]{:S(2)}) async-start(), calls=%async_computation | async-start | bytes 14942208 | tf_op jit(solution)/shard_map/psum | solution.py:1019
  8.2 12.8 %collective-permute-start = (bf16[4,16,1536]{2,1,0:T(8,128)(2,1)S(1)}, bf16[4,16,1536]{2,1,0:T(8,128)(2,1)S(1)}, u32[]{:S(2)}, u32[]{:S(2)}) collective-permute-start(bf16[4,16,1536]{2,1,0:T(8,128)(2,1)S(1)} %slice.108), channel_id=1, source_target_pairs={{0,4},{4,8},{8,12},{12,16},{16,20},{20,24},{24,28},{1,5},{5,9},{9,... | collective-permute-start | bytes 589832 | tf_op jit(solution)/shard_map/ppermute | solution.py:896
  21.0 0.7 copy-start.9
  215.4 24.1 %collective-permute-start.2 = (bf16[4,16,256]{2,1,0:T(8,128)(2,1)}, bf16[4,16,256]{2,1,0:T(8,128)(2,1)S(1)}, u32[]{:S(2)}, u32[]{:S(2)}) collective-permute-start(bf16[4,16,256]{2,1,0:T(8,128)(2,1)} %get-tuple-element.104), channel_id=1, source_target_pairs={{4,0},{8,4},{12,8},{16,12},{20,16},{24,20},{28,24},{5,1},{9,5},{13... | collective-permute-start | bytes 98312 | tf_op jit(solution)/shard_map/ppermute | solution.py:963
  216.7 25.6 %collective-permute-start.1 = (bf16[4,16,768]{2,1,0:T(8,128)(2,1)}, bf16[4,16,768]{2,1,0:T(8,128)(2,1)S(1)}, u32[]{:S(2)}, u32[]{:S(2)}) collective-permute-start(bf16[4,16,768]{2,1,0:T(8,128)(2,1)} %get-tuple-element.102), channel_id=1, source_target_pairs={{4,0},{8,4},{12,8},{16,12},{20,16},{24,20},{28,24},{5,1},{9,5},{13... | collective-permute-start | bytes 294920 | tf_op jit(solution)/shard_map/ppermute | solution.py:963
  218.0 4.8 copy-start.7
  218.0 14.4 %slice-start.2 = ((s8[6291456]{0:T(1024)(128)(4,1)}), s8[4194304]{0:T(1024)(128)(4,1)S(1)}, s32[]{:S(2)}) async-start(s8[6291456]{0:T(1024)(128)(4,1)} %bitcast.59), calls=%async_computation.3 | async-start | bytes 8388608
  222.8 9.6 %slice-start.3 = ((s8[6291456]{0:T(1024)(128)(4,1)}), s8[2097152]{0:T(1024)(128)(4,1)S(1)}, s32[]{:S(2)}) async-start(s8[6291456]{0:T(1024)(128)(4,1)} %bitcast.59), calls=%async_computation.4 | async-start | bytes 4194304
  222.8 9.6 %copy-start.8 = (bf16[4,512,768]{2,1,0:T(8,128)(2,1)S(1)}, bf16[4,512,768]{2,1,0:T(8,128)(2,1)}, u32[]{:S(2)}) copy-start(bf16[4,512,768]{2,1,0:T(8,128)(2,1)} %get-tuple-element.117) | copy-start | bytes 9437188
  222.8 16.7 %slice-start.4 = ((s8[6291456]{0:T(1024)(128)(4,1)}), s8[4194304]{0:T(1024)(128)(4,1)S(1)}, s32[]{:S(2)}) async-start(s8[6291456]{0:T(1024)(128)(4,1)} %bitcast.66), calls=%async_computation.5 | async-start | bytes 8388608
  232.4 6.4 %copy-start.2 = (f32[8,768]{1,0:T(8,128)S(1)}, f32[8,768]{1,0:T(8,128)}, u32[]{:S(2)}) copy-start(f32[8,768]{1,0:T(8,128)} %get-tuple-element.107) | copy-start | bytes 73732
  232.5 7.1 %copy-start.5 = (bf16[4,512,256]{2,1,0:T(8,128)(2,1)S(1)}, bf16[4,512,256]{2,1,0:T(8,128)(2,1)}, u32[]{:S(2)}) copy-start(bf16[4,512,256]{2,1,0:T(8,128)(2,1)} %get-tuple-element.103) | copy-start | bytes 3145732
  232.5 7.1 %slice-start.5 = ((s8[6291456]{0:T(1024)(128)(4,1)}), s8[2097152]{0:T(1024)(128)(4,1)S(1)}, s32[]{:S(2)}) async-start(s8[6291456]{0:T(1024)(128)(4,1)} %bitcast.66), calls=%async_computation.6 | async-start | bytes 4194304
  239.6 2.8 copy-start.6
  239.6 2.7 copy-start.3
  242.4 6.5 %copy-start.4 = (bf16[4,512,768]{2,1,0:T(8,128)(2,1)}, bf16[4,512,768]{2,1,0:T(8,128)(2,1)S(1)}, u32[]{:S(2)}) copy-start(bf16[4,512,768]{2,1,0:T(8,128)(2,1)S(1)} %add_dynamic-update-slice_fusion) | copy-start | bytes 9437188
  248.8 332.7 %copy-start.10 = (f32[12]{0:T(128)S(1)}, f32[12]{0:T(128)}, u32[]{:S(2)}) copy-start(f32[12]{0:T(128)} %param.31) | copy-start | bytes 148
  584.2 4.4 copy-start.1
  584.2 10.0 %slice-start = ((s8[6291456]{0:T(1024)(128)(4,1)}), s8[4194304]{0:T(1024)(128)(4,1)S(1)}, s32[]{:S(2)}) async-start(s8[6291456]{0:T(1024)(128)(4,1)} %bitcast.47), calls=%async_computation.1 | async-start | bytes 8388608
  588.5 2.8 copy-start
  588.5 5.6 slice-start.1
Sparse Core Ops, SparseCore 0:
  249.0 125.9 all-reduce.6

commit v3 on v2

--- a/solution.py
+++ b/solution.py
@@ -105,6 +105,195 @@
 
 
 MESH = pl.DeviceIdType.MESH
+CHUNK = 64
+LAG = 2
+
+
+def greet_head():
+    z = lax.axis_index("head")
+    for d in range(1, 4):
+        pl.semaphore_signal(
+            pltpu.get_barrier_semaphore(), inc=1, device_id={"head": lax.rem(z + d, 4)}, device_id_type=MESH)
+
+
+class Chain:
+    def __init__(self, own, got, far, sems):
+        z = lax.axis_index("head")
+        self.end = (z == 0) | (z == 3)
+        self.side = z + 1 - 2 * (z % 2)
+        self.other = 3 - z
+        self.own, self.got, self.far = own, got, far
+        self.sems = sems
+
+    @staticmethod
+    def scratch(n, chunk, width):
+        buffer = pltpu.VMEM((n, chunk, width), BF16)
+        return [buffer, buffer, buffer] + [pltpu.SemaphoreType.DMA((n,))] * 6
+
+    def copy(self, kind, k):
+        src, dst, to = [(self.own, self.got, self.side), (self.own, self.far, self.other), (self.got, self.got, self.side)][kind]
+        return pltpu.make_async_remote_copy(
+            src_ref=src.at[k], dst_ref=dst.at[k],
+            send_sem=self.sems[2 * kind].at[k], recv_sem=self.sems[2 * kind + 1].at[k],
+            device_id={"head": to}, device_id_type=MESH,
+        )
+
+    def inward(self, k):
+        @pl.when(self.end)
+        def _():
+            self.copy(0, k).start()
+
+    def meet(self, stage, k):
+        self.copy(stage, k).wait_recv()
+        if stage == 0:
+            self.own[k] = (self.own[k].astype(F32) + self.got[k].astype(F32)).astype(BF16)
+        else:
+            self.got[k] = (self.own[k].astype(F32) + self.far[k].astype(F32)).astype(BF16)
+
+    def onward(self, stage, k):
+        @pl.when(jnp.logical_not(self.end))
+        def _():
+            self.meet(stage - 1, k)
+            self.copy(stage, k).start()
+
+    def total(self, k):
+        @pl.when(self.end)
+        def _():
+            self.copy(2, k).wait_recv()
+
+        return self.got[k].astype(F32)
+
+    def drain(self, n):
+        def one(k, _):
+            @pl.when(self.end)
+            def _():
+                self.copy(0, k).wait_send()
+
+            @pl.when(jnp.logical_not(self.end))
+            def _():
+                self.copy(1, k).wait_send()
+                self.copy(2, k).wait_send()
+
+            return 0
+
+        lax.fori_loop(0, n, one, 0)
+
+
+class Rider:
+    def __init__(self, first, ticks, count, hbm, own, got, far, sems, local):
+        self.first, self.ticks, self.count = first, ticks, count
+        self.base = max(first - 2 * LAG, 0)
+        self.hbm, self.local = hbm, local
+        self.chain = Chain(own, got, far, sems)
+
+    @staticmethod
+    def size(first, ticks, count):
+        return min(first + ticks, count) - max(first - 2 * LAG, 0)
+
+    @staticmethod
+    def scratch(first, ticks, count, width):
+        return Chain.scratch(Rider.size(first, ticks, count), CHUNK, width) + [pltpu.SemaphoreType.DMA((2,))]
+
+    def span(self, stage):
+        low = self.first - stage * LAG
+        return max(low, 0), min(low + self.ticks, self.count)
+
+    def load(self):
+        size = self.size(self.first, self.ticks, self.count)
+        own = pltpu.make_async_copy(self.hbm.at[pl.ds(self.base, size)], self.chain.own, self.local.at[0])
+        own.start()
+        ready = min(max(self.first - LAG, 0), self.count) - self.base
+        if ready > 0:
+
+            @pl.when(jnp.logical_not(self.chain.end))
+            def _():
+                got = pltpu.make_async_copy(
+                    self.hbm.at[pl.ds(self.base, ready)], self.chain.got.at[pl.ds(0, ready)], self.local.at[1])
+                got.start()
+                got.wait()
+
+        own.wait()
+
+    def tick(self, t):
+        chain = self.chain
+        for stage in (2, 1, 0):
+            low, high = self.span(stage)
+            k = self.first - stage * LAG + t
+
+            @pl.when((k >= low) & (k < high) & (t < self.ticks))
+            def _():
+                at = k - self.base
+                if stage == 0:
+                    chain.inward(at)
+                else:
+                    self.follow(stage, at, t >= LAG)
+
+    def follow(self, stage, at, pending):
+        chain = self.chain
+        middle = jnp.logical_not(chain.end)
+
+        @pl.when(middle & pending)
+        def _():
+            chain.meet(stage - 1, at)
+
+        @pl.when(middle)
+        def _():
+            chain.copy(stage, at).start()
+
+    def drain(self):
+        chain = self.chain
+
+        def each(stage):
+            low, high = self.span(stage)
+            lax.fori_loop(low - self.base, high - self.base, lambda k, _: (chain.copy(stage, k).wait_send(), 0)[1], 0)
+
+        @pl.when(chain.end)
+        def _():
+            each(0)
+
+        @pl.when(jnp.logical_not(chain.end))
+        def _():
+            each(1)
+            each(2)
+
+    def close(self):
+        chain = self.chain
+        middle = jnp.logical_not(chain.end)
+
+        def each(low, high, do):
+            if high > low:
+                lax.fori_loop(low - self.base, high - self.base, lambda k, _: (do(k), 0)[1], 0)
+
+        @pl.when(middle)
+        def _():
+            for stage in (0, 1):
+                low, high = self.span(stage)
+                started = max(self.first - stage * LAG + self.ticks - LAG, low)
+                each(started, high, lambda k: chain.meet(stage, k))
+            for stage in (1, 2):
+                each(*self.span(stage), lambda k: chain.copy(stage, k).wait_send())
+
+        @pl.when(chain.end)
+        def _():
+            each(*self.span(2), lambda k: chain.copy(2, k).wait_recv())
+            each(*self.span(0), lambda k: chain.copy(0, k).wait_send())
+
+        def store(ref, low, high):
+            if high > low:
+                at = pl.ds(low - self.base, high - low)
+                copy = pltpu.make_async_copy(ref.at[at], self.hbm.at[pl.ds(low, high - low)], self.local.at[0])
+                copy.start()
+                copy.wait()
+
+        @pl.when(middle)
+        def _():
+            reached = self.span(1)[1]
+            store(chain.got, self.base, reached)
+            store(chain.own, reached, self.span(0)[1])
+
+        @pl.when(chain.end)
+        def _():
+            store(chain.got, *self.span(2))
 
 
 class Exchange:
@@ -118,11 +307,13 @@
         bit = 1 << r
         return self.me + bit - 2 * bit * (lax.div(self.me, bit) % 2)
 
-    def greet(self):
+    def greet(self, with_head=False):
         barrier = pltpu.get_barrier_semaphore()
         for r in range(self.rounds):
             pl.semaphore_signal(barrier, inc=1, device_id={"seq": self.partner(r)}, device_id_type=MESH)
-        pl.semaphore_wait(barrier, self.rounds)
+        if with_head:
+            greet_head()
+        pl.semaphore_wait(barrier, self.rounds + 3 * with_head)
 
     def copy(self, r, s):
         return pltpu.make_async_remote_copy(
@@ -333,17 +524,21 @@
 
 
 def back_one(
-    xact, bcact, step_i, cum_i, gate, ssd, gn, sums, lstart, entry, pre, mgain, skip, wide,
-    gnormed_o, gate_grad_o, xg_o, cumg_o, stepg_o, bcg_o, lend_o, rms_o, mgg_o, skg_o, after_o,
+    xact, bcact, step_i, cum_i, gate, ssd, gn, sums, lstart, entry, pre, mgain, skip, wide, y_in,
+    gnormed_o, gate_grad_o, xg_o, cumg_o, stepg_o, bcg_o, lend_o, rms_o, mgg_o, skg_o, after_o, y_all,
     z, acc, dys, use, total, before, logs, out, back, send, recv,
-    *, inner_all, seqs, rounds,
+    yown, ygot, yfar, ta, tb, tc, td, te, tf, ylocal,
+    *, inner_all, seqs, rounds, plan,
 ):
     i = pl.program_id(0)
+    blocks = xact.shape[1] // T
     scan = Exchange(rounds, True, total, before, logs, out, back, send, recv)
+    rider = Rider(*plan, y_all, yown, ygot, yfar, (ta, tb, tc, td, te, tf), ylocal)
 
     @pl.when(i == 0)
     def _():
-        scan.greet()
+        scan.greet(with_head=True)
+        rider.load()
         mgg_o[...] = jnp.zeros_like(mgg_o)
         skg_o[...] = jnp.zeros_like(skg_o)
 
@@ -352,22 +547,27 @@
         back_one_rows(
             xact, bcact, step_i, cum_i, gate, ssd, gn, sums, lstart, entry, pre, mgain, skip, wide,
             gnormed_o, gate_grad_o, xg_o, cumg_o, stepg_o, bcg_o, lend_o, rms_o, mgg_o, skg_o,
-            z, acc, dys, use, inner_all,
+            z, acc, dys, use, inner_all, lambda b: rider.tick(i * blocks + b),
         )
-        blocks = xact.shape[1] // T
         scan.begin(i, acc[...], expand_row(pre[0, blocks : blocks + 1], wide[...]))
 
     scan.advance(i, seqs)
 
+    @pl.when(i >= seqs)
+    def _():
+        for k in (0, 1):
+            rider.tick(seqs * blocks + (i - seqs) * 2 + k)
+
     @pl.when(i == seqs + rounds - 1)
     def _():
         after_o[...] = before[...]
+        rider.close()
 
 
 def back_one_rows(
     xact, bcact, step_i, cum_i, gate, ssd, gn, sums, lstart, entry, pre, mgain, skip, wide,
     gnormed_o, gate_grad_o, xg_o, cumg_o, stepg_o, bcg_o, lend_o, rms_o, mgg_o, skg_o,
-    z, acc, dys, use, inner_all,
+    z, acc, dys, use, inner_all, tick,
 ):
     length = xact.shape[1]
     blocks = length // T
@@ -376,6 +576,7 @@
     acc[...] = jnp.zeros_like(acc)
 
     def block(i, _):
+        tick(i)
         b = blocks - 1 - i
         r = rows_of(b)
         sums_b = sums[0, :, r]
@@ -459,18 +660,24 @@
 
 def back_two(
     xact, bcact, xext, bcext, step_i, cum_i, sraw, xg, cumg, stepg, bcg, lstart, entry, lend, after, pre,
-    vk, vo, sk, so, sbias, rate, wide, tri,
-    xpg_o, xhalo_o, bpg_o, bhalo_o, raw_o, vkg_o, skg_o, heads_o,
-    xe, be, xcg, bcg_s,
+    vk, vo, sk, so, sbias, rate, wide, tri, y_in,
+    xpg_o, xhalo_o, bpg_o, bhalo_o, raw_o, vkg_o, skg_o, heads_o, y_all,
+    xe, be, xcg, bcg_s, yown, ygot, yfar, ta, tb, tc, td, te, tf, ylocal,
+    *, seqs, plan,
 ):
     length = xact.shape[1]
     blocks = length // T
     n = bcact.shape[2] // 2
     taps = vk.shape[0]
     base = HALO - taps + 1
-
-    @pl.when(pl.program_id(0) == 0)
-    def _():
+    step_at = pl.program_id(0)
+    rider = Rider(*plan, y_all, yown, ygot, yfar, (ta, tb, tc, td, te, tf), ylocal)
+
+    @pl.when(step_at == 0)
+    def _():
+        greet_head()
+        pl.semaphore_wait(pltpu.get_barrier_semaphore(), 3)
+        rider.load()
         vkg_o[...] = jnp.zeros_like(vkg_o)
         skg_o[...] = jnp.zeros_like(skg_o)
         heads_o[...] = jnp.zeros_like(heads_o)
@@ -494,6 +701,7 @@
         out[taps : taps + 1] += jnp.sum(grad, axis=0, keepdims=True)
 
     for b in range(blocks):
+        rider.tick(step_at * blocks + b)
         r0 = b * T
         r = slice(r0, r0 + T)
         xa = xact[0, r, :].astype(F32)
@@ -547,6 +755,10 @@
         xpg_o[0, r0 : r0 + T] = conv_back(xcg, vk, HALO + r0, T)
         bpg_o[0, r0 : r0 + T] = conv_back(bcg_s, sk, HALO + r0, T)
 
+    @pl.when(step_at == seqs - 1)
+    def _():
+        rider.close()
+
 
 def head_sums(mine, out, slots, send, recv):
     z = lax.axis_index("head")
@@ -571,71 +783,6 @@
     out[...] = total
     for copy in copies:
         copy.wait_send()
-
-
-class Chain:
-    def __init__(self, own, got, far, sems):
-        z = lax.axis_index("head")
-        self.end = (z == 0) | (z == 3)
-        self.side = z + 1 - 2 * (z % 2)
-        self.other = 3 - z
-        self.own, self.got, self.far = own, got, far
-        self.sems = sems
-
-    @staticmethod
-    def scratch(n, chunk, width):
-        buffer = pltpu.VMEM((n, chunk, width), BF16)
-        return [buffer, buffer, buffer] + [pltpu.SemaphoreType.DMA((n,))] * 6
-
-    def copy(self, kind, k, source=None):
-        src, dst, to = [(self.own, self.got, self.side), (self.own, self.far, self.other), (self.got, self.got, self.side)][kind]
-        return pltpu.make_async_remote_copy(
-            src_ref=src.at[k] if source is None else source, dst_ref=dst.at[k],
-            send_sem=self.sems[2 * kind].at[k], recv_sem=self.sems[2 * kind + 1].at[k],
-            device_id={"head": to}, device_id_type=MESH,
-        )
-
-    def inward(self, k, source=None):
-        @pl.when(self.end)
-        def _():
-            self.copy(0, k, source).start()
-
-    def across(self, k, mine=None):
-        @pl.when(jnp.logical_not(self.end))
-        def _():
-            self.copy(0, k).wait_recv()
-            value = (self.own[k] if mine is None else mine[...]).astype(F32)
-            self.own[k] = (value + self.got[k].astype(F32)).astype(BF16)
-            self.copy(1, k).start()
-
-    def outward(self, k):
-        @pl.when(jnp.logical_not(self.end))
-        def _():
-            self.copy(1, k).wait_recv()
-            self.got[k] = (self.own[k].astype(F32) + self.far[k].astype(F32)).astype(BF16)
-            self.copy(2, k).start()
-
-    def total(self, k):
-        @pl.when(self.end)
-        def _():
-            self.copy(2, k).wait_recv()
-
-        return self.got[k].astype(F32)
-
-    def drain(self, n):
-        def one(k, _):
-            @pl.when(self.end)
-            def _():
-                self.copy(0, k).wait_send()
-
-            @pl.when(jnp.logical_not(self.end))
-            def _():
-                self.copy(1, k).wait_send()
-                self.copy(2, k).wait_send()
-
-            return 0
-
-        lax.fori_loop(0, n, one, 0)
 
 
 class SmallSums:
@@ -746,21 +893,17 @@
                 self.gathering(r - 1, True).start()
 
 
-CHUNK = 64
-LAG = 2
-
-
 def finish(
-    y_all, y, gate_grad, xpg, bpg, raw, tok, cot, rms, gate_w, value_w, state_w, step_w, ngain, small, state_grad, state_rows,
+    y, gate_grad, xpg, bpg, raw, tok, cot, rms, gate_w, value_w, state_w, step_w, ngain, small, state_grad, state_rows, y_all,
     result_o, tokens_grad_o, small_o, state_o,
-    own, got, far, sa, sb, sc, sd, se, sf, yown, ygot, yfar, ta, tb, tc, td, te, tf, rows, out, back, send, recv,
+    own, got, far, sa, sb, sc, sd, se, sf, yown, ygot, yfar, ta, tb, tc, td, te, tf, ylocal, rows, out, back, send, recv,
     s_acc, s_out, s_back, s_zback, s_done, s_sems, s_vec, s_vback, s_vsems,
-    *, n, rounds,
+    *, n, rounds, plan,
 ):
     i = pl.program_id(0)
     sums = SmallSums(rounds, s_acc, s_out, s_back, s_zback, s_done, s_sems, s_vec, s_vback, s_vsems)
     chain = Chain(own, got, far, (sa, sb, sc, sd, se, sf))
-    ychain = Chain(yown, ygot, yfar, (ta, tb, tc, td, te, tf))
+    rider = Rider(*plan, y_all, yown, ygot, yfar, (ta, tb, tc, td, te, tf), ylocal)
     me = lax.axis_index("seq")
 
     def partner(r):
@@ -772,32 +915,24 @@
         barrier = pltpu.get_barrier_semaphore()
         for r in range(rounds):
             pl.semaphore_signal(barrier, inc=1, device_id={"seq": partner(r)}, device_id_type=MESH)
-        z = lax.axis_index("head")
-        for d in range(1, 4):
-            pl.semaphore_signal(barrier, inc=1, device_id={"head": lax.rem(z + d, 4)}, device_id_type=MESH)
+        greet_head()
         pl.semaphore_wait(barrier, rounds + 3)
+        rider.load()
         s_acc[...] = state_grad[...].astype(F32)
         s_vec[...] = state_rows[...]
         rows[0:8] = small[...]
         rows[8:] = jnp.zeros_like(rows[8:])
 
-    k = i - 2 * LAG
-
-    @pl.when((k >= 0) & (k < n))
-    def _():
-        chain.outward(k)
-        ychain.outward(k)
-
-    k = i - LAG
-
-    @pl.when((k >= 0) & (k < n))
-    def _():
-        chain.across(k)
-        ychain.across(k, y)
+    rider.tick(i)
+    for stage in (2, 1):
+        k = i - stage * LAG
+
+        @pl.when((k >= 0) & (k < n))
+        def _():
+            chain.onward(stage, k)
 
     @pl.when(i < n)
     def _():
-        ychain.inward(i, y_all.at[pl.ds(pl.multiple_of(i * CHUNK, CHUNK), CHUNK)])
         value = mm_t(gate_grad[...], gate_w[...]) + mm_t(xpg[...], value_w[...])
         own[i] = (value + (mm_t(bpg[...], state_w[...]) + mm_t(raw[...], step_w[...]))).astype(BF16)
         chain.inward(i)
@@ -813,11 +948,20 @@
     @pl.when(k >= 0)
     def _():
         grad = chain.total(k)
-        branch = ychain.total(k)
+        rms_k = rms[:, 0:1]
         t = tok[...].astype(F32)
         width = t.shape[1]
         inv = lax.rsqrt(jnp.mean(t * t, axis=1, keepdims=True) + EPS)
-        result_o[...] = (t + branch * rms[:, 0:1]).astype(BF16)
+        if rider.base > 0:
+
+            @pl.when(k < rider.base)
+            def _():
+                result_o[...] = (t + y[...].astype(F32) * rms_k).astype(BF16)
+
+        @pl.when(k >= rider.base)
+        def _():
+            result_o[...] = (t + rider.chain.total(k - rider.base) * rms_k).astype(BF16)
+
         scaled = grad * ngain[...]
         dot = jnp.sum(scaled * t, axis=1, keepdims=True) / width
         tokens_grad_o[...] = cot[...].astype(F32) + inv * scaled - t * (inv * inv * inv * dot)
@@ -829,7 +973,7 @@
     @pl.when(i == n + 3 * LAG - 1)
     def _():
         chain.drain(n)
-        ychain.drain(n)
+        rider.drain()
         rows[16:24, 0 : s_vec.shape[1]] = s_vec[...]
         for r in range(rounds):
             copy = pltpu.make_async_remote_copy(
@@ -844,7 +988,7 @@
         small_o[...] = rows[...]
 
 
-def call(body, steps, seqs, ins, outs, scratch, flops, collective_id=None):
+def call(body, steps, seqs, ins, outs, scratch, flops, collective_id=None, carried=None):
     def cut(shape):
         rest = tuple(shape[1:])
         return pl.BlockSpec((1,) + rest, lambda s: (jnp.minimum(s, seqs - 1),) + (0,) * len(rest))
@@ -854,6 +998,14 @@
 
     in_specs = [cut(a.shape) if a.ndim >= 3 else whole(a.shape) for a in ins]
     out_specs = [cut(s) if c else whole(s) for s, _, c in outs]
+    out_shape = [jax.ShapeDtypeStruct(s, d) for s, d, _ in outs]
+    aliases = {}
+    if carried is not None:
+        aliases = {len(ins): len(outs)}
+        in_specs.append(pl.BlockSpec(memory_space=pl.ANY))
+        out_specs.append(pl.BlockSpec(memory_space=pl.ANY))
+        out_shape.append(jax.ShapeDtypeStruct(carried.shape, carried.dtype))
+        ins = ins + [carried]
     moved = sum(a.size * a.dtype.itemsize for a in ins)
     for s, d, _ in outs:
         size = jnp.dtype(d).itemsize
@@ -865,8 +1017,9 @@
         grid=(steps,),
         in_specs=in_specs,
         out_specs=out_specs,
-        out_shape=[jax.ShapeDtypeStruct(s, d) for s, d, _ in outs],
+        out_shape=out_shape,
         scratch_shapes=scratch,
+        input_output_aliases=aliases,
         compiler_params=pltpu.CompilerParams(
             dimension_semantics=("arbitrary",), vmem_limit_bytes=60 * 1024 * 1024,
             collective_id=collective_id, has_side_effects=collective_id is not None,
@@ -939,25 +1092,29 @@
         scratch_shapes=[vmem((group,) + sums.shape, F32), pltpu.SemaphoreType.DMA((group,)), pltpu.SemaphoreType.DMA((group,))],
         compiler_params=pltpu.CompilerParams(collective_id=2, has_side_effects=True),
     )(sums)
-    gnormed, gate_grad, xg, cumg, stepg, bcg, lend, rms, mgg, skg, after = call(
-        functools.partial(back_one, inner_all=inner_all, seqs=seqs, rounds=rounds), seqs + rounds, seqs,
+    n_chunks = flat // CHUNK
+    y = y.reshape(n_chunks, CHUNK, width)
+    plan = (0, seqs * blocks + 2 * rounds, n_chunks)
+    gnormed, gate_grad, xg, cumg, stepg, bcg, lend, rms, mgg, skg, after, y = call(
+        functools.partial(back_one, inner_all=inner_all, seqs=seqs, rounds=rounds, plan=plan), seqs + rounds, seqs,
         [xact, bcact, step, cum, gate, ssd, gn, sums, lstart, entry, pre, gain, skip, wide],
         [big(inner, BF16), big(inner, BF16), big(inner, F32), big(LANES, F32), big(LANES, F32), big(n2, F32),
          ((seqs, blocks, n, inner), F32, True), big(LANES, F32),
          ((8, inner), F32, False), ((8, inner), F32, False), ((seqs, n, inner), F32, False)],
         [vmem((T, inner), F32), vmem((n, inner), F32), vmem((T, inner), BF16), vmem((n, inner), F32)]
-        + Exchange.scratch(rounds, seqs, n, inner),
-        2 * flat * T * inner * 8, 3,
+        + Exchange.scratch(rounds, seqs, n, inner) + Rider.scratch(*plan, width),
+        2 * flat * T * inner * 8, 3, y,
     )
-    xpg, xhalo, bpg, bhalo, raw, vkg, skgr, head_rows = call(
-        back_two, seqs, seqs,
+    plan = (plan[0] + plan[1], seqs * blocks, n_chunks)
+    xpg, xhalo, bpg, bhalo, raw, vkg, skgr, head_rows, y = call(
+        functools.partial(back_two, seqs=seqs, plan=plan), seqs, seqs,
         [xact, bcact, xext, bcext, step, cum, sraw, xg, cumg, stepg, bcg, lstart, entry, lend, after, pre,
          value_kernel, vo, state_kernel, so, bias, rate, wide, tri],
         [big(inner, BF16), big(inner, BF16, HALO), big(n2, BF16), big(n2, BF16, HALO), big(LANES, BF16),
          ((8, inner), F32, False), ((8, n2), F32, False), ((8, LANES), F32, False)],
         [vmem((ext, inner), F32), vmem((ext, n2), F32), vmem((ext + HALO, inner), F32),
-         vmem((ext + HALO, n2), F32)],
-        2 * flat * T * inner * 4,
+         vmem((ext + HALO, n2), F32)] + Rider.scratch(*plan, width),
+        2 * flat * T * inner * 4, 5, y,
     )
     back = [(i + 1, i) for i in range(devices - 1)]
     xhalo, bhalo = lax.ppermute((xhalo, bhalo), "seq", back)
@@ -975,7 +1132,7 @@
     step_weight_grad = t_mm(normed_f, raw_f).astype(BF16)
     head_row = jnp.pad(head_rows[:2].reshape(1, 2 * LANES), ((0, 0), (0, inner - 2 * LANES)))
     small = jnp.concatenate([vkg[: taps + 1], mgg[:1], skg[:1], head_row], axis=0)
-    n_chunks = flat // CHUNK
+    plan = (plan[0] + plan[1], n_chunks - plan[0] - plan[1] + 3 * LAG, n_chunks)
 
     def lagged(cols, lag):
         return pl.BlockSpec((CHUNK, cols), lambda i: (jnp.clip(i - lag, 0, n_chunks - 1), 0))
@@ -983,22 +1140,21 @@
     def once(v):
         return pl.BlockSpec(v.shape, lambda i: (0,) * v.ndim, pipeline_mode=pl.Buffered(1))
 
-    y_f = flatten(y)
     late = (gate_weight, value_weight, state_weight, step_w, norm_gain[None], small, state_weight_grad, skgr)
     result, tokens_grad, small, state_weight_grad = pl.pallas_call(
-        functools.partial(finish, n=n_chunks, rounds=rounds),
+        functools.partial(finish, n=n_chunks, rounds=rounds, plan=plan),
         grid=(n_chunks + 3 * LAG,),
-        in_specs=[pl.BlockSpec(memory_space=pl.ANY), lagged(width, LAG)]
+        in_specs=[lagged(width, 3 * LAG)]
         + [lagged(v.shape[1], 0) for v in (gg_f, xpg_f, bpg_f, raw_f)]
         + [lagged(width, 3 * LAG), lagged(width, 3 * LAG), lagged(LANES, 3 * LAG)]
-        + [once(v) for v in late],
+        + [once(v) for v in late] + [pl.BlockSpec(memory_space=pl.ANY)],
         out_specs=[lagged(width, 3 * LAG), lagged(width, 3 * LAG), pl.BlockSpec((24, inner), lambda i: (0, 0)),
                    once(state_weight_grad)],
         out_shape=[
             jax.ShapeDtypeStruct((flat, width), BF16), jax.ShapeDtypeStruct((flat, width), F32),
             jax.ShapeDtypeStruct((24, inner), F32), jax.ShapeDtypeStruct(state_weight_grad.shape, BF16),
         ],
-        scratch_shapes=Chain.scratch(n_chunks, CHUNK, width) + Chain.scratch(n_chunks, CHUNK, width) + [
+        scratch_shapes=Chain.scratch(n_chunks, CHUNK, width) + Rider.scratch(*plan, width) + [
             vmem((24, inner), F32), vmem((rounds, 24, inner), F32), vmem((rounds, 24, inner), F32),
             pltpu.SemaphoreType.DMA((rounds,)), pltpu.SemaphoreType.DMA((rounds,)),
         ] + SmallSums.scratch(rounds, width, n2, skgr.shape),
@@ -1006,8 +1162,8 @@
             dimension_semantics=("arbitrary",), vmem_limit_bytes=62 * 1024 * 1024, collective_id=4, has_side_effects=True
         ),
         cost_estimate=pl.CostEstimate(flops=10**11, bytes_accessed=10**8, transcendentals=0),
-    )(y_f, y_f, gg_f, xpg_f, bpg_f, raw_f, flatten(tokens), flatten(cotangent), flatten(rms),
-      *late)
+    )(y.reshape(flat, width), gg_f, xpg_f, bpg_f, raw_f, flatten(tokens), flatten(cotangent), flatten(rms),
+      *late, y)
     result, tokens_grad = result.reshape(tokens.shape), tokens_grad.reshape(tokens.shape)
     vkg, mixer_gain_grad, skg, head_row = small[: taps + 1], small[taps + 1], small[taps + 2], small[taps + 3]
     norm_gain_grad = small[8:10].reshape(width)

time: 623 us -> 564 us (0.905)
  Pallas kernels: 513 us -> 453 us
    pallas_call x1, Pallas kernels: 322 us -> 231 us  [shards(): pl.pallas_call(functools.partial(finish, n=n_chunks, rounds=rounds, plan=...]
    pallas_call x4, Pallas kernels: 181 us -> 213 us  [call(): pl.pallas_call(body, grid=(steps,), in_specs=in_specs, out_specs=out_spec...]
  transfers between devices with their start and end apart: 4 -> 4, of which waited for: 0 -> 0; matrix products, arithmetic and copies ran while one was open for 8% -> 8% of each run, Pallas kernels for 52% -> 42%
where the time goes in v3:
time: 564 us; the launch traced here: 555 us
  Pallas kernels  453 us (80%)
  local copies, waits for them, and re-layouts  33.4 us (6%)
  matrix products  30 us (5%)
  other arithmetic  18.5 us (3%)
  between operations  14.8 us (3%)
    pallas_call x1, Pallas kernels, shards(): pl.pallas_call(functools.partial(finish, n=n_chunks, rounds=rounds, plan=...  231 us
    pallas_call x4, Pallas kernels, call(): pl.pallas_call(body, grid=(steps,), in_specs=in_specs, out_specs=out_spec...  213 us
    dot_general x5, matrix products, t_mm(): lax.dot_general(a, b, (((0,), (0,)), ((), ())), preferred_element_type=F32)  30 us
    unnamed x37, local copies, waits for them, and re-layouts  15.1 us
  transfers between devices with their start and end apart: 4, of which 0 were waited for; matrix products, arithmetic and copies ran while one was open for 8% of the time, Pallas kernels for 42%

profile of v3, /device:TPU:0, one launch (start us, length us, event | category | flops | bytes accessed | tf_op | source)
XLA Modules:
  0.0 555.1 jit_solution(2999478505889760074)
XLA Ops:
  8.2 2.4 collective-permute-start
  14.4 1.3 broadcast_in_dim.26.ngain
  21.7 55.2 %shard_map.279 = (bf16[4,512,1536]{2,1,0:T(8,128)(2,1)}, f32[4,512,768]{2,1,0:T(8,128)}, bf16[4,528,768]{2,1,0:T(8,128)(2,1)}, bf16[4,528,256]{2,1,0:T(8,128)(2,...) custom-call(bf16[4,512,1536]{2,1,0:T(8,128)(2,1)} %tok.1, ...), custom_call_target="tpu_custom_call" | custom-call | flops 12079595520 | bytes 41921536 | tf_op jit(solution)/shard_map/pallas_call | solution.py:1015
  76.9 31.3 %shard_map.280 = (f32[4,512,768]{2,1,0:T(8,128)}, f32[4,512,768]{2,1,0:T(8,128)}, bf16[4,512,1536]{2,1,0:T(8,128)(2,1)}, f32[4,8,512]{2,1,0:T(8,128)}) custom-call(bf16[4,512,768]{2,1,0:T(8,128)(2,1)} %get-tuple-element.81.xact, bf16[4,512,256]{2,1,0:T(8,128)(2,1)} %get-tuple-element.82.bcact, f32[4,512,128]{2,1,0:T(8,128)} %get-tuple-element.85.step_i, ...), custom_call_target="tpu_custom_call" | custom-call | flops 9663676416 | bytes 45307904 | tf_op jit(solution)/shard_map/pallas_call | solution.py:1015
  108.2 10.0 %shard_map.281.sums = f32[4,8,512]{2,1,0:T(8,128)} custom-call(f32[4,8,512]{2,1,0:T(8,128)} %get-tuple-element.94.mine), custom_call_target="tpu_custom_call" | custom-call | tf_op jit(solution)/shard_map/pallas_call | solution.py:1087
  118.3 81.5 %shard_map.282 = (bf16[4,512,768]{2,1,0:T(8,128)(2,1)}, bf16[4,512,768]{2,1,0:T(8,128)(2,1)}, f32[4,512,768]{2,1,0:T(8,128)}, f32[4,512,128]{2,1,0:T(8,128)}, f3...) custom-call(bf16[4,512,768]{2,1,0:T(8,128)(2,1)} %get-tuple-element., ...), custom_call_target="tpu_custom_call", output_to_operand_aliasing={{11}: (14, {})} | custom-call | flops 6442450944 | bytes 59250688 | tf_op jit(solution)/shard_map/pallas_call | solution.py:1015
  199.8 44.6 %shard_map.283 = (bf16[4,512,768]{2,1,0:T(8,128)(2,1)}, bf16[4,16,768]{2,1,0:T(8,128)(2,1)}, bf16[4,512,256]{2,1,0:T(8,128)(2,1)}, bf16[4,16,256]{2,1,0:T(8,128)...) custom-call(bf16[4,512,768]{2,1,0:T(8,128)(2,1)} %get-tuple-element., ...), custom_call_target="tpu_custom_call", output_to_operand_aliasing={{8}: (24, {})} | custom-call | flops 3221225472 | bytes 43328512 | tf_op jit(solution)/shard_map/pallas_call | solution.py:1015
  247.8 1.3 collective-permute-start.1
  249.1 4.8 fusion.1
  253.9 9.6 %bitcast_convert_fusion.2 = bf16[1536,768]{1,0:T(8,128)(2,1)} fusion(bf16[4,512,1536]{2,1,0:T(8,128)(2,1)} %get-tuple-element.115, bf16[4,512,768]{2,1,0:T(8,128)(2,1)S(1)} %copy-done.7), kind=kOutput, calls=%fused_computation.2 | convolution fusion | flops 4833017856 | bytes 11796480 | tf_op jit(solution)/shard_map/dot_general | solution.py:28
  263.6 6.4 %bitcast_convert_fusion = bf16[768,1536]{1,0:T(8,128)(2,1)} fusion(bf16[4,512,768]{2,1,0:T(8,128)(2,1)S(1)} %copy-done.8, bf16[4,512,1536]{2,1,0:T(8,128)(2,1)S(1)} %bitcast.63), kind=kOutput, calls=%fused_computation | convolution fusion | flops 4833017856 | bytes 11796480 | tf_op jit(solution)/shard_map/dot_general | solution.py:28
  270.7 2.7 fusion.state_grad
  273.5 6.4 %bitcast_convert_fusion.1 = bf16[1536,768]{1,0:T(8,128)(2,1)} fusion(bf16[4,512,1536]{2,1,0:T(8,128)(2,1)S(1)} %bitcast.68, bf16[4,512,768]{2,1,0:T(8,128)(2,1)S(1)} %add_dynamic-update-slice_fusion), kind=kOutput, calls=%fused_computation.1 | convolution fusion | flops 4833017856 | bytes 11796480 | tf_op jit(solution)/shard_map/dot_general | solution.py:28
  280.0 230.8 %shard_map.284 = (bf16[2048,1536]{1,0:T(8,128)(2,1)}, f32[2048,1536]{1,0:T(8,128)}, f32[24,768]{1,0:T(8,128)}, bf16[1536,256]{1,0:T(8,128)(2,1)}) custom-call(bf16[2048,1536]{1,0:T(8,128)(2,1)} %bitcast.48, bf16[2048,768]{1,0:T(8,128)(2,1)} %bitcast.64, bf16[2048,768]{1,0:T(8,128)(2,1)} %bitcast.56, bf16[2048,256]{1,0:T(8,128)(2,1)} %bitcast.59, ...), custom_call_target="tpu_custom_call" | custom-call | flops 99999997952 | bytes 100000000 | tf_op jit(solution)/shard_map/pallas_call | solution.py:1144
  512.0 1.3 slice.119
  514.1 1.3 slice.117
  516.0 1.5 slice_reduce_fusion
  517.6 2.4 convert_element_type.49
  523.0 1.4 slice_convert_fusion
  524.4 4.4 convert_element_type.46
  528.8 2.8 convert_element_type.48
  531.6 2.8 convert_element_type.53
  534.4 2.7 copy.55
  537.1 10.6 %copy.56 = f32[4,512,1536]{2,1,0:T(8,128)} copy(f32[4,512,1536]{2,1,0:T(8,128)} %bitcast.49) | data formatting | bytes 25165824
  (70 shorter events, 20.8 us)
Async XLA Ops:
  7.2 515.8 %all-reduce.7.cloned.1.call-start = ((), (), s32[]{:S(2)}) async-start(), calls=%async_computation | async-start | bytes 14942208 | tf_op jit(solution)/shard_map/psum | solution.py:1175
  8.2 12.9 %collective-permute-start = (bf16[4,16,1536]{2,1,0:T(8,128)(2,1)S(1)}, bf16[4,16,1536]{2,1,0:T(8,128)(2,1)S(1)}, u32[]{:S(2)}, u32[]{:S(2)}) collective-permute-start(bf16[4,16,1536]{2,1,0:T(8,128)(2,1)S(1)} %slice.108), channel_id=1, source_target_pairs={{0,4},{4,8},{8,12},{12,16},{16,20},{20,24},{24,28},{1,5},{5,9},{9,... | collective-permute-start | bytes 589832 | tf_op jit(solution)/shard_map/ppermute | solution.py:1049
  21.0 0.7 copy-start.9
  246.5 24.2 %collective-permute-start.2 = (bf16[4,16,256]{2,1,0:T(8,128)(2,1)}, bf16[4,16,256]{2,1,0:T(8,128)(2,1)S(1)}, u32[]{:S(2)}, u32[]{:S(2)}) collective-permute-start(bf16[4,16,256]{2,1,0:T(8,128)(2,1)} %get-tuple-element.108), channel_id=1, source_target_pairs={{4,0},{8,4},{12,8},{16,12},{20,16},{24,20},{28,24},{5,1},{9,5},{13... | collective-permute-start | bytes 98312 | tf_op jit(solution)/shard_map/ppermute | solution.py:1120
  247.8 25.7 %collective-permute-start.1 = (bf16[4,16,768]{2,1,0:T(8,128)(2,1)}, bf16[4,16,768]{2,1,0:T(8,128)(2,1)S(1)}, u32[]{:S(2)}, u32[]{:S(2)}) collective-permute-start(bf16[4,16,768]{2,1,0:T(8,128)(2,1)} %get-tuple-element.106), channel_id=1, source_target_pairs={{4,0},{8,4},{12,8},{16,12},{20,16},{24,20},{28,24},{5,1},{9,5},{13... | collective-permute-start | bytes 294920 | tf_op jit(solution)/shard_map/ppermute | solution.py:1120
  249.1 4.8 copy-start.7
  249.1 14.5 %slice-start.2 = ((s8[6291456]{0:T(1024)(128)(4,1)}), s8[4194304]{0:T(1024)(128)(4,1)S(1)}, s32[]{:S(2)}) async-start(s8[6291456]{0:T(1024)(128)(4,1)} %bitcast.62), calls=%async_computation.3 | async-start | bytes 8388608
  253.9 9.6 %slice-start.3 = ((s8[6291456]{0:T(1024)(128)(4,1)}), s8[2097152]{0:T(1024)(128)(4,1)S(1)}, s32[]{:S(2)}) async-start(s8[6291456]{0:T(1024)(128)(4,1)} %bitcast.62), calls=%async_computation.4 | async-start | bytes 4194304
  253.9 9.6 %copy-start.8 = (bf16[4,512,768]{2,1,0:T(8,128)(2,1)S(1)}, bf16[4,512,768]{2,1,0:T(8,128)(2,1)}, u32[]{:S(2)}) copy-start(bf16[4,512,768]{2,1,0:T(8,128)(2,1)} %get-tuple-element.121) | copy-start | bytes 9437188
  253.9 16.7 %slice-start.4 = ((s8[6291456]{0:T(1024)(128)(4,1)}), s8[4194304]{0:T(1024)(128)(4,1)S(1)}, s32[]{:S(2)}) async-start(s8[6291456]{0:T(1024)(128)(4,1)} %bitcast.67), calls=%async_computation.5 | async-start | bytes 8388608
  263.6 6.4 %copy-start.2 = (f32[8,768]{1,0:T(8,128)S(1)}, f32[8,768]{1,0:T(8,128)}, u32[]{:S(2)}) copy-start(f32[8,768]{1,0:T(8,128)} %get-tuple-element.111) | copy-start | bytes 73732
  263.6 7.1 %copy-start.5 = (bf16[4,512,256]{2,1,0:T(8,128)(2,1)S(1)}, bf16[4,512,256]{2,1,0:T(8,128)(2,1)}, u32[]{:S(2)}) copy-start(bf16[4,512,256]{2,1,0:T(8,128)(2,1)} %get-tuple-element.107) | copy-start | bytes 3145732
  263.6 7.1 %slice-start.5 = ((s8[6291456]{0:T(1024)(128)(4,1)}), s8[2097152]{0:T(1024)(128)(4,1)S(1)}, s32[]{:S(2)}) async-start(s8[6291456]{0:T(1024)(128)(4,1)} %bitcast.67), calls=%async_computation.6 | async-start | bytes 4194304
  270.7 2.7 copy-start.6
  270.7 2.7 copy-start.3
  273.5 6.4 %copy-start.4 = (bf16[4,512,768]{2,1,0:T(8,128)(2,1)}, bf16[4,512,768]{2,1,0:T(8,128)(2,1)S(1)}, u32[]{:S(2)}) copy-start(bf16[4,512,768]{2,1,0:T(8,128)(2,1)S(1)} %add_dynamic-update-slice_fusion) | copy-start | bytes 9437188
  280.0 241.8 %copy-start.10 = (f32[12]{0:T(128)S(1)}, f32[12]{0:T(128)}, u32[]{:S(2)}) copy-start(f32[12]{0:T(128)} %param.31) | copy-start | bytes 148
  524.4 4.4 copy-start.1
  524.4 10.0 %slice-start = ((s8[6291456]{0:T(1024)(128)(4,1)}), s8[4194304]{0:T(1024)(128)(4,1)S(1)}, s32[]{:S(2)}) async-start(s8[6291456]{0:T(1024)(128)(4,1)} %bitcast.50), calls=%async_computation.1 | async-start | bytes 8388608
  528.8 2.8 copy-start
  528.8 5.6 %slice-start.1 = ((s8[6291456]{0:T(1024)(128)(4,1)}), s8[2097152]{0:T(1024)(128)(4,1)S(1)}, s32[]{:S(2)}) async-start(s8[6291456]{0:T(1024)(128)(4,1)} %bitcast.50), calls=%async_computation.2 | async-start | bytes 4194304
Sparse Core Ops, SparseCore 0:
  280.1 128.6 all-reduce.6

commit v4 on v3

--- a/solution.py
+++ b/solution.py
@@ -317,8 +317,8 @@
 
     def copy(self, r, s):
         return pltpu.make_async_remote_copy(
-            src_ref=self.out.at[r, s], dst_ref=self.back.at[r, s],
-            send_sem=self.send.at[r, s], recv_sem=self.recv.at[r, s],
+            src_ref=self.out.at[r], dst_ref=self.back.at[r, s],
+            send_sem=self.send.at[r], recv_sem=self.recv.at[r, s],
             device_id={"seq": self.partner(r)}, device_id_type=MESH,
         )
 
@@ -330,11 +330,11 @@
 
     def push(self, r, s):
         n = self.total.shape[1]
-        self.out[r, s, 0:n] = self.total[s].astype(BF16)
+        self.out[r, 0:n] = self.total[s].astype(BF16)
         hi, mid, lo = [v.astype(F32) for v in split(self.logs[s, 0:1], 3)]
         at = lax.broadcasted_iota(jnp.int32, (HALO, hi.shape[1]), 0)
         tail = jnp.where(at == 0, hi, jnp.where(at == 1, mid, jnp.where(at == 2, lo, 0.0)))
-        self.out[r, s, n : n + HALO] = tail.astype(BF16)
+        self.out[r, n : n + HALO] = tail.astype(BF16)
         self.copy(r, s).start()
 
     def take(self, r, s):
@@ -356,11 +356,7 @@
         self.logs[s, 0:1] = mine + log
 
     def advance(self, i, seqs):
-        @pl.when(i < seqs)
-        def _():
-            self.push(0, i)
-
-        for r in range(self.rounds):
+        for r in reversed(range(self.rounds)):
             s = i - 1 - r
 
             @pl.when((s >= 0) & (s < seqs))
@@ -369,48 +365,175 @@
                 if r + 1 < self.rounds:
                     self.push(r + 1, s)
 
+        @pl.when(i < seqs)
+        def _():
+            self.push(0, i)
+
     @staticmethod
     def scratch(rounds, seqs, n, inner):
         return [
-            pltpu.VMEM((seqs, n, inner), F32), pltpu.VMEM((seqs, n, inner), F32), pltpu.VMEM((seqs, 8, inner), F32),
-            pltpu.VMEM((rounds, seqs, n + HALO, inner), BF16), pltpu.VMEM((rounds, seqs, n + HALO, inner), BF16),
-            pltpu.SemaphoreType.DMA((rounds, seqs)), pltpu.SemaphoreType.DMA((rounds, seqs)),
+            pltpu.VMEM((seqs, n, inner), F32), pltpu.VMEM((seqs, 8, inner), F32),
+            pltpu.VMEM((rounds, n + HALO, inner), BF16), pltpu.VMEM((rounds, seqs, n + HALO, inner), BF16),
+            pltpu.SemaphoreType.DMA((rounds,)), pltpu.SemaphoreType.DMA((rounds, seqs)),
         ]
 
 
-def front(
-    tok, halo, ngain, gate_w, value_w, state_w, step_w, vk, vo, sk, so, sbias, rate, wide, tri,
-    normed_o, gate_o, xext_o, bcext_o, sraw_o, xact_o, bcact_o, step_o, cum_o, lstart_o, pre_o, entry_o,
-    nx, xe, be, st, run, total, before, logs, out, back, send, recv,
-    *, seqs, rounds,
+def forward(
+    tok, tok_all, cot, ngain, gate_w, value_w, state_w, step_w, vk, vo, sk, so, sbias, rate, wide, tri, out_w, mgain, skip,
+    xext_o, bcext_o, sraw_o, pre_o, entry_o, sums_o,
+    xact_h, bcact_h, gate_h, step_h, cum_h, lstart_h, normed_h, ssd_h, gn_h, y_h,
+    xact, bcact, gate, step, cum, lstart, nx, ssd, gn, y_s, gm, xe, be, st, run, halo, mine, slots,
+    kept_sems, slot_sems, halo_send, halo_recv, sum_send, sum_recv,
+    total, logs, out, back, send, recv,
+    yown, ygot, yfar, ta, tb, tc, td, te, tf, ylocal,
+    *, seqs, rounds, plan,
 ):
     i = pl.program_id(0)
-    scan = Exchange(rounds, False, total, before, logs, out, back, send, recv)
+    s = i - rounds
+    steps = seqs + rounds
+    length = tok.shape[1]
+    me, devices = lax.axis_index("seq"), lax.axis_size("seq")
+    z = lax.axis_index("head")
+    scan = Exchange(rounds, False, total, entry_o, logs, out, back, send, recv)
+    rider = Rider(*plan, y_h, yown, ygot, yfar, (ta, tb, tc, td, te, tf), ylocal)
+    kept = [(xact, xact_h), (bcact, bcact_h), (gate, gate_h), (step, step_h), (cum, cum_h), (lstart, lstart_h)]
+    per_seq = length // CHUNK
+
+    def halo_copy(q):
+        return pltpu.make_async_remote_copy(
+            src_ref=tok_all.at[q, pl.ds(length - HALO, HALO)], dst_ref=halo.at[q],
+            send_sem=halo_send.at[q], recv_sem=halo_recv.at[q],
+            device_id={"seq": lax.rem(me + 1, devices)}, device_id_type=MESH,
+        )
+
+    def keep(k, q):
+        src, dst = kept[k]
+        return pltpu.make_async_copy(src.at[q], dst.at[q], kept_sems.at[k, q])
+
+    def normed_copy(q):
+        return pltpu.make_async_copy(nx.at[pl.ds(HALO, length)], normed_h.at[q], slot_sems.at[0])
+
+    def scan_copies(q):
+        return [
+            pltpu.make_async_copy(ssd.at[0], ssd_h.at[q], slot_sems.at[1]),
+            pltpu.make_async_copy(gn.at[0], gn_h.at[q], slot_sems.at[2]),
+        ]
+
+    def y_copy(q, skip_rider):
+        first = plan[1] if skip_rider else 0
+        at = pl.ds(q * per_seq + first, per_seq - first)
+        return pltpu.make_async_copy(y_s.at[pl.ds(first, per_seq - first)], y_h.at[at], slot_sems.at[3])
+
+    def sum_copy(q, d):
+        return pltpu.make_async_remote_copy(
+            src_ref=mine.at[q], dst_ref=slots.at[q, z], send_sem=sum_send.at[q, d], recv_sem=sum_recv.at[q, d],
+            device_id={"head": lax.rem(z + d, 4)}, device_id_type=MESH,
+        )
 
     @pl.when(i == 0)
     def _():
-        scan.greet()
+        barrier = pltpu.get_barrier_semaphore()
+        for d in range(1, devices):
+            pl.semaphore_signal(barrier, inc=1, device_id={"seq": lax.rem(me + d, devices)}, device_id_type=MESH)
+        greet_head()
+        pl.semaphore_wait(barrier, devices - 1 + 3)
+
+        @pl.when(me < devices - 1)
+        def _():
+            for q in range(seqs):
+                halo_copy(q).start()
+
+        @pl.when(me == 0)
+        def _():
+            halo[...] = jnp.zeros_like(halo)
 
     @pl.when(i < seqs)
     def _():
+        @pl.when(i > 0)
+        def _():
+            normed_copy(i).wait()
+
+        def arrive():
+            @pl.when(me > 0)
+            def _():
+                halo_copy(i).wait_recv()
+
+        one = pl.ds(i, 1)
         front_rows(
-            tok, halo, ngain, gate_w, value_w, state_w, step_w, vk, vo, sk, so, sbias, rate, wide, tri,
-            normed_o, gate_o, xext_o, bcext_o, sraw_o, xact_o, bcact_o, step_o, cum_o, lstart_o, pre_o,
-            nx, xe, be, st, run,
+            tok, halo.at[one], ngain, gate_w, value_w, state_w, step_w, vk, vo, sk, so, sbias, rate, wide, tri,
+            gate.at[one], xext_o, bcext_o, sraw_o, xact.at[one], bcact.at[one], step.at[one], cum.at[one],
+            lstart.at[one], pre_o.at[one], nx, xe, be, st, run, arrive,
         )
+        normed_copy(i).start()
+        for k in range(len(kept)):
+            keep(k, i).start()
         scan.begin(i, st[...], expand_row(run[0:1], wide[...]))
 
     scan.advance(i, seqs)
 
-    @pl.when(i == seqs + rounds - 1)
-    def _():
-        entry_o[...] = before[...]
+    @pl.when(s >= 0)
+    def _():
+        @pl.when(s > 0)
+        def _():
+            for copy in scan_copies(s):
+                copy.wait()
+
+        one = pl.ds(s, 1)
+        scan_out(
+            xact.at[one], bcact.at[one], step.at[one], cum.at[one], gate.at[one], lstart.at[one], entry_o.at[one],
+            pre_o.at[one], cot, out_w, mgain, skip, wide, ssd, gn, mine.at[one], gm, lambda b: rider.tick((s - 1) * 2 + b),
+        )
+        for copy in scan_copies(s):
+            copy.start()
+        for d in range(1, 4):
+            sum_copy(s, d).start()
+        slots[s, z] = mine[s]
+
+        @pl.when(s == 1)
+        def _():
+            y_copy(0, True).wait()
+
+        @pl.when(s > 1)
+        def _():
+            y_copy(s, False).wait()
+
+        for b in range(length // T):
+            value = mm(gm[b * T : (b + 1) * T], out_w[...]).astype(BF16)
+            y_s[b * T // CHUNK : (b + 1) * T // CHUNK] = value.reshape(T // CHUNK, CHUNK, value.shape[1])
+
+        @pl.when(s == 0)
+        def _():
+            yown[...] = y_s[0 : plan[1]]
+            y_copy(0, True).start()
+
+        @pl.when(s > 0)
+        def _():
+            y_copy(s, False).start()
+
+    @pl.when(i == steps - 1)
+    def _():
+        rider.close()
+        for q in range(seqs):
+            for d in range(1, 4):
+                sum_copy(q, d).wait()
+            sums_o[q] = (slots[q, 0] + slots[q, 1]) + (slots[q, 2] + slots[q, 3])
+            for k in range(len(kept)):
+                keep(k, q).wait()
+        normed_copy(0).wait()
+        for copy in scan_copies(0):
+            copy.wait()
+        y_copy(1, False).wait()
+
+        @pl.when(me < devices - 1)
+        def _():
+            for q in range(seqs):
+                halo_copy(q).wait_send()
 
 
 def front_rows(
     tok, halo, ngain, gate_w, value_w, state_w, step_w, vk, vo, sk, so, sbias, rate, wide, tri,
-    normed_o, gate_o, xext_o, bcext_o, sraw_o, xact_o, bcact_o, step_o, cum_o, lstart_o, pre_o,
-    nx, xe, be, st, run,
+    gate_o, xext_o, bcext_o, sraw_o, xact_o, bcact_o, step_o, cum_o, lstart_o, pre_o,
+    nx, xe, be, st, run, arrive,
 ):
     length = tok.shape[1]
     blocks = length // T
@@ -421,24 +544,21 @@
         inv = lax.rsqrt(jnp.mean(v * v, axis=1, keepdims=True) + EPS)
         return (v * inv * ngain[...]).astype(BF16)
 
+    def norm_rows(b, _):
+        nx[pl.ds(pl.multiple_of(HALO + b * SUB, HALO), SUB), :] = norm(tok[0, pl.ds(pl.multiple_of(b * SUB, SUB), SUB), :])
+        return 0
+
+    lax.fori_loop(0, length // SUB, norm_rows, 0)
+    gate_o[0] = mm(nx[HALO:], gate_w[...])
+    sraw_o[0] = mm(nx[HALO:], step_w[...])
+    arrive()
     nx[0:HALO] = norm(halo[0])
-
-    def norm_rows(b, _):
-        r = rows_of(b)
-        v = norm(tok[0, r, :])
-        nx[pl.ds(pl.multiple_of(HALO + b * T, HALO), T), :] = v
-        normed_o[0, r, :] = v
-        return 0
-
-    lax.fori_loop(0, blocks, norm_rows, 0)
     x = mm(nx[...], value_w[...]).astype(BF16)
     xext_o[0] = x
     xe[...] = x.astype(F32)
     bc = mm(nx[...], state_w[...]).astype(BF16)
     bcext_o[0] = bc
     be[...] = bc.astype(F32)
-    gate_o[0] = mm(nx[HALO:], gate_w[...])
-    sraw_o[0] = mm(nx[HALO:], step_w[...])
     st[...] = jnp.zeros_like(st)
     run[...] = jnp.zeros_like(run)
     pre_o[0] = jnp.zeros_like(pre_o[0])
@@ -472,8 +592,7 @@
 
 def scan_out(
     xact, bcact, step_i, cum_i, gate, lstart, entry, pre, cot, out_w, mgain, skip, wide,
-    ssd_o, gn_o, y_o, sums_o,
-    gm,
+    ssd_o, gn_o, sums_o, gm, tick,
 ):
     length = xact.shape[1]
     blocks = length // T
@@ -482,6 +601,7 @@
     gn_o[0] = mm_t(cot[0], out_w[...])
 
     def block(b, _):
+        tick(b)
         r = rows_of(b)
         xa = xact[0, r, :]
         bca = bcact[0, r, :]
@@ -520,19 +640,18 @@
         return 0
 
     lax.fori_loop(0, blocks, block, 0)
-    y_o[0] = mm(gm[...], out_w[...]).astype(BF16)
 
 
 def back_one(
     xact, bcact, step_i, cum_i, gate, ssd, gn, sums, lstart, entry, pre, mgain, skip, wide, y_in,
     gnormed_o, gate_grad_o, xg_o, cumg_o, stepg_o, bcg_o, lend_o, rms_o, mgg_o, skg_o, after_o, y_all,
-    z, acc, dys, use, total, before, logs, out, back, send, recv,
+    z, acc, dys, use, total, logs, out, back, send, recv,
     yown, ygot, yfar, ta, tb, tc, td, te, tf, ylocal,
     *, inner_all, seqs, rounds, plan,
 ):
     i = pl.program_id(0)
     blocks = xact.shape[1] // T
-    scan = Exchange(rounds, True, total, before, logs, out, back, send, recv)
+    scan = Exchange(rounds, True, total, after_o, logs, out, back, send, recv)
     rider = Rider(*plan, y_all, yown, ygot, yfar, (ta, tb, tc, td, te, tf), ylocal)
 
     @pl.when(i == 0)
@@ -560,7 +679,6 @@
 
     @pl.when(i == seqs + rounds - 1)
     def _():
-        after_o[...] = before[...]
         rider.close()
 
 
@@ -760,31 +878,6 @@
         rider.close()
 
 
-def head_sums(mine, out, slots, send, recv):
-    z = lax.axis_index("head")
-    count = slots.shape[0]
-    barrier = pltpu.get_barrier_semaphore()
-    for d in range(1, count):
-        pl.semaphore_signal(barrier, inc=1, device_id={"head": lax.rem(z + d, count)}, device_id_type=MESH)
-    pl.semaphore_wait(barrier, count - 1)
-    copies = []
-    for d in range(1, count):
-        copies.append(pltpu.make_async_remote_copy(
-            src_ref=mine, dst_ref=slots.at[z], send_sem=send.at[d], recv_sem=recv.at[d],
-            device_id={"head": lax.rem(z + d, count)}, device_id_type=MESH,
-        ))
-        copies[-1].start()
-    slots[z] = mine[...]
-    for copy in copies:
-        copy.wait_recv()
-    total = slots[0]
-    for d in range(1, count):
-        total = total + slots[d]
-    out[...] = total
-    for copy in copies:
-        copy.wait_send()
-
-
 class SmallSums:
     def __init__(self, rounds, acc, out, back, zback, done, sems, vec, vback, vsems):
         self.rounds = rounds
@@ -1046,7 +1139,6 @@
     assert devices == 1 << rounds
     inner_all = inner * lax.axis_size("head")
 
-    halo = lax.ppermute(tokens[:, length - HALO :], "seq", [(i, i + 1) for i in range(devices - 1)])
     pad = LANES - heads
     rate_row = -jnp.exp(log_rate)
     rate = jnp.pad(rate_row, (0, pad))[None]
@@ -1064,37 +1156,48 @@
 
     vmem = pltpu.VMEM
     ext = length + HALO
-    (normed, gate, xext, bcext, sraw, xact, bcact, step, cum, lstart, pre, entry) = call(
-        functools.partial(front, seqs=seqs, rounds=rounds), seqs + rounds, seqs,
-        [tokens, halo, norm_gain[None], gate_weight, value_weight, state_weight, step_w,
-         value_kernel, vo, state_kernel, so, bias, rate, wide, tri],
-        [big(width, BF16), big(inner, F32), big(inner, BF16, ext), big(n2, BF16, ext), big(LANES, F32),
-         big(inner, BF16), big(n2, BF16), big(LANES, F32), big(LANES, F32),
-         ((seqs, blocks, n, inner), F32, True), big(LANES, F32, 8),
-         ((seqs, n, inner), F32, False)],
-        [vmem((ext, width), BF16), vmem((ext, inner), F32), vmem((ext, n2), F32), vmem((n, inner), F32),
-         vmem((8, LANES), F32)] + Exchange.scratch(rounds, seqs, n, inner),
-        2 * flat * width * (2 * inner + n2 + LANES), 1,
-    )
-    ssd, gn, y, sums = call(
-        scan_out, seqs, seqs,
-        [xact, bcact, step, cum, gate, lstart, entry, pre, cotangent, out_weight, gain, skip, wide],
-        [big(inner, F32), big(inner, F32), big(width, BF16), ((seqs, 8, length), F32, True)],
-        [vmem((length, inner), BF16)],
-        4 * flat * width * inner,
-    )
-    group = lax.axis_size("head")
-    sums = pl.pallas_call(
-        head_sums,
-        out_shape=jax.ShapeDtypeStruct(sums.shape, F32),
-        in_specs=[pl.BlockSpec(memory_space=pltpu.VMEM)],
-        out_specs=pl.BlockSpec(memory_space=pltpu.VMEM),
-        scratch_shapes=[vmem((group,) + sums.shape, F32), pltpu.SemaphoreType.DMA((group,)), pltpu.SemaphoreType.DMA((group,))],
-        compiler_params=pltpu.CompilerParams(collective_id=2, has_side_effects=True),
-    )(sums)
     n_chunks = flat // CHUNK
-    y = y.reshape(n_chunks, CHUNK, width)
-    plan = (0, seqs * blocks + 2 * rounds, n_chunks)
+    steps = seqs + rounds
+    plan = (0, min(2 * (seqs - 1), length // CHUNK), n_chunks)
+    dma = pltpu.SemaphoreType.DMA
+
+    def block(shape, lag):
+        return pl.BlockSpec((1,) + shape, lambda i: (jnp.clip(i - lag, 0, seqs - 1), 0, 0))
+
+    def once(v):
+        return pl.BlockSpec(v.shape, lambda i: (0,) * len(v.shape), pipeline_mode=pl.Buffered(1))
+
+    def shape_of(cols, dtype, rows=length):
+        return jax.ShapeDtypeStruct((seqs, rows, cols), dtype)
+
+    fixed = (norm_gain[None], gate_weight, value_weight, state_weight, step_w, value_kernel, vo, state_kernel, so, bias, rate,
+             wide, tri, out_weight, gain, skip)
+    held = (shape_of(LANES, F32, 8), shape_of(inner, F32, n), shape_of(length, F32, 8))
+    anywhere = pl.BlockSpec(memory_space=pl.ANY)
+    (xext, bcext, sraw, pre, entry, sums, xact, bcact, gate, step, cum, lstart, normed, ssd, gn, y) = pl.pallas_call(
+        functools.partial(forward, seqs=seqs, rounds=rounds, plan=plan),
+        grid=(steps,),
+        in_specs=[block((length, width), 0), anywhere, block((length, width), rounds)] + [once(v) for v in fixed],
+        out_specs=[block((ext, inner), 0), block((ext, n2), 0), block((length, LANES), 0)] + [once(v) for v in held] + [anywhere] * 10,
+        out_shape=[shape_of(inner, BF16, ext), shape_of(n2, BF16, ext), shape_of(LANES, F32), *held,
+                   shape_of(inner, BF16), shape_of(n2, BF16), shape_of(inner, F32), shape_of(LANES, F32), shape_of(LANES, F32),
+                   jax.ShapeDtypeStruct((seqs, blocks, n, inner), F32), shape_of(width, BF16), shape_of(inner, F32),
+                   shape_of(inner, F32), jax.ShapeDtypeStruct((n_chunks, CHUNK, width), BF16)],
+        scratch_shapes=[
+            vmem((seqs, length, inner), BF16), vmem((seqs, length, n2), BF16), vmem((seqs, length, inner), F32),
+            vmem((seqs, length, LANES), F32), vmem((seqs, length, LANES), F32), vmem((seqs, blocks, n, inner), F32),
+            vmem((ext, width), BF16), vmem((1, length, inner), F32), vmem((1, length, inner), F32),
+            vmem((length // CHUNK, CHUNK, width), BF16), vmem((length, inner), BF16),
+            vmem((ext, inner), F32), vmem((ext, n2), F32), vmem((n, inner), F32), vmem((8, LANES), F32),
+            vmem((seqs, HALO, width), BF16), vmem((seqs, 8, length), F32), vmem((seqs, 4, 8, length), F32),
+            dma((6, seqs)), dma((4,)), dma((seqs,)), dma((seqs,)), dma((seqs, 4)), dma((seqs, 4)),
+        ] + Exchange.scratch(rounds, seqs, n, inner) + Rider.scratch(*plan, width),
+        compiler_params=pltpu.CompilerParams(
+            dimension_semantics=("arbitrary",), vmem_limit_bytes=62 * 1024 * 1024, collective_id=1, has_side_effects=True
+        ),
+        cost_estimate=pl.CostEstimate(flops=2 * flat * width * 4 * inner, bytes_accessed=10**8, transcendentals=0),
+    )(tokens, tokens, cotangent, *fixed)
+    plan = (plan[1], seqs * blocks + 2 * rounds, n_chunks)
     gnormed, gate_grad, xg, cumg, stepg, bcg, lend, rms, mgg, skg, after, y = call(
         functools.partial(back_one, inner_all=inner_all, seqs=seqs, rounds=rounds, plan=plan), seqs + rounds, seqs,
         [xact, bcact, step, cum, gate, ssd, gn, sums, lstart, entry, pre, gain, skip, wide],
@@ -1136,9 +1239,6 @@
 
     def lagged(cols, lag):
         return pl.BlockSpec((CHUNK, cols), lambda i: (jnp.clip(i - lag, 0, n_chunks - 1), 0))
-
-    def once(v):
-        return pl.BlockSpec(v.shape, lambda i: (0,) * v.ndim, pipeline_mode=pl.Buffered(1))
 
     late = (gate_weight, value_weight, state_weight, step_w, norm_gain[None], small, state_weight_grad, skgr)
     result, tokens_grad, small, state_weight_grad = pl.pallas_call(

time: 564 us -> 525 us (0.931)
  Pallas kernels: 453 us -> 415 us
  matrix products: 30 us -> 38 us
    pallas_call x4 -> x2, Pallas kernels: 213 us -> 130 us  [call(): pl.pallas_call(body, grid=(steps,), in_specs=in_specs, out_specs=out_spec...]
    pallas_call x1, Pallas kernels: 10 us -> 82 us  [shards(): pl.pallas_call(functools.partial(forward, seqs=seqs, rounds=rounds, plan=...]
    pallas_call x1, Pallas kernels: 231 us -> 203 us  [shards(): pl.pallas_call(functools.partial(finish, n=n_chunks, rounds=rounds, plan=...]
    dot_general x5, matrix products: 30 us -> 38 us  [t_mm(): lax.dot_general(a, b, (((0,), (0,)), ((), ())), preferred_element_type=F32)]
    unnamed x37 -> x35, local copies, waits for them, and re-layouts: 15.1 us -> 14.4 us
  transfers between devices with their start and end apart: 4 -> 3, of which waited for: 0 -> 0; matrix products, arithmetic and copies ran while one was open for 8% -> 9% of each run, Pallas kernels for 42% -> 39%
where the time goes in v4:
time: 525 us; the launch traced here: 520 us
  Pallas kernels  415 us (79%)
  matrix products  38 us (7%)
  local copies, waits for them, and re-layouts  31.8 us (6%)
  other arithmetic  18.5 us (4%)
  between operations  14.5 us (3%)
    pallas_call x1, Pallas kernels, shards(): pl.pallas_call(functools.partial(finish, n=n_chunks, rounds=rounds, plan=...  203 us
    pallas_call x2, Pallas kernels, call(): pl.pallas_call(body, grid=(steps,), in_specs=in_specs, out_specs=out_spec...  130 us
    pallas_call x1, Pallas kernels, shards(): pl.pallas_call(functools.partial(forward, seqs=seqs, rounds=rounds, plan=...  82 us
    dot_general x5, matrix products, t_mm(): lax.dot_general(a, b, (((0,), (0,)), ((), ())), preferred_element_type=F32)  38 us
    unnamed x35, local copies, waits for them, and re-layouts  14.4 us
  transfers between devices with their start and end apart: 3, of which 0 were waited for; matrix products, arithmetic and copies ran while one was open for 9% of the time, Pallas kernels for 39%

profile of v4, /device:TPU:0, one launch (start us, length us, event | category | flops | bytes accessed | tf_op | source)
XLA Modules:
  0.0 520.4 jit_solution(906429538326048039)
XLA Ops:
  8.6 1.3 broadcast_in_dim.27.vo
  9.8 1.3 broadcast_in_dim.31.mgain
  11.1 1.3 broadcast_in_dim.26.ngain
  17.7 82.0 %shard_map.279 = (bf16[4,528,768]{2,1,0:T(8,128)(2,1)}, bf16[4,528,256]{2,1,0:T(8,128)(2,1)}, f32[4,512,128]{2,1,0:T(8,128)}, f32[4,8,128]{2,1,0:T(8,128)}, f32[...) custom-call(bf16[4,512,1536]{2,1,0:T(8,128)(2,1)} %tok_all.1, ...), custom_call_target="tpu_custom_call" | custom-call | flops 19327352832 | bytes 100000000 | tf_op jit(solution)/shard_map/pallas_call | solution.py:1177
  99.7 84.6 %shard_map.280 = (bf16[4,512,768]{2,1,0:T(8,128)(2,1)}, bf16[4,512,768]{2,1,0:T(8,128)(2,1)}, f32[4,512,768]{2,1,0:T(8,128)}, f32[4,512,128]{2,1,0:T(8,128)}, f3...) custom-call(bf16[4,512,768]{2,1,0:T(8,128)(2,1)} %get-tuple-element., ...), custom_call_target="tpu_custom_call", output_to_operand_aliasing={{11}: (14, {})} | custom-call | flops 6442450944 | bytes 59250688 | tf_op jit(solution)/shard_map/pallas_call | solution.py:1108
  184.3 45.4 %shard_map.281 = (bf16[4,512,768]{2,1,0:T(8,128)(2,1)}, bf16[4,16,768]{2,1,0:T(8,128)(2,1)}, bf16[4,512,256]{2,1,0:T(8,128)(2,1)}, bf16[4,16,256]{2,1,0:T(8,128)...) custom-call(bf16[4,512,768]{2,1,0:T(8,128)(2,1)} %get-tuple-element., ...), custom_call_target="tpu_custom_call", output_to_operand_aliasing={{8}: (24, {})} | custom-call | flops 3221225472 | bytes 43328512 | tf_op jit(solution)/shard_map/pallas_call | solution.py:1108
  229.8 1.3 collective-permute-start.1
  231.1 1.3 collective-permute-start
  234.5 4.8 fusion.1
  239.3 17.6 %bitcast_convert_fusion.2 = bf16[1536,768]{1,0:T(8,128)(2,1)} fusion(bf16[4,512,1536]{2,1,0:T(8,128)(2,1)} %get-tuple-element.115, bf16[4,512,768]{2,1,0:T(8,128)(2,1)S(1)} %copy-done.7), kind=kOutput, calls=%fused_computation.2 | convolution fusion | flops 4833017856 | bytes 11796480 | tf_op jit(solution)/shard_map/dot_general | solution.py:28
  257.0 6.4 %bitcast_convert_fusion = bf16[768,1536]{1,0:T(8,128)(2,1)} fusion(bf16[4,512,768]{2,1,0:T(8,128)(2,1)S(1)} %copy-done.8, bf16[4,512,1536]{2,1,0:T(8,128)(2,1)S(1)} %bitcast.61), kind=kOutput, calls=%fused_computation | convolution fusion | flops 4833017856 | bytes 11796480 | tf_op jit(solution)/shard_map/dot_general | solution.py:28
  264.1 2.7 fusion.state_grad
  266.9 6.4 %bitcast_convert_fusion.1 = bf16[1536,768]{1,0:T(8,128)(2,1)} fusion(bf16[4,512,1536]{2,1,0:T(8,128)(2,1)S(1)} %bitcast.66, bf16[4,512,768]{2,1,0:T(8,128)(2,1)S(1)} %add_dynamic-update-slice_fusion), kind=kOutput, calls=%fused_computation.1 | convolution fusion | flops 4833017856 | bytes 11796480 | tf_op jit(solution)/shard_map/dot_general | solution.py:28
  273.4 203.0 %shard_map.282 = (bf16[2048,1536]{1,0:T(8,128)(2,1)}, f32[2048,1536]{1,0:T(8,128)}, f32[24,768]{1,0:T(8,128)}, bf16[1536,256]{1,0:T(8,128)(2,1)}) custom-call(bf16[2048,1536]{1,0:T(8,128)(2,1)} %bitcast.46, bf16[2048,768]{1,0:T(8,128)(2,1)} %bitcast.62, bf16[2048,768]{1,0:T(8,128)(2,1)} %bitcast.53, bf16[2048,256]{1,0:T(8,128)(2,1)} %bitcast.56, ...), custom_call_target="tpu_custom_call" | custom-call | flops 99999997952 | bytes 100000000 | tf_op jit(solution)/shard_map/pallas_call | solution.py:1244
  477.7 1.3 slice.115
  479.7 1.3 slice.113
  481.6 1.5 slice_reduce_fusion
  483.2 2.4 convert_element_type.49
  488.6 1.4 slice_convert_fusion
  490.1 4.4 convert_element_type.46
  494.4 2.8 convert_element_type.48
  497.2 2.8 convert_element_type.53
  500.0 2.7 copy.55
  502.7 10.6 %copy.56 = f32[4,512,1536]{2,1,0:T(8,128)} copy(f32[4,512,1536]{2,1,0:T(8,128)} %bitcast.47) | data formatting | bytes 25165824
  (63 shorter events, 15.3 us)
Async XLA Ops:
  7.2 481.4 %all-reduce.7.cloned.1.call-start = ((), (), s32[]{:S(2)}) async-start(), calls=%async_computation | async-start | bytes 14942208 | tf_op jit(solution)/shard_map/psum | solution.py:1275
  229.8 34.3 %collective-permute-start.1 = (bf16[4,16,256]{2,1,0:T(8,128)(2,1)}, bf16[4,16,256]{2,1,0:T(8,128)(2,1)S(1)}, u32[]{:S(2)}, u32[]{:S(2)}) collective-permute-start(bf16[4,16,256]{2,1,0:T(8,128)(2,1)} %get-tuple-element.108), channel_id=1, source_target_pairs={{4,0},{8,4},{12,8},{16,12},{20,16},{24,20},{28,24},{5,1},{9,5},{13... | collective-permute-start | bytes 98312 | tf_op jit(solution)/shard_map/ppermute | solution.py:1223
  231.1 35.8 %collective-permute-start = (bf16[4,16,768]{2,1,0:T(8,128)(2,1)}, bf16[4,16,768]{2,1,0:T(8,128)(2,1)S(1)}, u32[]{:S(2)}, u32[]{:S(2)}) collective-permute-start(bf16[4,16,768]{2,1,0:T(8,128)(2,1)} %get-tuple-element.106), channel_id=1, source_target_pairs={{4,0},{8,4},{12,8},{16,12},{20,16},{24,20},{28,24},{5,1},{9,5},{13... | collective-permute-start | bytes 294920 | tf_op jit(solution)/shard_map/ppermute | solution.py:1223
  234.5 4.8 copy-start.7
  234.5 22.4 %slice-start.2 = ((s8[6291456]{0:T(1024)(128)(4,1)}), s8[4194304]{0:T(1024)(128)(4,1)S(1)}, s32[]{:S(2)}) async-start(s8[6291456]{0:T(1024)(128)(4,1)} %bitcast.60), calls=%async_computation.3 | async-start | bytes 8388608
  239.3 17.6 %slice-start.3 = ((s8[6291456]{0:T(1024)(128)(4,1)}), s8[2097152]{0:T(1024)(128)(4,1)S(1)}, s32[]{:S(2)}) async-start(s8[6291456]{0:T(1024)(128)(4,1)} %bitcast.60), calls=%async_computation.4 | async-start | bytes 4194304
  239.3 17.6 %copy-start.8 = (bf16[4,512,768]{2,1,0:T(8,128)(2,1)S(1)}, bf16[4,512,768]{2,1,0:T(8,128)(2,1)}, u32[]{:S(2)}) copy-start(bf16[4,512,768]{2,1,0:T(8,128)(2,1)} %get-tuple-element.121) | copy-start | bytes 9437188
  239.3 24.7 %slice-start.4 = ((s8[6291456]{0:T(1024)(128)(4,1)}), s8[4194304]{0:T(1024)(128)(4,1)S(1)}, s32[]{:S(2)}) async-start(s8[6291456]{0:T(1024)(128)(4,1)} %bitcast.65), calls=%async_computation.5 | async-start | bytes 8388608
  257.0 6.4 %copy-start.2 = (f32[8,768]{1,0:T(8,128)S(1)}, f32[8,768]{1,0:T(8,128)}, u32[]{:S(2)}) copy-start(f32[8,768]{1,0:T(8,128)} %get-tuple-element.111) | copy-start | bytes 73732
  257.0 7.1 %copy-start.5 = (bf16[4,512,256]{2,1,0:T(8,128)(2,1)S(1)}, bf16[4,512,256]{2,1,0:T(8,128)(2,1)}, u32[]{:S(2)}) copy-start(bf16[4,512,256]{2,1,0:T(8,128)(2,1)} %get-tuple-element.107) | copy-start | bytes 3145732
  257.0 7.1 %slice-start.5 = ((s8[6291456]{0:T(1024)(128)(4,1)}), s8[2097152]{0:T(1024)(128)(4,1)S(1)}, s32[]{:S(2)}) async-start(s8[6291456]{0:T(1024)(128)(4,1)} %bitcast.65), calls=%async_computation.6 | async-start | bytes 4194304
  264.1 2.7 copy-start.6
  264.1 2.7 copy-start.3
  266.9 6.5 %copy-start.4 = (bf16[4,512,768]{2,1,0:T(8,128)(2,1)}, bf16[4,512,768]{2,1,0:T(8,128)(2,1)S(1)}, u32[]{:S(2)}) copy-start(bf16[4,512,768]{2,1,0:T(8,128)(2,1)S(1)} %add_dynamic-update-slice_fusion) | copy-start | bytes 9437188
  273.4 214.0 %copy-start.9 = (f32[12]{0:T(128)S(1)}, f32[12]{0:T(128)}, u32[]{:S(2)}) copy-start(f32[12]{0:T(128)} %param.31) | copy-start | bytes 148
  490.1 4.4 copy-start.1
  490.1 10.0 %slice-start = ((s8[6291456]{0:T(1024)(128)(4,1)}), s8[4194304]{0:T(1024)(128)(4,1)S(1)}, s32[]{:S(2)}) async-start(s8[6291456]{0:T(1024)(128)(4,1)} %bitcast.48), calls=%async_computation.1 | async-start | bytes 8388608
  494.4 2.8 copy-start
  494.4 5.6 %slice-start.1 = ((s8[6291456]{0:T(1024)(128)(4,1)}), s8[2097152]{0:T(1024)(128)(4,1)S(1)}, s32[]{:S(2)}) async-start(s8[6291456]{0:T(1024)(128)(4,1)} %bitcast.48), calls=%async_computation.2 | async-start | bytes 4194304
Sparse Core Ops, SparseCore 0:
  273.5 127.8 all-reduce.6

commit v5 on v4

--- a/solution.py
+++ b/solution.py
@@ -182,13 +182,14 @@
 class Rider:
     def __init__(self, first, ticks, count, hbm, own, got, far, sems, local):
         self.first, self.ticks, self.count = first, ticks, count
-        self.base = max(first - 2 * LAG, 0)
+        self.done = min(max(first - 2 * LAG, 0), count)
+        self.base = min(self.done, count - 1)
         self.hbm, self.local = hbm, local
         self.chain = Chain(own, got, far, sems)
 
     @staticmethod
     def size(first, ticks, count):
-        return min(first + ticks, count) - max(first - 2 * LAG, 0)
+        return max(min(first + ticks, count) - min(max(first - 2 * LAG, 0), count - 1), 1)
 
     @staticmethod
     def scratch(first, ticks, count, width):
@@ -203,7 +204,7 @@
         own = pltpu.make_async_copy(self.hbm.at[pl.ds(self.base, size)], self.chain.own, self.local.at[0])
         own.start()
         ready = min(max(self.first - LAG, 0), self.count) - self.base
-        if ready > 0:
+        if ready > 0 and self.done < self.count:
 
             @pl.when(jnp.logical_not(self.chain.end))
             def _():
@@ -288,7 +289,7 @@
         @pl.when(middle)
         def _():
             reached = self.span(1)[1]
-            store(chain.got, self.base, reached)
+            store(chain.got, self.done, reached)
             store(chain.own, reached, self.span(0)[1])
 
         @pl.when(chain.end)
@@ -364,10 +365,6 @@
                 self.take(r, s)
                 if r + 1 < self.rounds:
                     self.push(r + 1, s)
-
-        @pl.when(i < seqs)
-        def _():
-            self.push(0, i)
 
     @staticmethod
     def scratch(rounds, seqs, n, inner):
@@ -470,6 +467,10 @@
         scan.begin(i, st[...], expand_row(run[0:1], wide[...]))
 
     scan.advance(i, seqs)
+
+    @pl.when(i < seqs)
+    def _():
+        scan.push(0, i)
 
     @pl.when(s >= 0)
     def _():
@@ -643,16 +644,19 @@
 
 
 def back_one(
-    xact, bcact, step_i, cum_i, gate, ssd, gn, sums, lstart, entry, pre, mgain, skip, wide, y_in,
-    gnormed_o, gate_grad_o, xg_o, cumg_o, stepg_o, bcg_o, lend_o, rms_o, mgg_o, skg_o, after_o, y_all,
-    z, acc, dys, use, total, logs, out, back, send, recv,
+    xact, bcact, cum_i, gate, ssd, gn, sums, pre, mgain, skip, wide,
+    xact_b, bcact_b, step_b, cum_b, lstart_b, entry_b, pre_b, y_in,
+    gnormed_o, gate_grad_o, lend_o, rms_o, xg_o, cumg_o, stepg_o, bcg_o, mgg_o, skg_o, after_o, y_all,
+    z, acc, use, dys, cumg, total, logs, out, back, send, recv,
     yown, ygot, yfar, ta, tb, tc, td, te, tf, ylocal,
     *, inner_all, seqs, rounds, plan,
 ):
     i = pl.program_id(0)
+    s = i - rounds
     blocks = xact.shape[1] // T
     scan = Exchange(rounds, True, total, after_o, logs, out, back, send, recv)
     rider = Rider(*plan, y_all, yown, ygot, yfar, (ta, tb, tc, td, te, tf), ylocal)
+    per_step = plan[1] // (seqs + rounds)
 
     @pl.when(i == 0)
     def _():
@@ -661,31 +665,45 @@
         mgg_o[...] = jnp.zeros_like(mgg_o)
         skg_o[...] = jnp.zeros_like(skg_o)
 
+    ticks = min(per_step, 3)
+    rider.tick(i * per_step)
+
     @pl.when(i < seqs)
     def _():
-        back_one_rows(
-            xact, bcact, step_i, cum_i, gate, ssd, gn, sums, lstart, entry, pre, mgain, skip, wide,
-            gnormed_o, gate_grad_o, xg_o, cumg_o, stepg_o, bcg_o, lend_o, rms_o, mgg_o, skg_o,
-            z, acc, dys, use, inner_all, lambda b: rider.tick(i * blocks + b),
+        one = pl.ds(i, 1)
+        gate_back(
+            xact, bcact, cum_i, gate, ssd, gn, sums, mgain, skip, wide, gnormed_o, gate_grad_o, lend_o, rms_o, mgg_o, skg_o,
+            dys.at[one], cumg.at[one], acc, use, inner_all,
         )
         scan.begin(i, acc[...], expand_row(pre[0, blocks : blocks + 1], wide[...]))
 
     scan.advance(i, seqs)
 
-    @pl.when(i >= seqs)
-    def _():
-        for k in (0, 1):
-            rider.tick(seqs * blocks + (i - seqs) * 2 + k)
+    @pl.when(i < seqs)
+    def _():
+        scan.push(0, i)
+
+    @pl.when(s >= 0)
+    def _():
+        one = pl.ds(s, 1)
+        scan_back(
+            xact_b, bcact_b, step_b, cum_b, lstart_b, entry_b, pre_b, skip, wide, dys.at[one], cumg.at[one],
+            xg_o, cumg_o, stepg_o, bcg_o, z, lambda b: rider.tick(jnp.where(1 + b < ticks, i * per_step + 1 + b, plan[1])),
+        )
+
+    @pl.when(s < 0)
+    def _():
+        for k in range(1, per_step):
+            rider.tick(i * per_step + k)
 
     @pl.when(i == seqs + rounds - 1)
     def _():
         rider.close()
 
 
-def back_one_rows(
-    xact, bcact, step_i, cum_i, gate, ssd, gn, sums, lstart, entry, pre, mgain, skip, wide,
-    gnormed_o, gate_grad_o, xg_o, cumg_o, stepg_o, bcg_o, lend_o, rms_o, mgg_o, skg_o,
-    z, acc, dys, use, inner_all, tick,
+def gate_back(
+    xact, bcact, cum_i, gate, ssd, gn, sums, mgain, skip, wide, gnormed_o, gate_grad_o, lend_o, rms_o, mgg_o, skg_o,
+    dys, cumg, acc, use, inner_all,
 ):
     length = xact.shape[1]
     blocks = length // T
@@ -693,9 +711,8 @@
     inner = xact.shape[2]
     acc[...] = jnp.zeros_like(acc)
 
-    def block(i, _):
-        tick(i)
-        b = blocks - 1 - i
+    def block(k, _):
+        b = blocks - 1 - k
         r = rows_of(b)
         sums_b = sums[0, :, r]
         columns = jnp.concatenate([sums_b, jnp.zeros((LANES - 8, T), F32)], axis=0).T
@@ -705,7 +722,8 @@
             rms = lax.rsqrt(columns[tile(i), 0:1] / inner_all + EPS)
             rms_o[0, ri, :] = jnp.broadcast_to(rms, (SUB, LANES))
             coef = rms * rms * rms * (columns[tile(i), 1:2] / inner_all)
-            mixed = ssd[0, ri, :] + skip[...] * xa
+            ssd_r = ssd[0, ri, :]
+            mixed = ssd_r + skip[...] * xa
             g = gate[0, ri, :]
             sg = sigmoid(g)
             gated = mixed * (g * sg)
@@ -717,19 +735,48 @@
             gate_grad_o[0, ri, :] = (grad_gated * mixed * (sg * (1.0 + g * (1.0 - sg)))).astype(BF16)
             grad_mixed = grad_gated * (g * sg)
             skg_o[0:1] += jnp.sum(grad_mixed * xa, axis=0, keepdims=True)
-            xg_o[0, ri, :] = skip[...] * grad_mixed
-            dys[tile(i)] = grad_mixed.astype(BF16)
-        dy = dys[...]
+            dy = grad_mixed.astype(BF16)
+            dys[0, ri, :] = dy
+            cumg[0, ri, :] = head_sum(dy.astype(F32) * ssd_r, wide[...])
+        cm = bcact[0, r, n:].astype(F32)
+        grown = jnp.exp(cum_i[0, r, :])
+        for p in range(inner // LANES):
+            lanes = slice(p * LANES, (p + 1) * LANES)
+            scaled = [(cm * grown[:, h : h + 1]).astype(BF16) for h in (2 * p, 2 * p + 1)]
+            used = None
+            for i in range(T // SUB):
+                ri = pl.ds(pl.multiple_of(b * T + i * SUB, SUB), SUB)
+                term = t_mm(jnp.concatenate([v[tile(i)] for v in scaled], axis=0), pair_rows(dys[0, ri, lanes]))
+                used = term if used is None else used + term
+            use[:, lanes] = used
+        lend_o[0, b] = acc[...]
+        acc[...] = expand_row(grown[T - 1 : T], wide[...]) * acc[...] + use[...]
+        return 0
+
+    lax.fori_loop(0, blocks, block, 0)
+
+
+def scan_back(
+    xact, bcact, step_i, cum_i, lstart, entry, pre, skip, wide, dys, cumg, xg_o, cumg_o, stepg_o, bcg_o, z, tick,
+):
+    length = xact.shape[1]
+    blocks = length // T
+    n = bcact.shape[2] // 2
+    inner = xact.shape[2]
+
+    def block(b, _):
+        tick(b)
+        r = rows_of(b)
+        dy = dys[0, r, :]
         xa = xact[0, r, :].astype(F32)
         bca = bcact[0, r, :]
         bm, cm = bca[:, :n], bca[:, n:]
-        cm32 = cm.astype(F32)
         cum = cum_i[0, r, :]
         cum_t = cum.T
-        grown = jnp.exp(cum)
         start = expand_row(jnp.exp(pre[0, pl.ds(b, 1), :]), wide[...]) * entry[0] + lstart[0, b]
         start = start.astype(BF16)
-        gdy_hi, gdy_lo = split(expand(grown, wide[...]) * dy.astype(F32), 2)
+        dy32 = dy.astype(F32)
+        gdy_hi, gdy_lo = split(expand(jnp.exp(cum), wide[...]) * dy32, 2)
         c_grad = mm_t(gdy_hi, start) + mm_t(gdy_lo, start)
         step_wide = expand(step_i[0, r, :], wide[...])
         xs = (xa * step_wide).astype(BF16)
@@ -737,28 +784,20 @@
         cross_part = {ij: jnp.zeros((SUB, SUB), F32) for ij in tiles()}
         for p in range(inner // LANES):
             lanes = slice(p * LANES, (p + 1) * LANES)
-            two = (2 * p, 2 * p + 1)
-            scaled = [(cm32 * grown[:, h : h + 1]).astype(BF16) for h in two]
-            used = None
             zs = [None] * (T // SUB)
             for i in range(T // SUB):
                 dy_two = pair_rows(dy[tile(i), lanes])
-                term = t_mm(jnp.concatenate([v[tile(i)] for v in scaled], axis=0), dy_two)
-                used = term if used is None else used + term
                 for j in range(i + 1):
                     mix_grad = mm_t(dy_two, xs[tile(j), lanes])
                     mix = []
-                    for k, h in enumerate(two):
+                    for k, h in enumerate((2 * p, 2 * p + 1)):
                         decay = decay_tile(cum, cum_t, h, i, j)
                         mix.append((cross[i, j] * decay).astype(BF16))
                         cross_part[i, j] = cross_part[i, j] + mix_grad[tile(k)] * decay
                     term = t_mm(jnp.concatenate(mix, axis=0), dy_two)
                     zs[j] = term if zs[j] is None else zs[j] + term
-            use[:, lanes] = used
             for j in range(T // SUB):
                 z[tile(j), lanes] = zs[j]
-        lend_o[0, b] = acc[...]
-        acc[...] = expand_row(grown[T - 1 : T], wide[...]) * acc[...] + use[...]
         rows = []
         for i in range(T // SUB):
             row = [jnp.where(lower(), cross_part[i, j], 0.0) if i == j else cross_part[i, j] for j in range(i + 1)]
@@ -768,8 +807,8 @@
         bcg_o[0, r, 0:n] = t_mm(cross_low, cm)
         bcg_o[0, r, n : 2 * n] = c_grad + mm(cross_low, bm)
         zz = z[...]
-        xg_o[0, r, :] = xg_o[0, r, :] + step_wide * zz
-        cumg_o[0, r, :] = head_sum(dy.astype(F32) * ssd[0, r, :] - xs.astype(F32) * zz, wide[...])
+        xg_o[0, r, :] = skip[...] * dy32 + step_wide * zz
+        cumg_o[0, r, :] = cumg[0, r, :] - head_sum(xs.astype(F32) * zz, wide[...])
         stepg_o[0, r, :] = head_sum(xa * zz, wide[...])
         return 0
 
@@ -818,8 +857,9 @@
             out[k : k + 1] += jnp.sum(grad * ext[r0 + base + k : r0 + base + k + T], axis=0, keepdims=True)
         out[taps : taps + 1] += jnp.sum(grad, axis=0, keepdims=True)
 
+    per_step = plan[1] // seqs
     for b in range(blocks):
-        rider.tick(step_at * blocks + b)
+        rider.tick(step_at * per_step + b)
         r0 = b * T
         r = slice(r0, r0 + T)
         xa = xact[0, r, :].astype(F32)
@@ -869,6 +909,8 @@
     xhalo_o[0] = conv_back(xcg, vk, 0, HALO)
     bhalo_o[0] = conv_back(bcg_s, sk, 0, HALO)
     for b in range(blocks):
+        if blocks + b < per_step:
+            rider.tick(step_at * per_step + blocks + b)
         r0 = b * T
         xpg_o[0, r0 : r0 + T] = conv_back(xcg, vk, HALO + r0, T)
         bpg_o[0, r0 : r0 + T] = conv_back(bcg_s, sk, HALO + r0, T)
@@ -878,123 +920,150 @@
         rider.close()
 
 
-class SmallSums:
-    def __init__(self, rounds, acc, out, back, zback, done, sems, vec, vback, vsems):
-        self.rounds = rounds
-        self.acc, self.out, self.back, self.zback, self.done, self.sems = acc, out, back, zback, done, sems
-        self.vec, self.vback, self.vsems = vec, vback, vsems
+class GradSum:
+    def __init__(self, rounds, mine, back, out, sems, zback=None, shared=0):
+        self.rounds, self.mine, self.back, self.out, self.sems = rounds, mine, back, out, sems
+        self.zback, self.shared = zback, shared
         self.me, self.z = lax.axis_index("seq"), lax.axis_index("head")
-        self.stages = 2 * rounds + 2
+        self.rows = mine.shape[0]
+        self.share = self.rows >> rounds
 
     @staticmethod
-    def scratch(rounds, rows, cols, vec_shape):
-        half = pltpu.VMEM((rounds, rows // 2, cols), BF16)
-        return [
-            pltpu.VMEM((rows, cols), F32), half, half, pltpu.VMEM((4, rows >> rounds, cols), BF16), pltpu.VMEM((rows, cols), BF16),
-            pltpu.SemaphoreType.DMA((4 * rounds + 8,)), pltpu.VMEM(vec_shape, F32), pltpu.VMEM((4,) + vec_shape, F32), pltpu.SemaphoreType.DMA((8,)),
-        ]
+    def sem_count(rounds):
+        return 4 * rounds + 9
+
+    def bit(self, r):
+        return lax.div(self.me, 1 << r) % 2
 
     def partner(self, r):
-        bit = 1 << r
-        return self.me + bit - 2 * bit * (lax.div(self.me, bit) % 2)
-
-    def start_of(self, r):
-        rows = self.acc.shape[0]
-        first = 0
+        return self.me + (1 << r) - (2 << r) * self.bit(r)
+
+    def first(self, r):
+        row = 0
         for k in range(r):
-            first = first + (lax.div(self.me, 1 << k) % 2) * (rows >> (k + 1))
-        return first, rows >> r
+            row = row + self.bit(k) * (self.rows >> (k + 1))
+        return row
+
+    def at(self, row, size):
+        return pl.ds(pl.multiple_of(row, 16), size)
 
     def halving(self, r):
-        size = self.acc.shape[0] >> (r + 1)
+        half = self.rows >> (r + 1)
+        theirs = self.first(r) + half - half * self.bit(r)
         return pltpu.make_async_remote_copy(
-            src_ref=self.out.at[r, pl.ds(0, size)], dst_ref=self.back.at[r, pl.ds(0, size)],
+            src_ref=self.mine.at[self.at(theirs, half)], dst_ref=self.back.at[pl.ds(self.rows - 2 * half, half)],
             send_sem=self.sems.at[r], recv_sem=self.sems.at[self.rounds + r],
             device_id={"seq": self.partner(r)}, device_id_type=MESH,
         )
 
-    def gathering(self, r, mine):
-        first, size = self.start_of(r + 1)
-        if not mine:
-            first = first + size - 2 * size * (lax.div(self.me, 1 << r) % 2)
-        at = pl.ds(pl.multiple_of(first, 16), size)
+    def add_half(self, r):
+        copy = self.halving(r)
+        copy.wait()
+        half = self.rows >> (r + 1)
+        row = self.first(r + 1)
+
+        def one(k, _):
+            at = self.at(row + k * self.share, self.share)
+            come = self.back[pl.ds(pl.multiple_of(self.rows - 2 * half + k * self.share, 16), self.share), :]
+            self.mine[at, :] = (self.mine[at, :].astype(F32) + come.astype(F32)).astype(BF16)
+            return 0
+
+        lax.fori_loop(0, half // self.share, one, 0)
+
+    def gathering(self, r, arriving):
+        size = self.rows >> (r + 1)
+        row = self.first(r + 1)
+        if arriving:
+            row = row + size - 2 * size * self.bit(r)
+        at = self.at(row, size)
         return pltpu.make_async_remote_copy(
-            src_ref=self.done.at[at], dst_ref=self.done.at[at],
+            src_ref=self.out.at[at], dst_ref=self.out.at[at],
             send_sem=self.sems.at[2 * self.rounds + r], recv_sem=self.sems.at[3 * self.rounds + r],
             device_id={"seq": self.partner(r)}, device_id_type=MESH,
         )
 
-    def to_head(self, d, vec):
-        src, dst, sems, base = (self.vec, self.vback, self.vsems, 0) if vec else (self.share(), self.zback, self.sems, 4 * self.rounds)
+    def to_head(self, d):
+        base = 4 * self.rounds + 1
+        src = self.mine.at[self.at(self.first(self.rounds), self.share), pl.ds(0, self.shared)]
         return pltpu.make_async_remote_copy(
-            src_ref=src, dst_ref=dst.at[self.z], send_sem=sems.at[base + d], recv_sem=sems.at[base + 4 + d],
+            src_ref=src, dst_ref=self.zback.at[self.z], send_sem=self.sems.at[base + d], recv_sem=self.sems.at[base + 4 + d],
             device_id={"head": lax.rem(self.z + d, 4)}, device_id_type=MESH,
         )
 
-    def share(self):
-        first, size = self.start_of(self.rounds)
-        return self.done.at[pl.ds(pl.multiple_of(first, 16), size)]
-
-    def push_half(self, r):
-        first, size = self.start_of(r)
-        half = size // 2
-        theirs = first + half - half * (lax.div(self.me, 1 << r) % 2)
-        self.out[r, pl.ds(0, half), :] = self.acc[pl.ds(pl.multiple_of(theirs, 16), half), :].astype(BF16)
-        self.halving(r).start()
-
-    def stage(self, k):
-        rounds = self.rounds
-        if k == 0:
-            for d in range(1, 4):
-                self.to_head(d, True).start()
-            self.vback[self.z] = self.vec[...]
-        if 0 < k <= rounds:
-            r = k - 1
-            copy = self.halving(r)
-            copy.wait()
-            first, size = self.start_of(r + 1)
-            at = pl.ds(pl.multiple_of(first, 16), size)
-            self.acc[at, :] = self.acc[at, :] + self.back[r, pl.ds(0, size), :].astype(F32)
-        if k < rounds:
-            self.push_half(k)
-        if k == rounds:
-            first, size = self.start_of(rounds)
-            at = pl.ds(pl.multiple_of(first, 16), size)
-            self.done[at, :] = self.acc[at, :].astype(BF16)
-            for d in range(1, 4):
-                self.to_head(d, False).start()
-            self.zback[self.z] = self.done[at, :]
-        if k == rounds + 1:
-            for d in range(1, 4):
-                self.to_head(d, False).wait()
-                self.to_head(d, True).wait()
-            first, size = self.start_of(rounds)
-            at = pl.ds(pl.multiple_of(first, 16), size)
-            total = self.zback[0].astype(F32)
-            vec = self.vback[0]
-            for d in range(1, 4):
-                total = total + self.zback[d].astype(F32)
-                vec = vec + self.vback[d]
-            self.done[at, :] = total.astype(BF16)
-            self.vec[...] = vec
-            self.gathering(rounds - 1, True).start()
-        if k > rounds + 1:
-            r = rounds - 1 - (k - rounds - 2)
-            self.gathering(r, True).wait_send()
-            self.gathering(r, False).wait_recv()
-            if r > 0:
-                self.gathering(r - 1, True).start()
+    def publish(self):
+        at = self.at(self.first(self.rounds), self.share)
+        copy = pltpu.make_async_copy(self.mine.at[at], self.out.at[at], self.sems.at[4 * self.rounds])
+        copy.start()
+        copy.wait()
+        self.gathering(self.rounds - 1, False).start()
+
+    def stages(self):
+        spans = [2, 5, 3] + [2] * self.rounds
+        acts = [(spans[0], lambda: self.halving(0).start())]
+        for r in range(self.rounds):
+            def act(r=r):
+                self.add_half(r)
+                if r + 1 < self.rounds:
+                    self.halving(r + 1).start()
+                elif not self.shared:
+                    self.publish()
+                else:
+                    for d in range(1, 4):
+                        self.to_head(d).start()
+                    self.zback[self.z] = self.mine[self.at(self.first(self.rounds), self.share), 0 : self.shared]
+
+            acts.append((spans[r + 1] if r + 1 < self.rounds else spans[r], act))
+        if self.shared:
+            def meet():
+                for d in range(1, 4):
+                    self.to_head(d).wait()
+                at = self.at(self.first(self.rounds), self.share)
+                low = [self.zback[k].astype(F32) for k in range(4)]
+                self.mine[at, 0 : self.shared] = ((low[0] + low[1]) + (low[2] + low[3])).astype(BF16)
+                self.publish()
+
+            acts.append((spans[self.rounds - 1], meet))
+        for r in reversed(range(self.rounds)):
+            def act(r=r):
+                self.gathering(r, False).wait_send()
+                self.gathering(r, True).wait_recv()
+                if r > 0:
+                    self.gathering(r - 1, False).start()
+
+            acts.append((spans[max(r - 1, 0)], act))
+        return acts
 
 
 def finish(
-    y, gate_grad, xpg, bpg, raw, tok, cot, rms, gate_w, value_w, state_w, step_w, ngain, small, state_grad, state_rows, y_all,
-    result_o, tokens_grad_o, small_o, state_o,
+    y, gate_grad, xpg, bpg, raw, tok, cot, rms, gate_w, value_w, state_w, step_w, ngain, small, state_rows,
+    normed, tok_k, out_grad, gate_grad_w, y_all,
+    result_o, tokens_grad_o, small_o, wout_o, wgate_o, wvalue_o, wmixed_o,
     own, got, far, sa, sb, sc, sd, se, sf, yown, ygot, yfar, ta, tb, tc, td, te, tf, ylocal, rows, out, back, send, recv,
-    s_acc, s_out, s_back, s_zback, s_done, s_sems, s_vec, s_vback, s_vsems,
+    w_mine, w_back, m_mine, m_back, m_zback, w_acc, m_acc, w_sems, w_local, vec, vback, vsems,
     *, n, rounds, plan,
 ):
     i = pl.program_id(0)
-    sums = SmallSums(rounds, s_acc, s_out, s_back, s_zback, s_done, s_sems, s_vec, s_vback, s_vsems)
+    z = lax.axis_index("head")
+    last = n + 3 * LAG - 1
+    outs = (wout_o, wgate_o, wvalue_o)
+    grads = [GradSum(rounds, w_mine.at[k], w_back.at[k], outs[k], w_sems.at[k]) for k in range(3)]
+    grads.append(GradSum(rounds, m_mine, m_back, wmixed_o, w_sems.at[3], m_zback, bpg.shape[1]))
+    products = 2 * (n * CHUNK // T)
+
+    def vec_copy(d):
+        return pltpu.make_async_remote_copy(
+            src_ref=vec, dst_ref=vback.at[z], send_sem=vsems.at[d], recv_sem=vsems.at[4 + d],
+            device_id={"head": lax.rem(z + d, 4)}, device_id_type=MESH,
+        )
+
+    def local_copies():
+        rows_out, half = out_grad.shape[0], out_grad.shape[1] // 2
+        return [
+            pltpu.make_async_copy(gate_grad_w, w_mine.at[1], w_local.at[0]),
+            pltpu.make_async_copy(out_grad.at[:, pl.ds(0, half)], w_mine.at[0, pl.ds(0, rows_out)], w_local.at[1]),
+            pltpu.make_async_copy(out_grad.at[:, pl.ds(half, half)], w_mine.at[0, pl.ds(rows_out, rows_out)], w_local.at[2]),
+        ]
+
     chain = Chain(own, got, far, (sa, sb, sc, sd, se, sf))
     rider = Rider(*plan, y_all, yown, ygot, yfar, (ta, tb, tc, td, te, tf), ylocal)
     me = lax.axis_index("seq")
@@ -1011,10 +1080,13 @@
         greet_head()
         pl.semaphore_wait(barrier, rounds + 3)
         rider.load()
-        s_acc[...] = state_grad[...].astype(F32)
-        s_vec[...] = state_rows[...]
+        for copy in local_copies():
+            copy.start()
+        w_acc[...] = jnp.zeros_like(w_acc)
+        m_acc[...] = jnp.zeros_like(m_acc)
         rows[0:8] = small[...]
         rows[8:] = jnp.zeros_like(rows[8:])
+        rows[16:24, 0 : state_rows.shape[1]] = state_rows[...]
 
     rider.tick(i)
     for stage in (2, 1):
@@ -1024,17 +1096,76 @@
         def _():
             chain.onward(stage, k)
 
+    @pl.when((i < products) & (i % 2 == 0))
+    def _():
+        value = mm_t(gate_grad[...], gate_w[...]) + mm_t(xpg[...], value_w[...])
+        value = value + (mm_t(bpg[...], state_w[...]) + mm_t(raw[...], step_w[...]))
+        t = tok_k[...].astype(F32)
+        inv = lax.rsqrt(jnp.mean(t * t, axis=1, keepdims=True) + EPS)
+        gain = jnp.sum(value * (t * inv), axis=0, keepdims=True)
+        half = t.shape[1] // 2
+        rows[8:9] += gain[:, :half]
+        rows[9:10] += gain[:, half:]
+        chunks = T // CHUNK
+        first = lax.div(i, 2) * chunks
+        own[pl.ds(first, chunks)] = value.astype(BF16).reshape(chunks, CHUNK, value.shape[1])
+        mixed = jnp.concatenate([bpg[...], raw[...]], axis=1)
+        for m in range(w_acc.shape[0] // 256):
+            rows_m = slice(m * 256, (m + 1) * 256)
+            part = normed[:, rows_m]
+            w_acc[rows_m] += t_mm(part, xpg[...])
+            m_acc[rows_m] += t_mm(part, mixed)
+
     @pl.when(i < n)
     def _():
-        value = mm_t(gate_grad[...], gate_w[...]) + mm_t(xpg[...], value_w[...])
-        own[i] = (value + (mm_t(bpg[...], state_w[...]) + mm_t(raw[...], step_w[...]))).astype(BF16)
         chain.inward(i)
 
-    for stage in range(sums.stages):
-
-        @pl.when(i == 1 + 2 * stage)
-        def _():
-            sums.stage(stage)
+    @pl.when(i == products)
+    def _():
+        w_mine[2] = w_acc[...].astype(BF16)
+        m_mine[...] = m_acc[...].astype(BF16)
+
+    @pl.when(i == 1)
+    def _():
+        for copy in local_copies():
+            copy.wait()
+
+    for grad_sum, begin in zip(grads, (1, 5, products, products + 2)):
+        at = begin
+        for span, act in grad_sum.stages():
+            pl.when(i == min(at, last))(act)
+            at += span
+
+    @pl.when(i == products)
+    def _():
+        vec[...] = rows[8:24]
+        for d in range(1, 4):
+            vec_copy(d).start()
+        vback[z] = vec[...]
+
+    def row_copy(r):
+        return pltpu.make_async_remote_copy(
+            src_ref=out.at[r], dst_ref=back.at[r], send_sem=send.at[r], recv_sem=recv.at[r],
+            device_id={"seq": partner(r)}, device_id_type=MESH,
+        )
+
+    @pl.when(i == products + 4)
+    def _():
+        for d in range(1, 4):
+            vec_copy(d).wait()
+        rows[8:24] = (vback[0] + vback[1]) + (vback[2] + vback[3])
+        out[0] = rows[...]
+        row_copy(0).start()
+
+    for r in range(rounds):
+
+        @pl.when(i == products + 4 + 3 * (r + 1))
+        def _():
+            row_copy(r).wait()
+            rows[...] = rows[...] + back[r]
+            if r + 1 < rounds:
+                out[r + 1] = rows[...]
+                row_copy(r + 1).start()
 
     k = i - 3 * LAG
 
@@ -1045,52 +1176,41 @@
         t = tok[...].astype(F32)
         width = t.shape[1]
         inv = lax.rsqrt(jnp.mean(t * t, axis=1, keepdims=True) + EPS)
-        if rider.base > 0:
-
-            @pl.when(k < rider.base)
+        if rider.done > 0:
+
+            @pl.when(k < rider.done)
             def _():
                 result_o[...] = (t + y[...].astype(F32) * rms_k).astype(BF16)
 
-        @pl.when(k >= rider.base)
-        def _():
-            result_o[...] = (t + rider.chain.total(k - rider.base) * rms_k).astype(BF16)
+        if rider.done < n:
+
+            @pl.when(k >= rider.done)
+            def _():
+                result_o[...] = (t + rider.chain.total(k - rider.base) * rms_k).astype(BF16)
 
         scaled = grad * ngain[...]
         dot = jnp.sum(scaled * t, axis=1, keepdims=True) / width
-        tokens_grad_o[...] = cot[...].astype(F32) + inv * scaled - t * (inv * inv * inv * dot)
-        gain = jnp.sum(grad * t * inv, axis=0, keepdims=True)
-        half = width // 2
-        rows[8:9] += gain[:, :half]
-        rows[9:10] += gain[:, half:]
-
-    @pl.when(i == n + 3 * LAG - 1)
+        tokens_grad_o[...] = (cot[...].astype(F32) + inv * scaled - t * (inv * inv * inv * dot)).astype(BF16)
+
+    @pl.when(i == last)
     def _():
         chain.drain(n)
         rider.drain()
-        rows[16:24, 0 : s_vec.shape[1]] = s_vec[...]
-        for r in range(rounds):
-            copy = pltpu.make_async_remote_copy(
-                src_ref=out.at[r], dst_ref=back.at[r], send_sem=send.at[r], recv_sem=recv.at[r],
-                device_id={"seq": partner(r)}, device_id_type=MESH,
-            )
-            out[r] = rows[...]
-            copy.start()
-            copy.wait()
-            rows[...] = rows[...] + back[r]
-        state_o[...] = s_done[...]
         small_o[...] = rows[...]
 
 
 def call(body, steps, seqs, ins, outs, scratch, flops, collective_id=None, carried=None):
-    def cut(shape):
+    def cut(shape, lag):
         rest = tuple(shape[1:])
-        return pl.BlockSpec((1,) + rest, lambda s: (jnp.minimum(s, seqs - 1),) + (0,) * len(rest))
+        return pl.BlockSpec((1,) + rest, lambda s: (jnp.clip(s - lag, 0, seqs - 1),) + (0,) * len(rest))
 
     def whole(shape):
-        return pl.BlockSpec(tuple(shape), lambda s: (0,) * len(shape))
-
-    in_specs = [cut(a.shape) if a.ndim >= 3 else whole(a.shape) for a in ins]
-    out_specs = [cut(s) if c else whole(s) for s, _, c in outs]
+        return pl.BlockSpec(tuple(shape), lambda s: (0,) * len(shape), pipeline_mode=pl.Buffered(1))
+
+    pairs = [v if isinstance(v, tuple) else (v, 0) for v in ins]
+    ins = [v for v, _ in pairs]
+    in_specs = [cut(v.shape, lag) if v.ndim >= 3 else whole(v.shape) for v, lag in pairs]
+    out_specs = [whole(s) if lag is None else cut(s, lag) for s, _, lag in outs]
     out_shape = [jax.ShapeDtypeStruct(s, d) for s, d, _ in outs]
     aliases = {}
     if carried is not None:
@@ -1151,8 +1271,8 @@
     tri = (jnp.arange(T)[:, None] >= jnp.arange(T)[None, :]).astype(BF16)
     vo, so = value_offset[None], state_offset[None]
 
-    def big(cols, dtype, rows=length):
-        return ((seqs, rows, cols), dtype, True)
+    def big(cols, dtype, rows=length, lag=0):
+        return ((seqs, rows, cols), dtype, lag)
 
     vmem = pltpu.VMEM
     ext = length + HALO
@@ -1197,24 +1317,26 @@
         ),
         cost_estimate=pl.CostEstimate(flops=2 * flat * width * 4 * inner, bytes_accessed=10**8, transcendentals=0),
     )(tokens, tokens, cotangent, *fixed)
-    plan = (plan[1], seqs * blocks + 2 * rounds, n_chunks)
-    gnormed, gate_grad, xg, cumg, stepg, bcg, lend, rms, mgg, skg, after, y = call(
+    plan = (plan[1], 2 * (seqs + rounds), n_chunks)
+    gnormed, gate_grad, lend, rms, xg, cumg, stepg, bcg, mgg, skg, after, y = call(
         functools.partial(back_one, inner_all=inner_all, seqs=seqs, rounds=rounds, plan=plan), seqs + rounds, seqs,
-        [xact, bcact, step, cum, gate, ssd, gn, sums, lstart, entry, pre, gain, skip, wide],
-        [big(inner, BF16), big(inner, BF16), big(inner, F32), big(LANES, F32), big(LANES, F32), big(n2, F32),
-         ((seqs, blocks, n, inner), F32, True), big(LANES, F32),
-         ((8, inner), F32, False), ((8, inner), F32, False), ((seqs, n, inner), F32, False)],
-        [vmem((T, inner), F32), vmem((n, inner), F32), vmem((T, inner), BF16), vmem((n, inner), F32)]
+        [xact, bcact, cum, gate, ssd, gn, sums, pre, gain, skip, wide]
+        + [(v, rounds) for v in (xact, bcact, step, cum, lstart, entry, pre)],
+        [big(inner, BF16), big(inner, BF16), ((seqs, blocks, n, inner), F32, 0), big(LANES, F32),
+         big(inner, F32, lag=rounds), big(LANES, F32, lag=rounds), big(LANES, F32, lag=rounds), big(n2, F32, lag=rounds),
+         ((8, inner), F32, None), ((8, inner), F32, None), ((seqs, n, inner), F32, None)],
+        [vmem((T, inner), F32), vmem((n, inner), F32), vmem((n, inner), F32), vmem((seqs, length, inner), BF16),
+         vmem((seqs, length, LANES), F32)]
         + Exchange.scratch(rounds, seqs, n, inner) + Rider.scratch(*plan, width),
         2 * flat * T * inner * 8, 3, y,
     )
-    plan = (plan[0] + plan[1], seqs * blocks, n_chunks)
+    plan = (plan[0] + plan[1], 3 * seqs, n_chunks)
     xpg, xhalo, bpg, bhalo, raw, vkg, skgr, head_rows, y = call(
         functools.partial(back_two, seqs=seqs, plan=plan), seqs, seqs,
         [xact, bcact, xext, bcext, step, cum, sraw, xg, cumg, stepg, bcg, lstart, entry, lend, after, pre,
          value_kernel, vo, state_kernel, so, bias, rate, wide, tri],
         [big(inner, BF16), big(inner, BF16, HALO), big(n2, BF16), big(n2, BF16, HALO), big(LANES, BF16),
-         ((8, inner), F32, False), ((8, n2), F32, False), ((8, LANES), F32, False)],
+         ((8, inner), F32, None), ((8, n2), F32, None), ((8, LANES), F32, None)],
         [vmem((ext, inner), F32), vmem((ext, n2), F32), vmem((ext + HALO, inner), F32),
          vmem((ext + HALO, n2), F32)] + Rider.scratch(*plan, width),
         2 * flat * T * inner * 4, 5, y,
@@ -1230,52 +1352,57 @@
     normed_f, xpg_f, bpg_f, raw_f, gg_f = [flatten(v) for v in (normed, xpg, bpg, raw, gate_grad)]
     out_weight_grad = t_mm(flatten(gnormed), flatten(cotangent)).astype(BF16)
     gate_weight_grad = t_mm(normed_f, gg_f).astype(BF16)
-    value_weight_grad = t_mm(normed_f, xpg_f).astype(BF16)
-    state_weight_grad = t_mm(normed_f, bpg_f).astype(BF16)
-    step_weight_grad = t_mm(normed_f, raw_f).astype(BF16)
     head_row = jnp.pad(head_rows[:2].reshape(1, 2 * LANES), ((0, 0), (0, inner - 2 * LANES)))
     small = jnp.concatenate([vkg[: taps + 1], mgg[:1], skg[:1], head_row], axis=0)
-    plan = (plan[0] + plan[1], n_chunks - plan[0] - plan[1] + 3 * LAG, n_chunks)
+    first = min(plan[0] + plan[1], n_chunks + 2 * LAG)
+    plan = (first, max(n_chunks - first, 0) + 3 * LAG, n_chunks)
+
+    def product_rows(v):
+        return pl.BlockSpec((T, v.shape[1]), lambda i: (jnp.minimum(i // 2, flat // T - 1), 0))
 
     def lagged(cols, lag):
         return pl.BlockSpec((CHUNK, cols), lambda i: (jnp.clip(i - lag, 0, n_chunks - 1), 0))
 
-    late = (gate_weight, value_weight, state_weight, step_w, norm_gain[None], small, state_weight_grad, skgr)
-    result, tokens_grad, small, state_weight_grad = pl.pallas_call(
+    late = (gate_weight, value_weight, state_weight, step_w, norm_gain[None], small, skgr)
+    result, tokens_grad, small, wout, wgate, wvalue, wmixed = pl.pallas_call(
         functools.partial(finish, n=n_chunks, rounds=rounds, plan=plan),
         grid=(n_chunks + 3 * LAG,),
         in_specs=[lagged(width, 3 * LAG)]
-        + [lagged(v.shape[1], 0) for v in (gg_f, xpg_f, bpg_f, raw_f)]
+        + [product_rows(v) for v in (gg_f, xpg_f, bpg_f, raw_f)]
         + [lagged(width, 3 * LAG), lagged(width, 3 * LAG), lagged(LANES, 3 * LAG)]
-        + [once(v) for v in late] + [pl.BlockSpec(memory_space=pl.ANY)],
+        + [once(v) for v in late] + [product_rows(normed_f), product_rows(flatten(tokens))] + [anywhere] * 3,
         out_specs=[lagged(width, 3 * LAG), lagged(width, 3 * LAG), pl.BlockSpec((24, inner), lambda i: (0, 0)),
-                   once(state_weight_grad)],
+                   anywhere, anywhere, anywhere, anywhere],
         out_shape=[
-            jax.ShapeDtypeStruct((flat, width), BF16), jax.ShapeDtypeStruct((flat, width), F32),
-            jax.ShapeDtypeStruct((24, inner), F32), jax.ShapeDtypeStruct(state_weight_grad.shape, BF16),
+            jax.ShapeDtypeStruct((flat, width), BF16), jax.ShapeDtypeStruct((flat, width), BF16),
+            jax.ShapeDtypeStruct((24, inner), F32), *[jax.ShapeDtypeStruct((width, c), BF16) for c in (inner, inner, inner, n2 + LANES)],
         ],
         scratch_shapes=Chain.scratch(n_chunks, CHUNK, width) + Rider.scratch(*plan, width) + [
             vmem((24, inner), F32), vmem((rounds, 24, inner), F32), vmem((rounds, 24, inner), F32),
             pltpu.SemaphoreType.DMA((rounds,)), pltpu.SemaphoreType.DMA((rounds,)),
-        ] + SmallSums.scratch(rounds, width, n2, skgr.shape),
+
+            vmem((3, width, inner), BF16), vmem((3, width, inner), BF16), vmem((width, n2 + LANES), BF16),
+            vmem((width, n2 + LANES), BF16), vmem((4, width >> rounds, n2), BF16), vmem((width, inner), F32),
+            vmem((width, n2 + LANES), F32), dma((4, GradSum.sem_count(rounds))), dma((3,)),
+            vmem((16, inner), F32), vmem((4, 16, inner), F32), dma((8,)),
+        ],
         compiler_params=pltpu.CompilerParams(
             dimension_semantics=("arbitrary",), vmem_limit_bytes=62 * 1024 * 1024, collective_id=4, has_side_effects=True
         ),
         cost_estimate=pl.CostEstimate(flops=10**11, bytes_accessed=10**8, transcendentals=0),
     )(y.reshape(flat, width), gg_f, xpg_f, bpg_f, raw_f, flatten(tokens), flatten(cotangent), flatten(rms),
-      *late, y)
-    result, tokens_grad = result.reshape(tokens.shape), tokens_grad.reshape(tokens.shape)
+      *late, normed_f, flatten(tokens), out_weight_grad, gate_weight_grad, y)
+    result, tokens_grad = result.reshape(tokens.shape), tokens_grad.reshape(tokens.shape).astype(F32)
     vkg, mixer_gain_grad, skg, head_row = small[: taps + 1], small[taps + 1], small[taps + 2], small[taps + 3]
     norm_gain_grad = small[8:10].reshape(width)
     skgr = small[16:24, :n2]
     skip_gain_grad = jnp.sum(skg.reshape(heads, head_size), axis=1)
     step_bias_grad = head_row[:heads]
     log_rate_grad = head_row[LANES : LANES + heads] * rate_row
-    out_weight_grad = lax.psum(out_weight_grad, "seq").astype(F32)
-    gate_weight_grad = lax.psum(gate_weight_grad, "seq").astype(F32)
-    value_weight_grad = lax.psum(value_weight_grad, "seq").astype(F32)
-    step_weight_grad = lax.psum(step_weight_grad, "seq")[:, :heads].astype(F32)
-    state_weight_grad = state_weight_grad.astype(F32)
+    out_weight_grad = jnp.concatenate([wout[:inner], wout[inner:]], axis=1).astype(F32)
+    gate_weight_grad, value_weight_grad = wgate.astype(F32), wvalue.astype(F32)
+    state_weight_grad = wmixed[:, :n2].astype(F32)
+    step_weight_grad = wmixed[:, n2 : n2 + heads].astype(F32)
     return (
         result, tokens_grad, norm_gain_grad, gate_weight_grad, value_weight_grad, state_weight_grad,
         step_weight_grad, vkg[:taps], vkg[taps], skgr[:taps], skgr[taps], step_bias_grad, log_rate_grad,

time: 525 us -> 482 us (0.918)
  matrix products: 38 us -> 16 us
  Pallas kernels: 415 us -> 399 us
  between operations: 14.5 us -> 1.04 us
  other arithmetic: 18.5 us -> 27.3 us
    pallas_call x1, Pallas kernels: 203 us -> 178 us  [shards(): pl.pallas_call(functools.partial(finish, n=n_chunks, rounds=rounds, plan=...]
    dot_general x5 -> x2, matrix products: 38 us -> 16 us  [t_mm(): lax.dot_general(a, b, (((0,), (0,)), ((), ())), preferred_element_type=F32)]
    pallas_call x2, Pallas kernels: 130 us -> 139 us  [call(): pl.pallas_call(body, grid=(steps,), in_specs=in_specs, out_specs=out_spec...]
    unnamed x35 -> x19, local copies, waits for them, and re-layouts: 14.4 us -> 7.89 us
    convert_element_type x5 -> x6, other arithmetic: 13.8 us -> 19.7 us  [the longest x1 6.56 us: shards(): tokens_grad.reshape(tokens.shape).astype(F32)]
  transfers between devices with their start and end apart: 3 -> 2, of which waited for: 0 -> 0; matrix products, arithmetic and copies ran while one was open for 9% -> 4% of each run, Pallas kernels for 39% -> 0%
where the time goes in v5:
time: 482 us; the launch traced here: 473 us
  Pallas kernels  399 us (83%)
  other arithmetic  27.3 us (6%)
  local copies, waits for them, and re-layouts  27.2 us (6%)
  matrix products  16 us (3%)
    pallas_call x1, Pallas kernels, shards(): pl.pallas_call(functools.partial(finish, n=n_chunks, rounds=rounds, plan=...  178 us
    pallas_call x2, Pallas kernels, call(): pl.pallas_call(body, grid=(steps,), in_specs=in_specs, out_specs=out_spec...  139 us
    pallas_call x1, Pallas kernels, shards(): pl.pallas_call(functools.partial(forward, seqs=seqs, rounds=rounds, plan=...  82 us
    dot_general x2, matrix products, t_mm(): lax.dot_general(a, b, (((0,), (0,)), ((), ())), preferred_element_type=F32)  16 us
  transfers between devices with their start and end apart: 2, of which 0 were waited for; matrix products, arithmetic and copies ran while one was open for 4% of the time, Pallas kernels for 0%

profile of v5, /device:TPU:0, one launch (start us, length us, event | category | flops | bytes accessed | tf_op | source)
XLA Modules:
  0.0 473.0 jit_solution(9679995624758835981)
XLA Ops:
  2.0 1.3 broadcast_in_dim.27.vo
  3.3 1.3 broadcast_in_dim.31.mgain
  4.5 1.3 broadcast_in_dim.26.ngain
  11.1 82.0 %shard_map.279 = (bf16[4,528,768]{2,1,0:T(8,128)(2,1)}, bf16[4,528,256]{2,1,0:T(8,128)(2,1)}, f32[4,512,128]{2,1,0:T(8,128)}, f32[4,8,128]{2,1,0:T(8,128)}, f32[...) custom-call(bf16[4,512,1536]{2,1,0:T(8,128)(2,1)} %tok_all.1, ...), custom_call_target="tpu_custom_call" | custom-call | flops 19327352832 | bytes 100000000 | tf_op jit(solution)/shard_map/pallas_call | solution.py:1297
  93.1 75.7 %shard_map.280 = (bf16[4,512,768]{2,1,0:T(8,128)(2,1)}, bf16[4,512,768]{2,1,0:T(8,128)(2,1)}, f32[4,2,128,768]{3,2,1,0:T(8,128)}, f32[4,512,128]{2,1,0:T(8,128)}...) custom-call(bf16[4,512,768]{2,1,0:T(8,128)(2,1)} %get-tuple-element., ...), custom_call_target="tpu_custom_call", output_to_operand_aliasing={{11}: (18, {})} | custom-call | flops 6442450944 | bytes 64509952 | tf_op jit(solution)/shard_map/pallas_call | solution.py:1228
  168.8 63.4 %shard_map.281 = (bf16[4,512,768]{2,1,0:T(8,128)(2,1)}, bf16[4,16,768]{2,1,0:T(8,128)(2,1)}, bf16[4,512,256]{2,1,0:T(8,128)(2,1)}, bf16[4,16,256]{2,1,0:T(8,128)...) custom-call(bf16[4,512,768]{2,1,0:T(8,128)(2,1)} %get-tuple-element., ...), custom_call_target="tpu_custom_call", output_to_operand_aliasing={{8}: (24, {})} | custom-call | flops 3221225472 | bytes 43328512 | tf_op jit(solution)/shard_map/pallas_call | solution.py:1228
  232.3 1.3 collective-permute-start.1
  233.6 1.3 collective-permute-start
  237.0 9.5 %bitcast_convert_fusion.1.out_grad = bf16[768,1536]{1,0:T(8,128)(2,1)} fusion(bf16[4,512,768]{2,1,0:T(8,128)(2,1)S(1)} %copy-done.3, bf16[4,512,1536]{2,1,0:T(8,128)(2,1)} %cot.1), kind=kOutput, calls=%fused_computation.1 | convolution fusion | flops 4833017856 | bytes 11796480 | tf_op jit(solution)/shard_map/dot_general | solution.py:28
  246.5 6.5 %bitcast_convert_fusion.gate_grad_w = bf16[1536,768]{1,0:T(8,128)(2,1)} fusion(bf16[4,512,1536]{2,1,0:T(8,128)(2,1)S(1)} %copy-done.5, bf16[4,512,768]{2,1,0:T(8,128)(2,1)S(1)} %copy-done.2), kind=kOutput, calls=%fused_computation | convolution fusion | flops 4833017856 | bytes 11796480 | tf_op jit(solution)/shard_map/dot_general | solution.py:28
  253.7 1.4 add_dynamic-update-slice_fusion.1
  255.1 1.6 add_dynamic-update-slice_fusion
  256.6 177.8 %shard_map.282 = (bf16[2048,1536]{1,0:T(8,128)(2,1)}, bf16[2048,1536]{1,0:T(8,128)(2,1)}, f32[24,768]{1,0:T(8,128)}, bf16[1536,768]{1,0:T(8,128)(2,1)}, bf16[153...) custom-call(bf16[2048,1536]{1,0:T(8,128)(2,1)} %bitcast.32, bf16[2048,768]{1,0:T(8,128)(2,1)} %bitcast.47, ...), custom_call_target="tpu_custom_call" | custom-call | flops 99999997952 | bytes 100000000 | tf_op jit(solution)/shard_map/pallas_call | solution.py:1367
  436.9 1.3 slice.126
  438.1 1.3 slice.125
  440.2 1.3 slice.123
  441.5 1.5 slice_reduce_fusion
  444.0 2.4 slice_convert_fusion
  448.0 1.9 fusion.4
  450.0 4.4 convert_element_type.45
  454.3 2.5 convert_element_type.46
  456.9 6.6 %convert.2 = f32[4,512,1536]{2,1,0:T(8,128)} convert(bf16[4,512,1536]{2,1,0:T(8,128)(2,1)S(1)} %bitcast.36) | non-fusion elementwise | flops 3145728 | bytes 18874368 | tf_op jit(solution)/shard_map/convert_element_type | solution.py:1395
  464.1 2.8 maximum_convert_fusion
  466.9 5.9 %copy.45 = bf16[4,512,1536]{2,1,0:T(8,128)(2,1)} copy(bf16[4,512,1536]{2,1,0:T(8,128)(2,1)} %bitcast.33) | data formatting | bytes 12582912
  (41 shorter events, 15.8 us)
Async XLA Ops:
  168.8 68.2 %copy-start.3 = (bf16[4,512,768]{2,1,0:T(8,128)(2,1)S(1)}, bf16[4,512,768]{2,1,0:T(8,128)(2,1)}, u32[]{:S(2)}) copy-start(bf16[4,512,768]{2,1,0:T(8,128)(2,1)} %get-tuple-element.120) | copy-start | bytes 9437188
  232.3 21.4 %collective-permute-start.1 = (bf16[4,16,256]{2,1,0:T(8,128)(2,1)}, bf16[4,16,256]{2,1,0:T(8,128)(2,1)S(1)}, u32[]{:S(2)}, u32[]{:S(2)}) collective-permute-start(bf16[4,16,256]{2,1,0:T(8,128)(2,1)} %get-tuple-element.111), channel_id=1, source_target_pairs={{4,0},{8,4},{12,8},{16,12},{20,16},{24,20},{28,24},{5,1},{9,5},{13... | collective-permute-start | bytes 98312 | tf_op jit(solution)/shard_map/ppermute | solution.py:1345
  233.6 21.5 %collective-permute-start = (bf16[4,16,768]{2,1,0:T(8,128)(2,1)}, bf16[4,16,768]{2,1,0:T(8,128)(2,1)S(1)}, u32[]{:S(2)}, u32[]{:S(2)}) collective-permute-start(bf16[4,16,768]{2,1,0:T(8,128)(2,1)} %get-tuple-element.109), channel_id=1, source_target_pairs={{4,0},{8,4},{12,8},{16,12},{20,16},{24,20},{28,24},{5,1},{9,5},{13... | collective-permute-start | bytes 294920 | tf_op jit(solution)/shard_map/ppermute | solution.py:1345
  237.0 9.5 %copy-start.2 = (bf16[4,512,768]{2,1,0:T(8,128)(2,1)S(1)}, bf16[4,512,768]{2,1,0:T(8,128)(2,1)}, u32[]{:S(2)}) copy-start(bf16[4,512,768]{2,1,0:T(8,128)(2,1)} %get-tuple-element.107) | copy-start | bytes 9437188
  237.0 9.5 %copy-start.5 = (bf16[4,512,1536]{2,1,0:T(8,128)(2,1)S(1)}, bf16[4,512,1536]{2,1,0:T(8,128)(2,1)}, u32[]{:S(2)}) copy-start(bf16[4,512,1536]{2,1,0:T(8,128)(2,1)} %get-tuple-element.119) | copy-start | bytes 18874372
  246.5 6.5 %copy-start.1 = (f32[8,768]{1,0:T(8,128)S(1)}, f32[8,768]{1,0:T(8,128)}, u32[]{:S(2)}) copy-start(f32[8,768]{1,0:T(8,128)} %get-tuple-element.114) | copy-start | bytes 73732
  256.6 177.8 %copy-start.4 = (f32[12]{0:T(128)S(1)}, f32[12]{0:T(128)}, u32[]{:S(2)}) copy-start(f32[12]{0:T(128)} %param.31) | copy-start | bytes 148
  448.0 8.9 %slice-start = ((s8[6291456]{0:T(1024)(128)(4,1)}), s8[4194304]{0:T(1024)(128)(4,1)S(1)}, s32[]{:S(2)}) async-start(s8[6291456]{0:T(1024)(128)(4,1)} %bitcast.34), calls=%async_computation | async-start | bytes 8388608
  449.9 4.4 copy-start
  449.9 6.9 %slice-start.1 = ((s8[6291456]{0:T(1024)(128)(4,1)}), s8[2097152]{0:T(1024)(128)(4,1)S(1)}, s32[]{:S(2)}) async-start(s8[6291456]{0:T(1024)(128)(4,1)} %bitcast.34), calls=%async_computation.1 | async-start | bytes 4194304

commit v6 on v5

--- a/solution.py
+++ b/solution.py
@@ -375,6 +375,14 @@
         ]
 
 
+class Row:
+    def __init__(self, ref):
+        self.ref = ref
+
+    def __getitem__(self, _):
+        return self.ref[...].reshape(1, self.ref.shape[0])
+
+
 def forward(
     tok, tok_all, cot, ngain, gate_w, value_w, state_w, step_w, vk, vo, sk, so, sbias, rate, wide, tri, out_w, mgain, skip,
     xext_o, bcext_o, sraw_o, pre_o, entry_o, sums_o,
@@ -385,6 +393,7 @@
     yown, ygot, yfar, ta, tb, tc, td, te, tf, ylocal,
     *, seqs, rounds, plan,
 ):
+    ngain, vo, so, mgain = Row(ngain), Row(vo), Row(so), Row(mgain)
     i = pl.program_id(0)
     s = i - rounds
     steps = seqs + rounds
@@ -651,6 +660,7 @@
     yown, ygot, yfar, ta, tb, tc, td, te, tf, ylocal,
     *, inner_all, seqs, rounds, plan,
 ):
+    mgain = Row(mgain)
     i = pl.program_id(0)
     s = i - rounds
     blocks = xact.shape[1] // T
@@ -817,9 +827,9 @@
 
 def back_two(
     xact, bcact, xext, bcext, step_i, cum_i, sraw, xg, cumg, stepg, bcg, lstart, entry, lend, after, pre,
-    vk, vo, sk, so, sbias, rate, wide, tri, y_in,
-    xpg_o, xhalo_o, bpg_o, bhalo_o, raw_o, vkg_o, skg_o, heads_o, y_all,
-    xe, be, xcg, bcg_s, yown, ygot, yfar, ta, tb, tc, td, te, tf, ylocal,
+    gnormed, cot, normed, gate_grad, vk, vo, sk, so, sbias, rate, wide, tri, y_in,
+    xpg_o, xhalo_o, bpg_o, bhalo_o, raw_o, vkg_o, skg_o, heads_o, wout_o, wgate_o, y_all,
+    xe, be, xcg, bcg_s, out_acc, gate_acc, yown, ygot, yfar, ta, tb, tc, td, te, tf, ylocal,
     *, seqs, plan,
 ):
     length = xact.shape[1]
@@ -827,6 +837,7 @@
     n = bcact.shape[2] // 2
     taps = vk.shape[0]
     base = HALO - taps + 1
+    vo, so = Row(vo), Row(so)
     step_at = pl.program_id(0)
     rider = Rider(*plan, y_all, yown, ygot, yfar, (ta, tb, tc, td, te, tf), ylocal)
 
@@ -835,6 +846,8 @@
         greet_head()
         pl.semaphore_wait(pltpu.get_barrier_semaphore(), 3)
         rider.load()
+        out_acc[...] = jnp.zeros_like(out_acc)
+        gate_acc[...] = jnp.zeros_like(gate_acc)
         vkg_o[...] = jnp.zeros_like(vkg_o)
         skg_o[...] = jnp.zeros_like(skg_o)
         heads_o[...] = jnp.zeros_like(heads_o)
@@ -906,6 +919,11 @@
             total = total + kernel[k : k + 1] * ref[r0 + taps - 1 - k : r0 + taps - 1 - k + rows]
         return total.astype(BF16)
 
+    for acc, left, right in ((out_acc, gnormed, cot), (gate_acc, normed, gate_grad)):
+        for m in range(acc.shape[0] // 256):
+            at = slice(m * 256, (m + 1) * 256)
+            acc[at] += t_mm(left[0, :, at], right[0])
+
     xhalo_o[0] = conv_back(xcg, vk, 0, HALO)
     bhalo_o[0] = conv_back(bcg_s, sk, 0, HALO)
     for b in range(blocks):
@@ -917,6 +935,8 @@
 
     @pl.when(step_at == seqs - 1)
     def _():
+        wout_o[...] = out_acc[...].astype(BF16)
+        wgate_o[...] = gate_acc[...].astype(BF16)
         rider.close()
 
 
@@ -1035,14 +1055,15 @@
 
 
 def finish(
-    y, gate_grad, xpg, bpg, raw, tok, cot, rms, gate_w, value_w, state_w, step_w, ngain, small, state_rows,
+    y, gate_grad, xpg, bpg, raw, tok, cot, rms, gate_w, value_w, state_w, step_w, ngain, filter_rows, gain_rows, skip_rows, head_rows, state_rows, xtail, btail,
     normed, tok_k, out_grad, gate_grad_w, y_all,
     result_o, tokens_grad_o, small_o, wout_o, wgate_o, wvalue_o, wmixed_o,
     own, got, far, sa, sb, sc, sd, se, sf, yown, ygot, yfar, ta, tb, tc, td, te, tf, ylocal, rows, out, back, send, recv,
     w_mine, w_back, m_mine, m_back, m_zback, w_acc, m_acc, w_sems, w_local, vec, vback, vsems,
-    *, n, rounds, plan,
+    *, n, rounds, plan, per_seq,
 ):
     i = pl.program_id(0)
+    ngain = Row(ngain)
     z = lax.axis_index("head")
     last = n + 3 * LAG - 1
     outs = (wout_o, wgate_o, wvalue_o)
@@ -1084,8 +1105,12 @@
             copy.start()
         w_acc[...] = jnp.zeros_like(w_acc)
         m_acc[...] = jnp.zeros_like(m_acc)
-        rows[0:8] = small[...]
-        rows[8:] = jnp.zeros_like(rows[8:])
+        rows[...] = jnp.zeros_like(rows)
+        rows[0:5] = filter_rows[0:5]
+        rows[5:6] = gain_rows[0:1]
+        rows[6:7] = skip_rows[0:1]
+        rows[7:8, 0:LANES] = head_rows[0:1]
+        rows[7:8, LANES : 2 * LANES] = head_rows[1:2]
         rows[16:24, 0 : state_rows.shape[1]] = state_rows[...]
 
     rider.tick(i)
@@ -1098,8 +1123,15 @@
 
     @pl.when((i < products) & (i % 2 == 0))
     def _():
-        value = mm_t(gate_grad[...], gate_w[...]) + mm_t(xpg[...], value_w[...])
-        value = value + (mm_t(bpg[...], state_w[...]) + mm_t(raw[...], step_w[...]))
+        part = lax.div(i, 2)
+        ends = lax.rem(part, per_seq) == per_seq - 1
+        tails = [jnp.where(ends, v[lax.div(part, per_seq)].astype(F32), 0.0) for v in (xtail, btail)]
+        x_rows, b_rows = [
+            jnp.concatenate([v[0 : T - HALO], (v[T - HALO : T].astype(F32) + tail).astype(BF16)], axis=0)
+            for v, tail in zip((xpg, bpg), tails)
+        ]
+        value = mm_t(gate_grad[...], gate_w[...]) + mm_t(x_rows, value_w[...])
+        value = value + (mm_t(b_rows, state_w[...]) + mm_t(raw[...], step_w[...]))
         t = tok_k[...].astype(F32)
         inv = lax.rsqrt(jnp.mean(t * t, axis=1, keepdims=True) + EPS)
         gain = jnp.sum(value * (t * inv), axis=0, keepdims=True)
@@ -1109,12 +1141,12 @@
         chunks = T // CHUNK
         first = lax.div(i, 2) * chunks
         own[pl.ds(first, chunks)] = value.astype(BF16).reshape(chunks, CHUNK, value.shape[1])
-        mixed = jnp.concatenate([bpg[...], raw[...]], axis=1)
+        mixed = jnp.concatenate([b_rows, raw[...]], axis=1)
         for m in range(w_acc.shape[0] // 256):
             rows_m = slice(m * 256, (m + 1) * 256)
-            part = normed[:, rows_m]
-            w_acc[rows_m] += t_mm(part, xpg[...])
-            m_acc[rows_m] += t_mm(part, mixed)
+            left = normed[:, rows_m]
+            w_acc[rows_m] += t_mm(left, x_rows)
+            m_acc[rows_m] += t_mm(left, mixed)
 
     @pl.when(i < n)
     def _():
@@ -1197,6 +1229,36 @@
         chain.drain(n)
         rider.drain()
         small_o[...] = rows[...]
+
+
+def unpack(
+    tgrad, res, wout_l, wout_r, wgate, wvalue, wmixed, small, rate, wide,
+    res_o, tgrad_o, ngain_o, wgate_o, wvalue_o, state_o, step_o, vk_o, vo_o, sk_o, so_o, sbias_o, rate_o, skip_o, mgain_o, wout_o,
+    *, taps, heads,
+):
+    res_o[...] = res[...]
+    tgrad_o[...] = tgrad[...].astype(F32)
+    wgate_o[...] = wgate[...].astype(F32)
+    wvalue_o[...] = wvalue[...].astype(F32)
+    half = wout_l.shape[1]
+    wout_o[:, :half] = wout_l[...].astype(F32)
+    wout_o[:, half:] = wout_r[...].astype(F32)
+    n2 = state_o.shape[1]
+    state_o[...] = wmixed[:, :n2].astype(F32)
+    step_o[...] = wmixed[:, n2 : n2 + heads].astype(F32)
+
+    @pl.when(pl.program_id(0) == 0)
+    def _():
+        vk_o[...] = small[0:taps]
+        vo_o[...] = small[taps]
+        mgain_o[...] = small[taps + 1]
+        skip_o[...] = head_sum(jnp.broadcast_to(small[taps + 2 : taps + 3], (16, half)), wide[...])[0, 0:heads]
+        sbias_o[...] = small[taps + 3, 0:heads]
+        rate_o[...] = small[taps + 3, LANES : LANES + heads] * rate[0, 0:heads]
+        ngain_o[pl.ds(0, half)] = small[8]
+        ngain_o[pl.ds(half, half)] = small[9]
+        sk_o[...] = small[16 : 16 + taps, 0:n2]
+        so_o[...] = small[16 + taps, 0:n2]
 
 
 def call(body, steps, seqs, ins, outs, scratch, flops, collective_id=None, carried=None):
@@ -1256,7 +1318,7 @@
     blocks = length // T
     devices = lax.axis_size("seq")
     rounds = devices.bit_length() - 1
-    assert devices == 1 << rounds
+    assert devices == 1 << rounds and taps == 4
     inner_all = inner * lax.axis_size("head")
 
     pad = LANES - heads
@@ -1265,11 +1327,11 @@
     bias = jnp.pad(step_bias, (0, pad))[None]
     step_w = jnp.pad(step_weight, ((0, 0), (0, pad)))
     skip = jnp.repeat(skip_gain, head_size)[None]
-    gain = mixer_gain[None]
+    gain = mixer_gain
     one = (jnp.arange(inner)[None, :] // head_size == jnp.arange(LANES)[:, None]).astype(BF16)
     wide = jnp.concatenate([one, one], axis=0)
     tri = (jnp.arange(T)[:, None] >= jnp.arange(T)[None, :]).astype(BF16)
-    vo, so = value_offset[None], state_offset[None]
+    vo, so = value_offset, state_offset
 
     def big(cols, dtype, rows=length, lag=0):
         return ((seqs, rows, cols), dtype, lag)
@@ -1290,7 +1352,7 @@
     def shape_of(cols, dtype, rows=length):
         return jax.ShapeDtypeStruct((seqs, rows, cols), dtype)
 
-    fixed = (norm_gain[None], gate_weight, value_weight, state_weight, step_w, value_kernel, vo, state_kernel, so, bias, rate,
+    fixed = (norm_gain, gate_weight, value_weight, state_weight, step_w, value_kernel, vo, state_kernel, so, bias, rate,
              wide, tri, out_weight, gain, skip)
     held = (shape_of(LANES, F32, 8), shape_of(inner, F32, n), shape_of(length, F32, 8))
     anywhere = pl.BlockSpec(memory_space=pl.ANY)
@@ -1331,29 +1393,23 @@
         2 * flat * T * inner * 8, 3, y,
     )
     plan = (plan[0] + plan[1], 3 * seqs, n_chunks)
-    xpg, xhalo, bpg, bhalo, raw, vkg, skgr, head_rows, y = call(
+    xpg, xhalo, bpg, bhalo, raw, vkg, skgr, head_rows, out_weight_grad, gate_weight_grad, y = call(
         functools.partial(back_two, seqs=seqs, plan=plan), seqs, seqs,
         [xact, bcact, xext, bcext, step, cum, sraw, xg, cumg, stepg, bcg, lstart, entry, lend, after, pre,
-         value_kernel, vo, state_kernel, so, bias, rate, wide, tri],
+         gnormed, cotangent, normed, gate_grad, value_kernel, vo, state_kernel, so, bias, rate, wide, tri],
         [big(inner, BF16), big(inner, BF16, HALO), big(n2, BF16), big(n2, BF16, HALO), big(LANES, BF16),
-         ((8, inner), F32, None), ((8, n2), F32, None), ((8, LANES), F32, None)],
+         ((8, inner), F32, None), ((8, n2), F32, None), ((8, LANES), F32, None),
+         ((inner, width), BF16, None), ((width, inner), BF16, None)],
         [vmem((ext, inner), F32), vmem((ext, n2), F32), vmem((ext + HALO, inner), F32),
-         vmem((ext + HALO, n2), F32)] + Rider.scratch(*plan, width),
+         vmem((ext + HALO, n2), F32), vmem((inner, width), F32), vmem((width, inner), F32)] + Rider.scratch(*plan, width),
         2 * flat * T * inner * 4, 5, y,
     )
     back = [(i + 1, i) for i in range(devices - 1)]
     xhalo, bhalo = lax.ppermute((xhalo, bhalo), "seq", back)
-    xpg = xpg.at[:, length - HALO :].add(xhalo)
-    bpg = bpg.at[:, length - HALO :].add(bhalo)
-
     def flatten(v):
         return v.reshape(flat, v.shape[-1])
 
     normed_f, xpg_f, bpg_f, raw_f, gg_f = [flatten(v) for v in (normed, xpg, bpg, raw, gate_grad)]
-    out_weight_grad = t_mm(flatten(gnormed), flatten(cotangent)).astype(BF16)
-    gate_weight_grad = t_mm(normed_f, gg_f).astype(BF16)
-    head_row = jnp.pad(head_rows[:2].reshape(1, 2 * LANES), ((0, 0), (0, inner - 2 * LANES)))
-    small = jnp.concatenate([vkg[: taps + 1], mgg[:1], skg[:1], head_row], axis=0)
     first = min(plan[0] + plan[1], n_chunks + 2 * LAG)
     plan = (first, max(n_chunks - first, 0) + 3 * LAG, n_chunks)
 
@@ -1363,9 +1419,9 @@
     def lagged(cols, lag):
         return pl.BlockSpec((CHUNK, cols), lambda i: (jnp.clip(i - lag, 0, n_chunks - 1), 0))
 
-    late = (gate_weight, value_weight, state_weight, step_w, norm_gain[None], small, skgr)
+    late = (gate_weight, value_weight, state_weight, step_w, norm_gain, vkg, mgg, skg, head_rows, skgr, xhalo, bhalo)
     result, tokens_grad, small, wout, wgate, wvalue, wmixed = pl.pallas_call(
-        functools.partial(finish, n=n_chunks, rounds=rounds, plan=plan),
+        functools.partial(finish, n=n_chunks, rounds=rounds, plan=plan, per_seq=blocks),
         grid=(n_chunks + 3 * LAG,),
         in_specs=[lagged(width, 3 * LAG)]
         + [product_rows(v) for v in (gg_f, xpg_f, bpg_f, raw_f)]
@@ -1392,22 +1448,31 @@
         cost_estimate=pl.CostEstimate(flops=10**11, bytes_accessed=10**8, transcendentals=0),
     )(y.reshape(flat, width), gg_f, xpg_f, bpg_f, raw_f, flatten(tokens), flatten(cotangent), flatten(rms),
       *late, normed_f, flatten(tokens), out_weight_grad, gate_weight_grad, y)
-    result, tokens_grad = result.reshape(tokens.shape), tokens_grad.reshape(tokens.shape).astype(F32)
-    vkg, mixer_gain_grad, skg, head_row = small[: taps + 1], small[taps + 1], small[taps + 2], small[taps + 3]
-    norm_gain_grad = small[8:10].reshape(width)
-    skgr = small[16:24, :n2]
-    skip_gain_grad = jnp.sum(skg.reshape(heads, head_size), axis=1)
-    step_bias_grad = head_row[:heads]
-    log_rate_grad = head_row[LANES : LANES + heads] * rate_row
-    out_weight_grad = jnp.concatenate([wout[:inner], wout[inner:]], axis=1).astype(F32)
-    gate_weight_grad, value_weight_grad = wgate.astype(F32), wvalue.astype(F32)
-    state_weight_grad = wmixed[:, :n2].astype(F32)
-    step_weight_grad = wmixed[:, n2 : n2 + heads].astype(F32)
-    return (
-        result, tokens_grad, norm_gain_grad, gate_weight_grad, value_weight_grad, state_weight_grad,
-        step_weight_grad, vkg[:taps], vkg[taps], skgr[:taps], skgr[taps], step_bias_grad, log_rate_grad,
-        skip_gain_grad, mixer_gain_grad, out_weight_grad,
-    )
+    parts = 16
+
+    def strip(rows, cols, at=0):
+        return pl.BlockSpec((rows // parts, cols), lambda i: (i + at, 0))
+
+    def entire(shape):
+        return pl.BlockSpec(shape, lambda i: (0,) * len(shape))
+
+    fine = [strip(inner, inner), strip(inner, inner, parts)]
+    flat_out = [
+        ((flat, width), BF16), ((flat, width), F32), ((width,), F32), ((width, inner), F32), ((width, inner), F32), ((width, n2), F32),
+        ((width, heads), F32), ((taps, inner), F32), ((inner,), F32), ((taps, n2), F32), ((n2,), F32), ((heads,), F32), ((heads,), F32),
+        ((heads,), F32), ((inner,), F32), ((inner, width), F32),
+    ]
+    cut = (0, 1, 3, 4, 5, 6, 15)
+    found = pl.pallas_call(
+        functools.partial(unpack, taps=taps, heads=heads),
+        grid=(parts,),
+        in_specs=[strip(flat, width), strip(flat, width)] + fine + [strip(width, inner)] * 2 + [strip(width, n2 + LANES)]
+        + [entire(small.shape), entire(rate.shape), entire(wide.shape)],
+        out_specs=[strip(*shape) if k in cut else entire(shape) for k, (shape, _) in enumerate(flat_out)],
+        out_shape=[jax.ShapeDtypeStruct(shape, dtype) for shape, dtype in flat_out],
+        compiler_params=pltpu.CompilerParams(dimension_semantics=("arbitrary",), vmem_limit_bytes=60 * 1024 * 1024),
+    )(tokens_grad, result, wout, wout, wgate, wvalue, wmixed, small, rate, wide)
+    return (found[0].reshape(tokens.shape), found[1].reshape(tokens.shape)) + tuple(found[2:])
 
 
 def solution(mesh):

time: 482 us -> 443 us (0.919); the launches traced: 473 us -> 442 us
  Pallas kernels: 399 us -> 427 us
  other arithmetic: 27.3 us -> 2.16 us
  local copies, waits for them, and re-layouts: 27.2 us -> 7.12 us
  matrix products: 16 us -> 0 us
    pallas_call x0 -> x1, Pallas kernels: none -> 22.1 us  [shards(): pl.pallas_call(functools.partial(unpack, taps=taps, heads=heads), grid=(p...]
    convert_element_type x6 -> x0, other arithmetic: 19.7 us -> none  [the longest x1 6.56 us: shards(): tokens_grad.reshape(tokens.shape).astype(F32)]
    dot_general x2 -> x0, matrix products: 16 us -> none  [t_mm(): lax.dot_general(a, b, (((0,), (0,)), ((), ())), preferred_element_type=F32)]
    slice x10 -> x0, local copies, waits for them, and re-layouts: 11.4 us -> none  [the longest x1 1.93 us: shards(): wout[:inner]]
  transfers between devices with their start and end apart: 2 -> 2, of which waited for: 0 -> 1; matrix products, arithmetic and copies ran while one was open for 4% -> 0% of each run, Pallas kernels for 0% -> 0%
where the time goes in v6:
time: 443 us; the launch traced here: 442 us
  Pallas kernels  427 us (96%)
  local copies, waits for them, and re-layouts  7.12 us (2%)
    pallas_call x1, Pallas kernels, shards(): pl.pallas_call(functools.partial(finish, n=n_chunks, rounds=rounds, plan=...  180 us
    pallas_call x2, Pallas kernels, call(): pl.pallas_call(body, grid=(steps,), in_specs=in_specs, out_specs=out_spec...  143 us
    pallas_call x1, Pallas kernels, shards(): pl.pallas_call(functools.partial(forward, seqs=seqs, rounds=rounds, plan=...  82 us
    pallas_call x1, Pallas kernels, shards(): pl.pallas_call(functools.partial(unpack, taps=taps, heads=heads), grid=(p...  22.1 us
  transfers between devices with their start and end apart: 2, of which 1 were waited for; matrix products, arithmetic and copies ran while one was open for 0% of the time, Pallas kernels for 0%

profile of v6, /device:TPU:0, one launch (start us, length us, event | category | flops | bytes accessed | tf_op | source)
XLA Modules:
  0.0 442.3 jit_solution(3394044744508470150)
XLA Ops:
  0.7 0.7 fusion.tri
  1.3 0.7 exponential_negate_fusion
  2.0 0.7 broadcast_in_dim.15
  2.7 0.7 broadcast_in_dim_reshape.3.skip
  3.4 0.1 iota_compare_fusion
  3.4 0.8 add_convert_fusion.wide
  4.2 1.0 copy.34
  5.3 1.2 pad_bitcast_fusion
  6.4 0.8 pad.11.step_w
  7.3 82.0 %shard_map.279 = (bf16[4,528,768]{2,1,0:T(8,128)(2,1)}, bf16[4,528,256]{2,1,0:T(8,128)(2,1)}, f32[4,512,128]{2,1,0:T(8,128)}, f32[4,8,128]{2,1,0:T(8,128)}, f32[...) custom-call(bf16[4,512,1536]{2,1,0:T(8,128)(2,1)} %tok_all.1, ...), custom_call_target="tpu_custom_call" | custom-call | flops 19327352832 | bytes 100000000 | tf_op jit(solution)/shard_map/pallas_call | solution.py:1359
  89.3 75.4 %shard_map.280 = (bf16[4,512,768]{2,1,0:T(8,128)(2,1)}, bf16[4,512,768]{2,1,0:T(8,128)(2,1)}, f32[4,2,128,768]{3,2,1,0:T(8,128)}, f32[4,512,128]{2,1,0:T(8,128)}...) custom-call(bf16[4,512,768]{2,1,0:T(8,128)(2,1)} %get-tuple-element., ...), custom_call_target="tpu_custom_call", output_to_operand_aliasing={{11}: (18, {})} | custom-call | flops 6442450944 | bytes 64509952 | tf_op jit(solution)/shard_map/pallas_call | solution.py:1290
  164.6 68.1 %shard_map.281 = (bf16[4,512,768]{2,1,0:T(8,128)(2,1)}, bf16[4,16,768]{2,1,0:T(8,128)(2,1)}, bf16[4,512,256]{2,1,0:T(8,128)(2,1)}, bf16[4,16,256]{2,1,0:T(8,128)...) custom-call(bf16[4,512,768]{2,1,0:T(8,128)(2,1)} %get-tuple-element., ...), custom_call_target="tpu_custom_call", output_to_operand_aliasing={{10}: (28, {})} | custom-call | flops 3221225472 | bytes 66921472 | tf_op jit(solution)/shard_map/pallas_call | solution.py:1290
  232.7 1.3 collective-permute-start
  234.0 1.3 collective-permute-start.1
  235.3 2.6 collective-permute-done.1.btail
  237.9 0.0 copy-start.1
  237.9 0.0 collective-permute-done.xtail
  237.9 0.0 copy-start
  238.0 0.6 copy-done.1
  238.6 0.0 copy-done
  238.6 179.6 %shard_map.282 = (bf16[2048,1536]{1,0:T(8,128)(2,1)}, bf16[2048,1536]{1,0:T(8,128)(2,1)}, f32[24,768]{1,0:T(8,128)}, bf16[1536,768]{1,0:T(8,128)(2,1)}, bf16[153...) custom-call(bf16[2048,1536]{1,0:T(8,128)(2,1)} %bitcast.15, bf16[2048,768]{1,0:T(8,128)(2,1)} %bitcast.18, ...), custom_call_target="tpu_custom_call" | custom-call | flops 99999997952 | bytes 100000000 | tf_op jit(solution)/shard_map/pallas_call | solution.py:1423
  418.2 22.1 %shard_map.283 = (bf16[2048,1536]{1,0:T(8,128)(2,1)}, f32[2048,1536]{1,0:T(8,128)}, f32[1536]{0:T(1024)}, f32[1536,768]{1,0:T(8,128)}, f32[1536,768]{1,0:T(8,128...) custom-call(bf16[2048,1536]{1,0:T(8,128)(2,1)} %get-tuple-element.11, ...), custom_call_target="tpu_custom_call" | custom-call | tf_op jit(solution)/shard_map/pallas_call | solution.py:1466
  440.3 2.0 copy.35
  (1 shorter events, 0.0 us)
Async XLA Ops:
  232.7 5.2 %collective-permute-start = (bf16[4,16,768]{2,1,0:T(8,128)(2,1)}, bf16[4,16,768]{2,1,0:T(8,128)(2,1)S(1)}, u32[]{:S(2)}, u32[]{:S(2)}) collective-permute-start(bf16[4,16,768]{2,1,0:T(8,128)(2,1)} %get-tuple-element.113), channel_id=1, source_target_pairs={{4,0},{8,4},{12,8},{16,12},{20,16},{24,20},{28,24},{5,1},{9,5},{13... | collective-permute-start | bytes 294920 | tf_op jit(solution)/shard_map/ppermute | solution.py:1408
  234.0 3.9 collective-permute-start.1
  237.9 0.6 copy-start.1
  237.9 0.6 copy-start

commit v7 on v6

--- a/solution.py
+++ b/solution.py
@@ -1055,21 +1055,32 @@
 
 
 def finish(
-    y, gate_grad, xpg, bpg, raw, tok, cot, rms, gate_w, value_w, state_w, step_w, ngain, filter_rows, gain_rows, skip_rows, head_rows, state_rows, xtail, btail,
+    y, gate_grad, xpg, bpg, raw, tok, cot, rms, gate_w, value_w, state_w, step_w, ngain, filter_rows, gain_rows, skip_rows, head_rows, state_rows, xhalo, bhalo,
     normed, tok_k, out_grad, gate_grad_w, y_all,
     result_o, tokens_grad_o, small_o, wout_o, wgate_o, wvalue_o, wmixed_o,
     own, got, far, sa, sb, sc, sd, se, sf, yown, ygot, yfar, ta, tb, tc, td, te, tf, ylocal, rows, out, back, send, recv,
-    w_mine, w_back, m_mine, m_back, m_zback, w_acc, m_acc, w_sems, w_local, vec, vback, vsems,
+    w_mine, w_back, m_mine, m_back, m_zback, w_acc, m_acc, w_sems, w_local, vec, vback, vsems, xtail, btail, halo_sems, xnow, bnow,
     *, n, rounds, plan, per_seq,
 ):
     i = pl.program_id(0)
     ngain = Row(ngain)
-    z = lax.axis_index("head")
+    z, me = lax.axis_index("head"), lax.axis_index("seq")
     last = n + 3 * LAG - 1
     outs = (wout_o, wgate_o, wvalue_o)
     grads = [GradSum(rounds, w_mine.at[k], w_back.at[k], outs[k], w_sems.at[k]) for k in range(3)]
     grads.append(GradSum(rounds, m_mine, m_back, wmixed_o, w_sems.at[3], m_zback, bpg.shape[1]))
-    products = 2 * (n * CHUNK // T)
+    products = n * CHUNK // T
+
+    devices = lax.axis_size("seq")
+
+    def halo_copies():
+        return [
+            pltpu.make_async_remote_copy(
+                src_ref=src, dst_ref=dst, send_sem=halo_sems.at[k], recv_sem=halo_sems.at[2 + k],
+                device_id={"seq": lax.rem(me + devices - 1, devices)}, device_id_type=MESH,
+            )
+            for k, (src, dst) in enumerate(((xhalo, xtail), (bhalo, btail)))
+        ]
 
     def vec_copy(d):
         return pltpu.make_async_remote_copy(
@@ -1096,10 +1107,21 @@
     @pl.when(i == 0)
     def _():
         barrier = pltpu.get_barrier_semaphore()
-        for r in range(rounds):
-            pl.semaphore_signal(barrier, inc=1, device_id={"seq": partner(r)}, device_id_type=MESH)
+        for d in range(1, devices):
+            pl.semaphore_signal(barrier, inc=1, device_id={"seq": lax.rem(me + d, devices)}, device_id_type=MESH)
         greet_head()
-        pl.semaphore_wait(barrier, rounds + 3)
+        pl.semaphore_wait(barrier, devices - 1 + 3)
+
+        @pl.when(me > 0)
+        def _():
+            for copy in halo_copies():
+                copy.start()
+
+        @pl.when(me == devices - 1)
+        def _():
+            xtail[...] = jnp.zeros_like(xtail)
+            btail[...] = jnp.zeros_like(btail)
+
         rider.load()
         for copy in local_copies():
             copy.start()
@@ -1121,26 +1143,50 @@
         def _():
             chain.onward(stage, k)
 
-    @pl.when((i < products) & (i % 2 == 0))
-    def _():
-        part = lax.div(i, 2)
-        ends = lax.rem(part, per_seq) == per_seq - 1
-        tails = [jnp.where(ends, v[lax.div(part, per_seq)].astype(F32), 0.0) for v in (xtail, btail)]
-        x_rows, b_rows = [
-            jnp.concatenate([v[0 : T - HALO], (v[T - HALO : T].astype(F32) + tail).astype(BF16)], axis=0)
-            for v, tail in zip((xpg, bpg), tails)
+    def with_tails():
+        return [
+            jnp.concatenate([v[0 : T - HALO], (v[T - HALO : T].astype(F32) + tail[...]).astype(BF16)], axis=0)
+            for v, tail in ((xpg, xnow), (bpg, bnow))
         ]
+
+    @pl.when((i == per_seq - 1) & (me < devices - 1))
+    def _():
+        for copy in halo_copies():
+            copy.wait_recv()
+
+    ends = lax.rem(i, per_seq) == per_seq - 1
+
+    @pl.when((i < products) & ends)
+    def _():
+        xnow[...] = xtail[lax.div(i, per_seq)].astype(F32)
+        bnow[...] = btail[lax.div(i, per_seq)].astype(F32)
+
+    @pl.when((i < products) & jnp.logical_not(ends))
+    def _():
+        xnow[...] = jnp.zeros_like(xnow)
+        bnow[...] = jnp.zeros_like(bnow)
+
+    @pl.when(i < products)
+    def _():
+        x_rows, b_rows = with_tails()
         value = mm_t(gate_grad[...], gate_w[...]) + mm_t(x_rows, value_w[...])
         value = value + (mm_t(b_rows, state_w[...]) + mm_t(raw[...], step_w[...]))
+        chunks = T // CHUNK
+        own[pl.ds(i * chunks, chunks)] = value.astype(BF16).reshape(chunks, CHUNK, value.shape[1])
         t = tok_k[...].astype(F32)
         inv = lax.rsqrt(jnp.mean(t * t, axis=1, keepdims=True) + EPS)
         gain = jnp.sum(value * (t * inv), axis=0, keepdims=True)
         half = t.shape[1] // 2
         rows[8:9] += gain[:, :half]
         rows[9:10] += gain[:, half:]
-        chunks = T // CHUNK
-        first = lax.div(i, 2) * chunks
-        own[pl.ds(first, chunks)] = value.astype(BF16).reshape(chunks, CHUNK, value.shape[1])
+
+    @pl.when(i < n)
+    def _():
+        chain.inward(i)
+
+    @pl.when(i < products)
+    def _():
+        x_rows, b_rows = with_tails()
         mixed = jnp.concatenate([b_rows, raw[...]], axis=1)
         for m in range(w_acc.shape[0] // 256):
             rows_m = slice(m * 256, (m + 1) * 256)
@@ -1148,10 +1194,6 @@
             w_acc[rows_m] += t_mm(left, x_rows)
             m_acc[rows_m] += t_mm(left, mixed)
 
-    @pl.when(i < n)
-    def _():
-        chain.inward(i)
-
     @pl.when(i == products)
     def _():
         w_mine[2] = w_acc[...].astype(BF16)
@@ -1162,7 +1204,7 @@
         for copy in local_copies():
             copy.wait()
 
-    for grad_sum, begin in zip(grads, (1, 5, products, products + 2)):
+    for grad_sum, begin in zip(grads, (1, 4, products + 1, products + 5)):
         at = begin
         for span, act in grad_sum.stages():
             pl.when(i == min(at, last))(act)
@@ -1228,11 +1270,17 @@
     def _():
         chain.drain(n)
         rider.drain()
+
+        @pl.when(me > 0)
+        def _():
+            for copy in halo_copies():
+                copy.wait_send()
+
         small_o[...] = rows[...]
 
 
 def unpack(
-    tgrad, res, wout_l, wout_r, wgate, wvalue, wmixed, small, rate, wide,
+    tgrad, res, wout_l, wout_r, wgate, wvalue, wmixed, mixed_all, small, rate, wide,
     res_o, tgrad_o, ngain_o, wgate_o, wvalue_o, state_o, step_o, vk_o, vo_o, sk_o, so_o, sbias_o, rate_o, skip_o, mgain_o, wout_o,
     *, taps, heads,
 ):
@@ -1245,10 +1293,12 @@
     wout_o[:, half:] = wout_r[...].astype(F32)
     n2 = state_o.shape[1]
     state_o[...] = wmixed[:, :n2].astype(F32)
-    step_o[...] = wmixed[:, n2 : n2 + heads].astype(F32)
 
     @pl.when(pl.program_id(0) == 0)
     def _():
+        for k in range(mixed_all.shape[0] // LANES):
+            at = slice(k * LANES, (k + 1) * LANES)
+            step_o[:, at] = mixed_all[at, n2 : n2 + LANES].astype(F32).T[0:heads]
         vk_o[...] = small[0:taps]
         vo_o[...] = small[taps]
         mgain_o[...] = small[taps + 1]
@@ -1404,8 +1454,6 @@
          vmem((ext + HALO, n2), F32), vmem((inner, width), F32), vmem((width, inner), F32)] + Rider.scratch(*plan, width),
         2 * flat * T * inner * 4, 5, y,
     )
-    back = [(i + 1, i) for i in range(devices - 1)]
-    xhalo, bhalo = lax.ppermute((xhalo, bhalo), "seq", back)
     def flatten(v):
         return v.reshape(flat, v.shape[-1])
 
@@ -1414,7 +1462,7 @@
     plan = (first, max(n_chunks - first, 0) + 3 * LAG, n_chunks)
 
     def product_rows(v):
-        return pl.BlockSpec((T, v.shape[1]), lambda i: (jnp.minimum(i // 2, flat // T - 1), 0))
+        return pl.BlockSpec((T, v.shape[1]), lambda i: (jnp.minimum(i, flat // T - 1), 0))
 
     def lagged(cols, lag):
         return pl.BlockSpec((CHUNK, cols), lambda i: (jnp.clip(i - lag, 0, n_chunks - 1), 0))
@@ -1440,7 +1488,8 @@
             vmem((3, width, inner), BF16), vmem((3, width, inner), BF16), vmem((width, n2 + LANES), BF16),
             vmem((width, n2 + LANES), BF16), vmem((4, width >> rounds, n2), BF16), vmem((width, inner), F32),
             vmem((width, n2 + LANES), F32), dma((4, GradSum.sem_count(rounds))), dma((3,)),
-            vmem((16, inner), F32), vmem((4, 16, inner), F32), dma((8,)),
+            vmem((16, inner), F32), vmem((4, 16, inner), F32), dma((8,)), vmem(xhalo.shape, BF16), vmem(bhalo.shape, BF16), dma((4,)),
+            vmem((HALO, inner), F32), vmem((HALO, n2), F32),
         ],
         compiler_params=pltpu.CompilerParams(
             dimension_semantics=("arbitrary",), vmem_limit_bytes=62 * 1024 * 1024, collective_id=4, has_side_effects=True
@@ -1448,7 +1497,7 @@
         cost_estimate=pl.CostEstimate(flops=10**11, bytes_accessed=10**8, transcendentals=0),
     )(y.reshape(flat, width), gg_f, xpg_f, bpg_f, raw_f, flatten(tokens), flatten(cotangent), flatten(rms),
       *late, normed_f, flatten(tokens), out_weight_grad, gate_weight_grad, y)
-    parts = 16
+    parts = 8
 
     def strip(rows, cols, at=0):
         return pl.BlockSpec((rows // parts, cols), lambda i: (i + at, 0))
@@ -1459,20 +1508,21 @@
     fine = [strip(inner, inner), strip(inner, inner, parts)]
     flat_out = [
         ((flat, width), BF16), ((flat, width), F32), ((width,), F32), ((width, inner), F32), ((width, inner), F32), ((width, n2), F32),
-        ((width, heads), F32), ((taps, inner), F32), ((inner,), F32), ((taps, n2), F32), ((n2,), F32), ((heads,), F32), ((heads,), F32),
+        ((heads, width), F32), ((taps, inner), F32), ((inner,), F32), ((taps, n2), F32), ((n2,), F32), ((heads,), F32), ((heads,), F32),
         ((heads,), F32), ((inner,), F32), ((inner, width), F32),
     ]
-    cut = (0, 1, 3, 4, 5, 6, 15)
+    cut = (0, 1, 3, 4, 5, 15)
     found = pl.pallas_call(
         functools.partial(unpack, taps=taps, heads=heads),
         grid=(parts,),
         in_specs=[strip(flat, width), strip(flat, width)] + fine + [strip(width, inner)] * 2 + [strip(width, n2 + LANES)]
-        + [entire(small.shape), entire(rate.shape), entire(wide.shape)],
+        + [entire(wmixed.shape), entire(small.shape), entire(rate.shape), entire(wide.shape)],
         out_specs=[strip(*shape) if k in cut else entire(shape) for k, (shape, _) in enumerate(flat_out)],
         out_shape=[jax.ShapeDtypeStruct(shape, dtype) for shape, dtype in flat_out],
         compiler_params=pltpu.CompilerParams(dimension_semantics=("arbitrary",), vmem_limit_bytes=60 * 1024 * 1024),
-    )(tokens_grad, result, wout, wout, wgate, wvalue, wmixed, small, rate, wide)
-    return (found[0].reshape(tokens.shape), found[1].reshape(tokens.shape)) + tuple(found[2:])
+    )(tokens_grad, result, wout, wout, wgate, wvalue, wmixed, wmixed, small, rate, wide)
+    found = [found[0].reshape(tokens.shape), found[1].reshape(tokens.shape), *found[2:6], found[6].T, *found[7:]]
+    return tuple(found)
 
 
 def solution(mesh):

time: 443 us -> 432 us (0.975)
  transfers between devices with their start and end apart: 2 -> 0, of which waited for: 1 -> 0; matrix products, arithmetic and copies ran while one was open for 0% -> 0% of each run, Pallas kernels for 0% -> 0%
where the time goes in v7:
time: 432 us; the launch traced here: 431 us
  Pallas kernels  424 us (98%)
  local copies, waits for them, and re-layouts  4.49 us (1%)
    pallas_call x1, Pallas kernels, shards(): pl.pallas_call(functools.partial(finish, n=n_chunks, rounds=rounds, plan=...  177 us
    pallas_call x2, Pallas kernels, call(): pl.pallas_call(body, grid=(steps,), in_specs=in_specs, out_specs=out_spec...  143 us
    pallas_call x1, Pallas kernels, shards(): pl.pallas_call(functools.partial(forward, seqs=seqs, rounds=rounds, plan=...  82 us
    pallas_call x1, Pallas kernels, shards(): pl.pallas_call(functools.partial(unpack, taps=taps, heads=heads), grid=(p...  20.8 us

profile of v7, /device:TPU:0, one launch (start us, length us, event | category | flops | bytes accessed | tf_op | source)
XLA Modules:
  0.0 431.1 jit_solution(11121826425053594002)
XLA Ops:
  0.6 0.7 exponential_negate_fusion
  1.3 1.2 pad_bitcast_fusion
  2.5 0.7 broadcast_in_dim.15
  3.3 0.7 broadcast_in_dim_reshape.3.skip
  3.9 0.1 iota_compare_fusion
  4.0 0.7 fusion.tri
  4.7 0.8 add_convert_fusion.wide
  5.4 1.0 copy.34
  6.5 0.8 pad.11.step_w
  7.3 82.0 %shard_map.279 = (bf16[4,528,768]{2,1,0:T(8,128)(2,1)}, bf16[4,528,256]{2,1,0:T(8,128)(2,1)}, f32[4,512,128]{2,1,0:T(8,128)}, f32[4,8,128]{2,1,0:T(8,128)}, f32[...) custom-call(bf16[4,512,1536]{2,1,0:T(8,128)(2,1)} %tok_all.1, ...), custom_call_target="tpu_custom_call" | custom-call | flops 19327352832 | bytes 100000000 | tf_op jit(solution)/shard_map/pallas_call | solution.py:1409
  89.4 75.4 %shard_map.280 = (bf16[4,512,768]{2,1,0:T(8,128)(2,1)}, bf16[4,512,768]{2,1,0:T(8,128)(2,1)}, f32[4,2,128,768]{3,2,1,0:T(8,128)}, f32[4,512,128]{2,1,0:T(8,128)}...) custom-call(bf16[4,512,768]{2,1,0:T(8,128)(2,1)} %get-tuple-element., ...), custom_call_target="tpu_custom_call", output_to_operand_aliasing={{11}: (18, {})} | custom-call | flops 6442450944 | bytes 64509952 | tf_op jit(solution)/shard_map/pallas_call | solution.py:1340
  164.8 68.0 %shard_map.281 = (bf16[4,512,768]{2,1,0:T(8,128)(2,1)}, bf16[4,16,768]{2,1,0:T(8,128)(2,1)}, bf16[4,512,256]{2,1,0:T(8,128)(2,1)}, bf16[4,16,256]{2,1,0:T(8,128)...) custom-call(bf16[4,512,768]{2,1,0:T(8,128)(2,1)} %get-tuple-element., ...), custom_call_target="tpu_custom_call", output_to_operand_aliasing={{10}: (28, {})} | custom-call | flops 3221225472 | bytes 66921472 | tf_op jit(solution)/shard_map/pallas_call | solution.py:1340
  232.8 177.4 %shard_map.282 = (bf16[2048,1536]{1,0:T(8,128)(2,1)}, bf16[2048,1536]{1,0:T(8,128)(2,1)}, f32[24,768]{1,0:T(8,128)}, bf16[1536,768]{1,0:T(8,128)(2,1)}, bf16[153...) custom-call(bf16[2048,1536]{1,0:T(8,128)(2,1)} %bitcast.16, bf16[2048,768]{1,0:T(8,128)(2,1)} %bitcast.19, ...), custom_call_target="tpu_custom_call" | custom-call | flops 99999997952 | bytes 100000000 | tf_op jit(solution)/shard_map/pallas_call | solution.py:1471
  410.2 20.8 %shard_map.283 = (bf16[2048,1536]{1,0:T(8,128)(2,1)}, f32[2048,1536]{1,0:T(8,128)}, f32[1536]{0:T(1024)}, f32[1536,768]{1,0:T(8,128)}, f32[1536,768]{1,0:T(8,128...) custom-call(bf16[2048,1536]{1,0:T(8,128)(2,1)} %get-tuple-element.11, ...), custom_call_target="tpu_custom_call" | custom-call | tf_op jit(solution)/shard_map/pallas_call | solution.py:1515
  (1 shorter events, 0.0 us)

commit v8 on v7

--- a/solution.py
+++ b/solution.py
@@ -2,6 +2,7 @@
 
 import jax
 import jax.numpy as jnp
+import numpy as np
 from jax import lax
 from jax.experimental import pallas as pl
 from jax.experimental.pallas import tpu as pltpu
@@ -1378,9 +1379,9 @@
     step_w = jnp.pad(step_weight, ((0, 0), (0, pad)))
     skip = jnp.repeat(skip_gain, head_size)[None]
     gain = mixer_gain
-    one = (jnp.arange(inner)[None, :] // head_size == jnp.arange(LANES)[:, None]).astype(BF16)
-    wide = jnp.concatenate([one, one], axis=0)
-    tri = (jnp.arange(T)[:, None] >= jnp.arange(T)[None, :]).astype(BF16)
+    one = np.arange(inner)[None, :] // head_size == np.arange(LANES)[:, None]
+    wide = jnp.asarray(np.concatenate([one, one], axis=0).astype(BF16))
+    tri = jnp.asarray(np.tril(np.ones((T, T))).astype(BF16))
     vo, so = value_offset, state_offset
 
     def big(cols, dtype, rows=length, lag=0):
@@ -1497,7 +1498,7 @@
         cost_estimate=pl.CostEstimate(flops=10**11, bytes_accessed=10**8, transcendentals=0),
     )(y.reshape(flat, width), gg_f, xpg_f, bpg_f, raw_f, flatten(tokens), flatten(cotangent), flatten(rms),
       *late, normed_f, flatten(tokens), out_weight_grad, gate_weight_grad, y)
-    parts = 8
+    parts = 4
 
     def strip(rows, cols, at=0):
         return pl.BlockSpec((rows // parts, cols), lambda i: (i + at, 0))

time: 432 us -> 430 us (level)
  no operation moved by 1% of the time
where the time goes in v8:
time: 430 us
  Pallas kernels  424 us (99%)
  local copies, waits for them, and re-layouts  4.46 us (1%)
    pallas_call x1, Pallas kernels, shards(): pl.pallas_call(functools.partial(finish, n=n_chunks, rounds=rounds, plan=...  177 us
    pallas_call x2, Pallas kernels, call(): pl.pallas_call(body, grid=(steps,), in_specs=in_specs, out_specs=out_spec...  144 us
    pallas_call x1, Pallas kernels, shards(): pl.pallas_call(functools.partial(forward, seqs=seqs, rounds=rounds, plan=...  82 us
    pallas_call x1, Pallas kernels, shards(): pl.pallas_call(functools.partial(unpack, taps=taps, heads=heads), grid=(p...  20.5 us

profile of v8, /device:TPU:0, one launch (start us, length us, event | category | flops | bytes accessed | tf_op | source)
XLA Modules:
  0.0 429.6 jit_solution(5549339508142551486)
XLA Ops:
  0.6 0.7 exponential_negate_fusion
  1.3 1.2 pad_bitcast_fusion
  2.5 0.7 broadcast_in_dim.11
  3.2 0.7 broadcast_in_dim_reshape.3.skip
  3.9 1.0 copy.36
  4.9 0.8 pad.11.step_w
  5.8 82.0 %shard_map.297 = (bf16[4,528,768]{2,1,0:T(8,128)(2,1)}, bf16[4,528,256]{2,1,0:T(8,128)(2,1)}, f32[4,512,128]{2,1,0:T(8,128)}, f32[4,8,128]{2,1,0:T(8,128)}, f32[...) custom-call(bf16[4,512,1536]{2,1,0:T(8,128)(2,1)} %tok_all.1, ...), custom_call_target="tpu_custom_call" | custom-call | flops 19327352832 | bytes 100000000 | tf_op jit(solution)/shard_map/pallas_call | solution.py:1410
  87.8 75.4 %shard_map.298 = (bf16[4,512,768]{2,1,0:T(8,128)(2,1)}, bf16[4,512,768]{2,1,0:T(8,128)(2,1)}, f32[4,2,128,768]{3,2,1,0:T(8,128)}, f32[4,512,128]{2,1,0:T(8,128)}...) custom-call(bf16[4,512,768]{2,1,0:T(8,128)(2,1)} %get-tuple-element., ...), custom_call_target="tpu_custom_call", output_to_operand_aliasing={{11}: (18, {})} | custom-call | flops 6442450944 | bytes 64509952 | tf_op jit(solution)/shard_map/pallas_call | solution.py:1341
  163.2 68.2 %shard_map.299 = (bf16[4,512,768]{2,1,0:T(8,128)(2,1)}, bf16[4,16,768]{2,1,0:T(8,128)(2,1)}, bf16[4,512,256]{2,1,0:T(8,128)(2,1)}, bf16[4,16,256]{2,1,0:T(8,128)...) custom-call(bf16[4,512,768]{2,1,0:T(8,128)(2,1)} %get-tuple-element., ...), custom_call_target="tpu_custom_call", output_to_operand_aliasing={{10}: (28, {})} | custom-call | flops 3221225472 | bytes 66921472 | tf_op jit(solution)/shard_map/pallas_call | solution.py:1341
  231.4 177.5 %shard_map.300 = (bf16[2048,1536]{1,0:T(8,128)(2,1)}, bf16[2048,1536]{1,0:T(8,128)(2,1)}, f32[24,768]{1,0:T(8,128)}, bf16[1536,768]{1,0:T(8,128)(2,1)}, bf16[153...) custom-call(bf16[2048,1536]{1,0:T(8,128)(2,1)} %bitcast.16, bf16[2048,768]{1,0:T(8,128)(2,1)} %bitcast.19, ...), custom_call_target="tpu_custom_call" | custom-call | flops 99999997952 | bytes 100000000 | tf_op jit(solution)/shard_map/pallas_call | solution.py:1472
  408.9 20.5 %shard_map.301 = (bf16[2048,1536]{1,0:T(8,128)(2,1)}, f32[2048,1536]{1,0:T(8,128)}, f32[1536]{0:T(1024)}, f32[1536,768]{1,0:T(8,128)}, f32[1536,768]{1,0:T(8,128...) custom-call(bf16[2048,1536]{1,0:T(8,128)(2,1)} %get-tuple-element.11, ...), custom_call_target="tpu_custom_call" | custom-call | tf_op jit(solution)/shard_map/pallas_call | solution.py:1516
